TPU v7x, 1024 devices: a whole 8x8x8 slice. The times are simulated.
1024 devices in a mesh: expert: 64 (over z, y), dp: 16 (over x, core).
Axes of the slice: x: 8, y: 8, z: 8, core: 2. Of those that a mesh axis runs over, the one named last changes fastest.
Arguments:
- tokens: bfloat16 [131072, 3584], P(('expert', 'dp')), may hold values from -6 to 6
- cotangent: bfloat16 [131072, 3584], P(('expert', 'dp')), may hold values from -6 to 6
- gates: bfloat16 [131072, 2], P(('expert', 'dp')), may hold values from 0.099609375 to 1
- route_ids: int32 [131072, 2], P(('expert', 'dp')), may hold values from 0 to 127, as said below
- w_gate: bfloat16 [9728, 3584], P('expert'), may hold values from -0.09375 to 0.09375
- w_up: bfloat16 [9728, 3584], P('expert'), may hold values from -0.09375 to 0.09375
- w_down: bfloat16 [9728, 3584], P('expert'), may hold values from -0.125 to 0.125
Outputs:
- grad_tokens: bfloat16 [131072, 3584], P(('expert', 'dp'))
- grad_gate: bfloat16 [9728, 3584], P('expert', 'dp')
- grad_up: bfloat16 [9728, 3584], P('expert', 'dp')
- grad_down: bfloat16 [9728, 3584], P('expert', 'dp')
Inputs may be any that keep to these rules, and one draw needn't show every extreme that they name: `route_ids`: each row names two different experts. In every aligned block of 128 rows one expert under 4 is named at least 2 times.
All inputs are finite; a program needn't handle non-finite values.
Results may differ from a plain program's by a relative error of at most 0.023.
Values may be sent and summed in bfloat16 or wider, within the bound.
No kernel may reach another device: no remote copies, remote signals or barrier semaphores. Data moves between devices by JAX's collectives and lax.ppermute only.
A program may use at most 32 MiB of HBM per device.

v0:
```python
import jax
import jax.numpy as jnp
from jax import lax
from jax.sharding import PartitionSpec as P

EXPERTS = 4
CAP = 2


def route_table(route_block, expert_count, capacity):
    flat_ids = route_block.reshape(-1)
    onehot = (flat_ids[:, None] == jnp.arange(expert_count, dtype=jnp.int32)[None, :]).astype(
        jnp.int32
    )
    position = jnp.cumsum(onehot, axis=0) - 1
    slot_index = jnp.sum(onehot * position, axis=1)
    kept = (flat_ids < expert_count) & (slot_index < capacity)
    target = jnp.where(kept, flat_ids * capacity + slot_index, -1)
    slot_range = jnp.arange(expert_count * capacity, dtype=jnp.int32)
    route_grid = (target[None, :] == slot_range[:, None]).astype(jnp.float32)
    return route_grid.reshape(expert_count * capacity, route_block.shape[0], 2)


def forward_part(inputs_rows, weight_gate, weight_up):
    gate_pre = jnp.dot(inputs_rows, weight_gate.T, preferred_element_type=jnp.float32)
    up_pre = jnp.dot(inputs_rows, weight_up.T, preferred_element_type=jnp.float32)
    return (gate_pre, up_pre)


def backward_part(cotan_rows, gate_rows, gate_pre, up_pre, weight_gate, weight_up, weight_down):
    sigmoid_gate = jax.nn.sigmoid(gate_pre)
    activation = gate_pre * sigmoid_gate * up_pre
    back_proj = jnp.dot(cotan_rows, weight_down.T, preferred_element_type=jnp.float32)
    gate_col = gate_rows.astype(jnp.float32)[:, None]
    grad_hidden = gate_col * back_proj
    grad_up_pre = (grad_hidden * gate_pre * sigmoid_gate).astype(jnp.bfloat16)
    grad_gate_pre = (
        grad_hidden * up_pre * sigmoid_gate * (1.0 + gate_pre * (1.0 - sigmoid_gate))
    ).astype(jnp.bfloat16)
    scaled_act = (gate_col * activation).astype(jnp.bfloat16)
    slot_partial = jnp.dot(grad_gate_pre, weight_gate, preferred_element_type=jnp.float32)
    slot_partial = slot_partial + jnp.dot(
        grad_up_pre, weight_up, preferred_element_type=jnp.float32
    )
    return (grad_gate_pre, grad_up_pre, scaled_act, slot_partial)


def shards(tokens, cotangent, gates, route_ids, w_gate, w_up, w_down):
    device_count = lax.axis_size("expert")
    expert_pieces = device_count // EXPERTS
    feature_count = tokens.shape[1]
    token_count = tokens.shape[0]
    route_grid = route_table(route_ids, EXPERTS, CAP)
    per_token = jnp.sum(route_grid, axis=2).astype(jnp.bfloat16)

    def spread(slot_rows):
        shaped = slot_rows.reshape((EXPERTS, CAP) + slot_rows.shape[1:])
        return jnp.repeat(shaped, expert_pieces, axis=0)

    send_inputs = spread(
        jnp.dot(per_token, tokens, preferred_element_type=jnp.float32).astype(jnp.bfloat16)
    )
    send_cotan = spread(
        jnp.dot(per_token, cotangent, preferred_element_type=jnp.float32).astype(jnp.bfloat16)
    )
    send_gates = spread(
        jnp.sum(route_grid * gates.astype(jnp.float32)[None], axis=(1, 2)).astype(jnp.bfloat16)
    )
    arrived_inputs, arrived_cotan, arrived_gates = (
        lax.all_to_all(send_inputs, "expert", split_axis=0, concat_axis=0, tiled=True),
        lax.all_to_all(send_cotan, "expert", split_axis=0, concat_axis=0, tiled=True),
        lax.all_to_all(send_gates, "expert", split_axis=0, concat_axis=0, tiled=True),
    )
    sources = arrived_inputs.shape[0]
    inputs_rows = arrived_inputs.reshape(sources * CAP, feature_count)
    cotan_rows = arrived_cotan.reshape(sources * CAP, feature_count)
    gate_pre, up_pre = forward_part(inputs_rows, w_gate, w_up)
    gate_rows = arrived_gates.reshape(sources * CAP)
    grad_gate_pre, grad_up_pre, scaled_act, slot_partial = backward_part(
        cotan_rows, gate_rows, gate_pre, up_pre, w_gate, w_up, w_down
    )
    local_grads = (
        jnp.dot(grad_gate_pre.T, inputs_rows, preferred_element_type=jnp.float32).astype(
            jnp.bfloat16
        ),
        jnp.dot(grad_up_pre.T, inputs_rows, preferred_element_type=jnp.float32).astype(
            jnp.bfloat16
        ),
        jnp.dot(scaled_act.T, cotan_rows, preferred_element_type=jnp.float32).astype(jnp.bfloat16),
    )
    local_grads = lax.optimization_barrier(local_grads)
    summed_gate, summed_up, summed_down = (
        lax.psum_scatter(
            local_grads[0].astype(jnp.float32).astype(jnp.bfloat16),
            "dp",
            scatter_dimension=1,
            tiled=True,
        ).astype(jnp.float32),
        lax.psum_scatter(
            local_grads[1].astype(jnp.float32).astype(jnp.bfloat16),
            "dp",
            scatter_dimension=1,
            tiled=True,
        ).astype(jnp.float32),
        lax.psum_scatter(
            local_grads[2].astype(jnp.float32).astype(jnp.bfloat16),
            "dp",
            scatter_dimension=1,
            tiled=True,
        ).astype(jnp.float32),
    )
    grad_gate = summed_gate.astype(jnp.bfloat16)
    grad_up = summed_up.astype(jnp.bfloat16)
    grad_down = summed_down.astype(jnp.bfloat16)
    piece_grad = slot_partial.astype(jnp.bfloat16).reshape(sources, CAP, feature_count)
    returned = lax.all_to_all(piece_grad, "expert", split_axis=0, concat_axis=0, tiled=True)
    returned_rows = returned.reshape(device_count * CAP, feature_count)
    pair_table = jnp.broadcast_to(
        per_token.reshape(EXPERTS, 1, CAP, token_count), (EXPERTS, expert_pieces, CAP, token_count)
    )
    pair_table = pair_table.reshape(device_count * CAP, token_count)
    grad_tokens = jnp.dot(pair_table.T, returned_rows, preferred_element_type=jnp.float32).astype(
        jnp.bfloat16
    )
    return (grad_tokens, grad_gate, grad_up, grad_down)


def solution(mesh):
    in_specs = (
        P(("expert", "dp"), None),
        P(("expert", "dp"), None),
        P(("expert", "dp"), None),
        P(("expert", "dp"), None),
        P("expert", None),
        P("expert", None),
        P("expert", None),
    )
    out_specs = (P(("expert", "dp"), None), P("expert", "dp"), P("expert", "dp"), P("expert", "dp"))
    return jax.shard_map(shards, mesh=mesh, in_specs=in_specs, out_specs=out_specs, check_vma=False)
```

profile of v0, /device:TPU:1, one launch (start us, length us, event | category | flops | bytes accessed | tf_op | source)
XLA Modules:
  0.0 323.1 jit_solution(15895376441567123933)
XLA Ops:
  7.2 0.0 copy-start
  7.2 0.9 copy.50
  8.1 0.1 eq.43
  8.2 0.1 eq.39
  8.4 1.2 reduce-window.6
  9.6 0.1 slice.8
  9.7 0.1 copy.52
  9.8 0.1 copy.53
  9.9 0.1 add_bitcast_fusion
  10.0 0.1 reduce_sum.30
  10.1 0.1 copy.54
  10.2 0.7 and_select_fusion
  10.9 0.7 convert_element_type.85
  11.6 0.1 select_reduce_fusion
  11.7 0.1 convert_element_type.87
  11.8 0.1 copy.56
  11.9 0.1 broadcast_in_dim.25
  12.0 0.1 all_to_all.15
  12.0 0.7 copy.57
  12.8 24.0 %all-to-all-start = ((bf16[64,1,2]{2,1,0:T(2,128)(2,1)}), bf16[64,1,2]{2,1,0:T(2,128)(2,1)S(1)}, u32[]{:S(2)}, u32[]{:S(2)}) async-start(bf16[64,1,2]{2,1,0:T(2,128)(2,1)} %copy.57), calls=%async_computation | async-start | bytes 65536 | tf_op jit(solution)/shard_map/all_to_all | solution.py:72
  36.8 1.4 convolution_convert_fusion.4
  38.2 9.3 %all-to-all-done = bf16[64,1,2]{2,1,0:T(2,128)(2,1)S(1)} async-done(((bf16[64,1,2]{2,1,0:T(2,128)(2,1)}), bf16[64,1,2]{2,1,0:T(2,128)(2,1)S(1)}, u32[]{:S(2)}, u32[]{:S(2)}) %all-to-all-start) | async-done | bytes 288 | tf_op jit(solution)/shard_map/all_to_all | solution.py:72
  47.5 1.4 broadcast_in_dim.27
  48.9 4.8 %all-to-all-start.2 = ((bf16[64,2,3584]{2,1,0:T(2,128)(2,1)}), bf16[64,2,3584]{2,1,0:T(2,128)(2,1)S(1)}, u32[]{:S(2)}, u32[]{:S(2)}) async-start(bf16[64,2,3584]{2,1,0:T(2,128)(2,1)} %bitcast.5), calls=%async_computation.2 | async-start | bytes 1835008 | tf_op jit(solution)/shard_map/all_to_all | solution.py:70
  53.7 0.2 convolution_convert_fusion.5
  54.0 23.3 %all-to-all-done.2 = bf16[64,2,3584]{2,1,0:T(2,128)(2,1)S(1)} async-done(((bf16[64,2,3584]{2,1,0:T(2,128)(2,1)}), bf16[64,2,3584]{2,1,0:T(2,128)(2,1)S(1)}, u32[]{:S(2)}, u32[]{:S(2)}) %all-to-all-start.2) | async-done | bytes 917536 | tf_op jit(solution)/shard_map/all_to_all | solution.py:70
  77.3 1.4 broadcast_in_dim.26
  78.7 8.1 %all-to-all-start.1 = ((bf16[64,2,3584]{2,1,0:T(2,128)(2,1)}), bf16[64,2,3584]{2,1,0:T(2,128)(2,1)}, u32[]{:S(2)}, u32[]{:S(2)}) async-start(bf16[64,2,3584]{2,1,0:T(2,128)(2,1)} %bitcast.4), calls=%async_computation.1 | async-start | bytes 1835008 | tf_op jit(solution)/shard_map/all_to_all | solution.py:71
  86.9 0.0 copy-start.2
  86.9 0.0 reduce-scatter.10.cloned.1.call-start
  86.9 0.1 convert_reduce_fusion
  87.0 0.1 reshape.112
  87.2 2.5 reshape.109
  89.7 0.4 fusion.6
  90.1 0.4 fusion.7
  90.6 19.1 %all-to-all-done.1 = bf16[64,2,3584]{2,1,0:T(2,128)(2,1)} async-done(((bf16[64,2,3584]{2,1,0:T(2,128)(2,1)}), bf16[64,2,3584]{2,1,0:T(2,128)(2,1)}, u32[]{:S(2)}, u32[]{:S(2)}) %all-to-all-start.1) | async-done | bytes 917536 | tf_op jit(solution)/shard_map/all_to_all | solution.py:71
  109.7 2.5 reshape.106
  112.1 0.0 copy-start.4
  112.1 1.4 convolution_convert_fusion
  113.6 0.0 copy-done.4
  113.6 0.5 multiply_convert_fusion.1
  114.0 0.4 convolution_convert_fusion.1
  114.5 1.4 convolution_convert_fusion.2
  115.9 2.6 copy.58
  118.6 0.0 reduce-scatter.10.cloned.1.call-update
  118.6 0.0 reduce-scatter.12.cloned.1.call-start
  118.6 1.7 copy.60
  120.3 0.0 reduce-scatter.12.cloned.1.call-update
  120.3 0.2 reduce-scatter.14.cloned.1.call-start
  120.6 1.0 copy-done.1
  121.5 1.6 copy.62
  123.2 0.4 fusion.8
  123.6 0.0 reduce-scatter.14.cloned.1.call-update
  123.7 2.6 fusion
  126.3 2.3 reshape.110
  128.6 30.4 %all_to_all.24 = bf16[64,2,3584]{2,1,0:T(2,128)(2,1)S(1)} all-to-all(bf16[64,2,3584]{2,1,0:T(2,128)(2,1)S(1)} %reshape.110), channel_id=1, replica_groups=mesh['expert'=64,'dp'=16] {'expert'}, dimensions={0} | all-to-all | bytes 1835008 | tf_op jit(solution)/shard_map/all_to_all | solution.py:116
  159.0 0.3 reshape.111
  159.4 1.4 convolution_convert_fusion.3
  160.7 20.7 %reduce-scatter.10.cloned.1.call-done = bf16[224,152]{1,0:T(8,128)(2,1)} async-done(((bf16[3584,152]{1,0:T(8,128)(2,1)}), bf16[224,152]{1,0:T(8,128)(2,1)}) %reduce-scatter.10.cloned.1.call-update) | async-done | bytes 68112
  181.4 1.6 copy.59
  183.1 65.3 %reduce-scatter.12.cloned.1.call-done = bf16[224,152]{1,0:T(8,128)(2,1)} async-done(((bf16[3584,152]{1,0:T(8,128)(2,1)}), bf16[224,152]{1,0:T(8,128)(2,1)}) %reduce-scatter.12.cloned.1.call-update) | async-done | bytes 68112
  248.3 1.6 copy.61
  250.0 65.0 %reduce-scatter.14.cloned.1.call-done = bf16[224,152]{1,0:T(8,128)(2,1)} async-done(((bf16[3584,152]{1,0:T(8,128)(2,1)}), bf16[224,152]{1,0:T(8,128)(2,1)}) %reduce-scatter.14.cloned.1.call-update) | async-done | bytes 68112
  315.0 1.6 copy.63
  (14 shorter events, 0.2 us)
Async XLA Ops:
  7.2 83.0 %copy-start = (bf16[152,3584]{1,0:T(8,128)(2,1)S(1)}, bf16[152,3584]{1,0:T(8,128)(2,1)}, u32[]{:S(2)}) copy-start(bf16[152,3584]{1,0:T(8,128)(2,1)} %param.11) | copy-start | bytes 3268612
  12.8 34.7 %all-to-all-start = ((bf16[64,1,2]{2,1,0:T(2,128)(2,1)}), bf16[64,1,2]{2,1,0:T(2,128)(2,1)S(1)}, u32[]{:S(2)}, u32[]{:S(2)}) async-start(bf16[64,1,2]{2,1,0:T(2,128)(2,1)} %copy.57), calls=%async_computation | async-start | bytes 65536 | tf_op jit(solution)/shard_map/all_to_all | solution.py:72
  48.9 4.8 %copy-start.5 = (bf16[128,3584]{1,0:T(8,128)(2,1)S(1)}, bf16[128,3584]{1,0:T(8,128)(2,1)}, u32[]{:S(2)}) copy-start(bf16[128,3584]{1,0:T(8,128)(2,1)} %param.8) | copy-start | bytes 2752516
  48.9 28.4 %all-to-all-start.2 = ((bf16[64,2,3584]{2,1,0:T(2,128)(2,1)}), bf16[64,2,3584]{2,1,0:T(2,128)(2,1)S(1)}, u32[]{:S(2)}, u32[]{:S(2)}) async-start(bf16[64,2,3584]{2,1,0:T(2,128)(2,1)} %bitcast.5), calls=%async_computation.2 | async-start | bytes 1835008 | tf_op jit(solution)/shard_map/all_to_all | solution.py:70
  77.3 1.4 copy-start.3
  78.7 30.9 %all-to-all-start.1 = ((bf16[64,2,3584]{2,1,0:T(2,128)(2,1)}), bf16[64,2,3584]{2,1,0:T(2,128)(2,1)}, u32[]{:S(2)}, u32[]{:S(2)}) async-start(bf16[64,2,3584]{2,1,0:T(2,128)(2,1)} %bitcast.4), calls=%async_computation.1 | async-start | bytes 1835008 | tf_op jit(solution)/shard_map/all_to_all | solution.py:71
  86.9 2.8 copy-start.2
  86.9 94.6 %reduce-scatter.10.cloned.1.call-start = ((), (), s32[]{:S(2)}) async-start(), calls=%async_computation.7 | async-start | bytes 1949696
  112.1 1.4 copy-start.4
  118.6 129.7 %reduce-scatter.12.cloned.1.call-start = ((), (), s32[]{:S(2)}) async-start(), calls=%async_computation.8 | async-start | bytes 1949696
  120.3 1.2 copy-start.1
  120.3 194.7 %reduce-scatter.14.cloned.1.call-start = ((), (), s32[]{:S(2)}) async-start(), calls=%async_computation.9 | async-start | bytes 1949696
Sparse Core Ops, SparseCore 0:
  118.7 62.6 reduce-scatter.9
  185.2 63.0 reduce-scatter.11
  251.7 63.1 reduce-scatter.13
where the time goes:
time: 324 us; the launch traced here: 323 us
  waiting for transfers between devices  203 us (63%)
  starting transfers between devices  37.2 us (11%)
  blocking collectives  30.4 us (9%)
  local copies, waits for them, and re-layouts  25.4 us (8%)
  between operations  13.9 us (4%)
  matrix products  10.6 us (3%)
    unnamed x6, waiting for transfers between devices  151 us
    all_to_all x1, blocking collectives, shards(): lax.all_to_all(piece_grad, 'expert', split_axis=0, concat_axis=0, tiled=T...  30.4 us
    all_to_all x1, starting transfers between devices, shards(): lax.all_to_all(send_gates, 'expert', split_axis=0, concat_axis=0, tiled=T...  24 us
    all_to_all x1, waiting for transfers between devices, shards(): lax.all_to_all(send_inputs, 'expert', split_axis=0, concat_axis=0, tiled=...  23.3 us
    all_to_all x1, waiting for transfers between devices, shards(): lax.all_to_all(send_cotan, 'expert', split_axis=0, concat_axis=0, tiled=T...  19.1 us
    unnamed x19, local copies, waits for them, and re-layouts  12.8 us
    all_to_all x1, waiting for transfers between devices, shards(): lax.all_to_all(send_gates, 'expert', split_axis=0, concat_axis=0, tiled=T...  9.32 us
    all_to_all x1, starting transfers between devices, shards(): lax.all_to_all(send_cotan, 'expert', split_axis=0, concat_axis=0, tiled=T...  8.13 us
  transfers between devices with their start and end apart: 6, of which 6 were waited for; matrix products, arithmetic and copies ran while one was open for 6% of the time, Pallas kernels for 0%

commit v1 on v0

v1 whole, which is shorter than its diff:
```python
import functools

import jax
import jax.numpy as jnp
from jax import lax
from jax.experimental import pallas as pl
from jax.experimental.pallas import tpu as pltpu
from jax.sharding import PartitionSpec as P

EXPERTS = 4
CAP = 2


def select_kernel(ids_ref, gates_ref, tokens_ref, cotan_ref, send_ref, table_ref, rows_ref, sems):
    slots, tokens = table_ref.shape
    features = tokens_ref.shape[1]
    slot = lax.broadcasted_iota(jnp.int32, (slots, tokens), 0)
    expert, place = slot // CAP, slot % CAP
    first = ids_ref[0:1, :] == expert
    second = ids_ref[1:2, :] == expert
    named = jnp.where(first | second, 1.0, 0.0)
    earlier = lax.broadcasted_iota(jnp.int32, (tokens, tokens), 0) < lax.broadcasted_iota(
        jnp.int32, (tokens, tokens), 1
    )
    before = jnp.dot(
        named.astype(jnp.bfloat16),
        jnp.where(earlier, 1.0, 0.0).astype(jnp.bfloat16),
        preferred_element_type=jnp.float32,
    )
    table = jnp.where(before == place.astype(jnp.float32), named, 0.0)
    gates = gates_ref[...].astype(jnp.float32)
    gate = jnp.where(first, gates[0:1, :], gates[1:2, :])
    table_ref[...] = table.astype(jnp.bfloat16)
    for weight, source_ref, start in (
        (table, tokens_ref, 0),
        (table * gate, cotan_ref, features),
    ):
        picked = jnp.dot(
            weight.astype(jnp.bfloat16), source_ref[...], preferred_element_type=jnp.float32
        )
        for e in range(EXPERTS):
            rows_ref[e, :, start : start + features] = picked[e * CAP : (e + 1) * CAP].astype(
                jnp.bfloat16
            )
    copies = [
        pltpu.make_async_copy(rows_ref, send_ref.at[:, piece], sems.at[piece])
        for piece in range(send_ref.shape[1])
    ]
    for copy in copies:
        copy.start()
    for copy in copies:
        copy.wait()


def grads_kernel(width, core_ref, rows_ref, gate_ref, up_ref, down_ref, mine_ref, other_ref, pre_ref):
    sources, cap, both = rows_ref.shape
    features = both // 2
    chunks, _, lanes = mine_ref.shape
    inputs = rows_ref[:, :, :features].reshape(sources * cap, features)
    cotan = rows_ref[:, :, features:].reshape(sources * cap, features)
    across = (((1,), (1,)), ((), ()))
    gate_pre = lax.dot_general(gate_ref[...], inputs, across, preferred_element_type=jnp.float32)
    up_pre = lax.dot_general(up_ref[...], inputs, across, preferred_element_type=jnp.float32)
    hidden = lax.dot_general(down_ref[...], cotan, across, preferred_element_type=jnp.float32)
    sig = 1.0 / (1.0 + jnp.exp(-gate_pre))
    activation = (gate_pre * sig * up_pre).astype(jnp.bfloat16)
    grad_up = hidden * gate_pre * sig
    grad_gate = hidden * up_pre * sig * (1.0 + gate_pre * (1.0 - sig))
    pre = jnp.concatenate([grad_gate, grad_up], axis=0).astype(jnp.bfloat16)
    pre_ref[...] = pre
    beyond = jnp.zeros((sources * cap, lanes - lanes // 2), jnp.bfloat16)
    inputs = jnp.concatenate([inputs, beyond], axis=1)
    cotan = jnp.concatenate([cotan, beyond], axis=1)
    for chunk in range(chunks):
        pair = []
        for core in range(2):
            start = (chunk * 2 + core) * width
            part = jnp.concatenate(
                [
                    jnp.dot(
                        pre, inputs[:, start : start + lanes], preferred_element_type=jnp.float32
                    ),
                    jnp.dot(
                        activation,
                        cotan[:, start : start + lanes],
                        preferred_element_type=jnp.float32,
                    ),
                ],
                axis=0,
            )
            pair.append(part.astype(jnp.bfloat16))

        @pl.when(core_ref[0] == 0)
        def _():
            mine_ref[chunk] = pair[0]
            other_ref[chunk] = pair[1]

        @pl.when(core_ref[0] == 1)
        def _():
            mine_ref[chunk] = pair[1]
            other_ref[chunk] = pair[0]


def shards(tokens, cotangent, gates, route_ids, w_gate, w_up, w_down):
    device_count = lax.axis_size("expert")
    replicas = lax.axis_size("dp")
    pieces = device_count // EXPERTS
    token_count, feature_count = tokens.shape
    hidden = w_gate.shape[0]
    chips = replicas // 2
    width = feature_count // replicas
    lanes = -(-width // 128) * 128
    vmem = pl.BlockSpec(memory_space=pltpu.VMEM)
    send, table = pl.pallas_call(
        select_kernel,
        out_shape=(
            jax.ShapeDtypeStruct((EXPERTS, pieces, CAP, 2 * feature_count), jnp.bfloat16),
            jax.ShapeDtypeStruct((EXPERTS * CAP, token_count), jnp.bfloat16),
        ),
        in_specs=[vmem] * 4,
        out_specs=(pl.BlockSpec(memory_space=pltpu.HBM), vmem),
        scratch_shapes=[
            pltpu.VMEM((EXPERTS, CAP, 2 * feature_count), jnp.bfloat16),
            pltpu.SemaphoreType.DMA((pieces,)),
        ],
        compiler_params=pltpu.CompilerParams(vmem_limit_bytes=16 * 2**20),
    )(route_ids.T, gates.T, tokens, cotangent)
    arrived = lax.all_to_all(
        send.reshape(device_count, CAP, 2 * feature_count),
        "expert",
        split_axis=0,
        concat_axis=0,
        tiled=True,
    )
    core = (lax.axis_index("dp") % 2).astype(jnp.int32).reshape(1)
    mine, other, pre = pl.pallas_call(
        functools.partial(grads_kernel, width),
        out_shape=(
            jax.ShapeDtypeStruct((chips, 3 * hidden, lanes), jnp.bfloat16),
            jax.ShapeDtypeStruct((chips, 3 * hidden, lanes), jnp.bfloat16),
            jax.ShapeDtypeStruct((2 * hidden, device_count * CAP), jnp.bfloat16),
        ),
        in_specs=[pl.BlockSpec(memory_space=pltpu.SMEM)] + [vmem] * 4,
        out_specs=(vmem, vmem, vmem),
        compiler_params=pltpu.CompilerParams(vmem_limit_bytes=40 * 2**20),
    )(core, arrived, w_gate, w_up, w_down)
    swap = [(i, i ^ 1) for i in range(replicas)]
    theirs = lax.ppermute(other, "dp", swap)
    chip_sum = (mine.astype(jnp.float32) + theirs.astype(jnp.float32)).astype(jnp.bfloat16)
    chip_sum, pre = lax.optimization_barrier((chip_sum, pre))
    same_core = [[2 * x + c for x in range(chips)] for c in range(2)]
    summed = lax.psum_scatter(
        chip_sum.reshape(chips * 3 * hidden, lanes),
        "dp",
        scatter_dimension=0,
        axis_index_groups=same_core,
        tiled=True,
    )
    down_first = (((0,), (0,)), ((), ()))
    partial = lax.dot_general(pre[:hidden], w_gate, down_first, preferred_element_type=jnp.float32)
    partial = partial + lax.dot_general(
        pre[hidden:], w_up, down_first, preferred_element_type=jnp.float32
    )
    piece_grad = partial.astype(jnp.bfloat16).reshape(device_count, CAP, feature_count)
    returned = lax.all_to_all(piece_grad, "expert", split_axis=0, concat_axis=0, tiled=True)
    returned_rows = returned.reshape(device_count * CAP, feature_count)
    pair_table = jnp.broadcast_to(
        table.reshape(EXPERTS, 1, CAP, token_count), (EXPERTS, pieces, CAP, token_count)
    ).reshape(device_count * CAP, token_count)
    grad_tokens = jnp.dot(pair_table.T, returned_rows, preferred_element_type=jnp.float32).astype(
        jnp.bfloat16
    )
    return (
        grad_tokens,
        summed[:hidden, :width],
        summed[hidden : 2 * hidden, :width],
        summed[2 * hidden :, :width],
    )


def solution(mesh):
    in_specs = (
        P(("expert", "dp"), None),
        P(("expert", "dp"), None),
        P(("expert", "dp"), None),
        P(("expert", "dp"), None),
        P("expert", None),
        P("expert", None),
        P("expert", None),
    )
    out_specs = (P(("expert", "dp"), None), P("expert", "dp"), P("expert", "dp"), P("expert", "dp"))
    return jax.shard_map(shards, mesh=mesh, in_specs=in_specs, out_specs=out_specs, check_vma=False)
```

time: 324 us -> 149 us (0.46)
  the two profiles are of different devices: /device:TPU:1 before, /device:TPU:6 now
where the time goes in v1:
time: 149 us
  waiting for transfers between devices  54.3 us (36%)
  blocking collectives  34.5 us (23%)
  starting transfers between devices  25.5 us (17%)
  between operations  14.1 us (9%)
  local copies, waits for them, and re-layouts  10.6 us (7%)
  Pallas kernels  5.71 us (4%)
  matrix products  2.21 us (1%)
  other arithmetic  1.83 us (1%)
    all_to_all x1, waiting for transfers between devices, shards(): lax.all_to_all(send.reshape(device_count, CAP, 2 * feature_count), 'exper...  47 us
    all_to_all x1, blocking collectives, shards(): lax.all_to_all(piece_grad, 'expert', split_axis=0, concat_axis=0, tiled=T...  34.5 us
    all_to_all x1, starting transfers between devices, shards(): lax.all_to_all(send.reshape(device_count, CAP, 2 * feature_count), 'exper...  23.5 us
    unnamed x18, local copies, waits for them, and re-layouts  8.24 us
    pallas_call x1, Pallas kernels, shards(): pl.pallas_call(functools.partial(grads_kernel, width), out_shape=(jax.Sha...  4.49 us
    ppermute x1, waiting for transfers between devices, shards(): theirs = lax.ppermute(other, 'dp', swap)  3.8 us
    reduce_scatter x1, waiting for transfers between devices, shards(): lax.psum_scatter(chip_sum.reshape(chips * 3 * hidden, lanes), 'dp', scatt...  3.5 us
  transfers between devices with their start and end apart: 3, of which 3 were waited for; matrix products, arithmetic and copies ran while one was open for 2% of the time, Pallas kernels for 0%

profile of v1, /device:TPU:6, one launch (start us, length us, event | category | flops | bytes accessed | tf_op | source)
XLA Modules:
  0.0 148.8 jit_solution(3293319290588898076)
XLA Ops:
  7.2 0.0 copy-start.5
  7.2 1.2 copy-done.5
  8.3 0.0 copy-start.6
  8.3 1.2 copy-done.6
  9.5 0.0 copy-start.7
  9.5 0.7 copy-done.7
  10.2 0.0 copy-start.8
  10.2 0.7 copy-done.8
  10.9 1.2 shard_map.102
  12.1 0.0 copy-start.3
  12.1 1.3 copy-done.3
  13.4 0.0 copy-start
  13.4 23.5 %all-to-all-start = ((bf16[64,2,7168]{2,1,0:T(2,128)(2,1)}), bf16[64,2,7168]{2,1,0:T(2,128)(2,1)S(1)}, u32[]{:S(2)}, u32[]{:S(2)}) async-start(bf16[64,2,7168]{2,1,0:T(2,128)(2,1)} %bitcast.11), calls=%async_computation | async-start | bytes 3670016 | tf_op jit(solution)/shard_map/all_to_all | solution.py:128
  36.9 0.0 reduce-scatter.2.cloned.1.call-start
  37.0 47.0 %all-to-all-done.rows_ref = bf16[64,2,7168]{2,1,0:T(2,128)(2,1)S(1)} async-done(((bf16[64,2,7168]{2,1,0:T(2,128)(2,1)}), bf16[64,2,7168]{2,1,0:T(2,128)(2,1)S(1)}, u32[]{:S(2)}, u32[]{:S(2)}) %all-to-all-start) | async-done | bytes 1835040 | tf_op jit(solution)/shard_map/all_to_all | solution.py:128
  83.9 0.0 copy-done
  83.9 0.0 copy-start.1
  83.9 1.2 copy-done.1
  85.2 0.0 copy-start.4
  85.2 1.2 copy-done.4
  86.4 4.5 %shard_map.103 = (bf16[8,456,256]{2,1,0:T(8,128)(2,1)S(1)}, bf16[8,456,256]{2,1,0:T(8,128)(2,1)S(1)}, bf16[304,128]{1,0:T(8,128)(2,1)S(1)}) custom-call(s32[1]{0:T(128)} %bitcast.4.core_ref, bf16[64,2,7168]{2,1,0:T(2,128)(2,1)S(1)} %all-to-all-done.rows_ref, bf16[152,3584]{1,0:T(8,128)(2,1)S(1)} %copy-done, bf16[152,3584]{1,0:T(8,128)(2,1)S(1)} %copy-done.1, ...), custom_call_target="tpu_custom_call" | custom-call | tf_op jit(solution)/shard_map/pallas_call | solution.py:136
  90.9 1.9 %collective-permute-start = (bf16[8,456,256]{2,1,0:T(8,128)(2,1)S(1)}, bf16[8,456,256]{2,1,0:T(8,128)(2,1)S(1)}, u32[]{:S(2)}, u32[]{:S(2)}) collective-permute-start(bf16[8,456,256]{2,1,0:T(8,128)(2,1)S(1)} %get-tuple-element.14), channel_id=1, source_target_pairs={{0,1},{1,0},{2,3},{3,2},{4,5},{5,4},{6,7},{7,6},{8,9},{9,8},{10,11... | collective-permute-start | bytes 5603336 | tf_op jit(solution)/shard_map/ppermute | solution.py:148
  92.9 3.8 %collective-permute-done = bf16[8,456,256]{2,1,0:T(8,128)(2,1)S(1)} collective-permute-done((bf16[8,456,256]{2,1,0:T(8,128)(2,1)S(1)}, bf16[8,456,256]{2,1,0:T(8,128)(2,1)S(1)}, u32[]{:S(2)}, u32[]{:S(2)}) %collective-permute-start) | collective-permute-done | bytes 1867808 | tf_op jit(solution)/shard_map/ppermute | solution.py:148
  96.6 1.8 %add_convert_fusion = bf16[8,456,256]{2,1,0:T(8,128)(2,1)} fusion(bf16[8,456,256]{2,1,0:T(8,128)(2,1)S(1)} %collective-permute-done, bf16[8,456,256]{2,1,0:T(8,128)(2,1)S(1)} %get-tuple-element.13), kind=kLoop, calls=%fused_computation.3 | loop fusion | flops 3735552 | bytes 5603328 | tf_op jit(solution)/shard_map/convert_element_type | solution.py:149
  98.5 0.0 reduce-scatter.2.cloned.1.call-update
  98.5 0.0 copy-start.2
  98.5 0.4 fusion.2
  98.9 0.8 copy-done.2
  99.7 0.4 fusion
  100.2 0.3 reshape.31
  100.5 34.5 %all_to_all.10 = bf16[64,2,3584]{2,1,0:T(2,128)(2,1)S(1)} all-to-all(bf16[64,2,3584]{2,1,0:T(2,128)(2,1)S(1)} %reshape.31), channel_id=1, replica_groups=mesh['expert'=64,'dp'=16] {'expert'}, dimensions={0} | all-to-all | bytes 1835008 | tf_op jit(solution)/shard_map/all_to_all | solution.py:165
  135.0 0.3 reshape.32
  135.4 1.3 convolution_convert_fusion
  136.8 3.5 %reduce-scatter.2.cloned.1.call-done = bf16[456,256]{1,0:T(8,128)(2,1)} async-done(((bf16[3648,256]{1,0:T(8,128)(2,1)}), bf16[456,256]{1,0:T(8,128)(2,1)}) %reduce-scatter.2.cloned.1.call-update) | async-done | bytes 233488 | tf_op jit(solution)/shard_map/reduce_scatter | solution.py:152
  140.3 1.6 %fusion.4 = (bf16[152,224]{1,0:T(8,128)(2,1)}, bf16[152,224]{1,0:T(8,128)(2,1)}, bf16[152,224]{1,0:T(8,128)(2,1)}) fusion(bf16[456,256]{1,0:T(8,128)(2,1)} %reduce-scatter.2.cloned.1.call-done), kind=kLoop, calls=%fused_computation.7 | loop fusion | bytes 408576 | tf_op jit(solution)/shard_map/slice | solution.py:177
  (1 shorter events, 0.0 us)
Async XLA Ops:
  7.2 1.2 copy-start.5
  8.3 1.2 copy-start.6
  9.5 0.7 copy-start.7
  10.2 0.7 copy-start.8
  12.1 1.3 copy-start.3
  13.4 70.6 %copy-start = (bf16[152,3584]{1,0:T(8,128)(2,1)S(1)}, bf16[152,3584]{1,0:T(8,128)(2,1)}, u32[]{:S(2)}) copy-start(bf16[152,3584]{1,0:T(8,128)(2,1)} %gate_ref.1) | copy-start | bytes 3268612
  13.4 70.6 %all-to-all-start = ((bf16[64,2,7168]{2,1,0:T(2,128)(2,1)}), bf16[64,2,7168]{2,1,0:T(2,128)(2,1)S(1)}, u32[]{:S(2)}, u32[]{:S(2)}) async-start(bf16[64,2,7168]{2,1,0:T(2,128)(2,1)} %bitcast.11), calls=%async_computation | async-start | bytes 3670016 | tf_op jit(solution)/shard_map/all_to_all | solution.py:128
  36.9 103.4 %reduce-scatter.2.cloned.1.call-start = ((), (), s32[]{:S(2)}) async-start(), calls=%async_computation.3 | async-start | bytes 2101248 | tf_op jit(solution)/shard_map/reduce_scatter | solution.py:152
  83.9 1.2 copy-start.1
  85.2 1.2 copy-start.4
  90.9 5.7 %collective-permute-start = (bf16[8,456,256]{2,1,0:T(8,128)(2,1)S(1)}, bf16[8,456,256]{2,1,0:T(8,128)(2,1)S(1)}, u32[]{:S(2)}, u32[]{:S(2)}) collective-permute-start(bf16[8,456,256]{2,1,0:T(8,128)(2,1)S(1)} %get-tuple-element.14), channel_id=1, source_target_pairs={{0,1},{1,0},{2,3},{3,2},{4,5},{5,4},{6,7},{7,6},{8,9},{9,8},{10,11... | collective-permute-start | bytes 5603336 | tf_op jit(solution)/shard_map/ppermute | solution.py:148
  98.5 1.2 copy-start.2
Sparse Core Ops, SparseCore 0:
  98.6 41.5 reduce-scatter.1

commit v2 on v1

v2 whole, which is shorter than its diff:
```python
import functools

import jax
import jax.numpy as jnp
from jax import lax
from jax.experimental import pallas as pl
from jax.experimental.pallas import tpu as pltpu
from jax.sharding import PartitionSpec as P

EXPERTS = 4
CAP = 2


def select_kernel(
    ids_hbm, gates_hbm, tokens_hbm, cotan_hbm, send_ref, table_ref, ids_ref, gates_ref, tokens_ref,
    cotan_ref, rows_ref, in_sems, out_sems,
):
    slots, tokens = table_ref.shape
    loads = [
        pltpu.make_async_copy(source, target, in_sems.at[index])
        for index, (source, target) in enumerate(
            (
                (ids_hbm, ids_ref),
                (gates_hbm, gates_ref),
                (tokens_hbm, tokens_ref),
                (cotan_hbm, cotan_ref),
            )
        )
    ]
    for load in loads:
        load.start()
    slot = lax.broadcasted_iota(jnp.int32, (slots, tokens), 0)
    expert, place = slot // CAP, slot % CAP
    earlier = lax.broadcasted_iota(jnp.int32, (tokens, tokens), 0) < lax.broadcasted_iota(
        jnp.int32, (tokens, tokens), 1
    )
    earlier = jnp.where(earlier, 1.0, 0.0).astype(jnp.bfloat16)
    loads[0].wait()
    first = ids_ref[0:1, :] == expert
    second = ids_ref[1:2, :] == expert
    named = jnp.where(first | second, 1.0, 0.0)
    before = jnp.dot(named.astype(jnp.bfloat16), earlier, preferred_element_type=jnp.float32)
    table = jnp.where(before == place.astype(jnp.float32), named, 0.0)
    table_ref[...] = table.astype(jnp.bfloat16)
    loads[1].wait()
    gates = gates_ref[...].astype(jnp.float32)
    gated = table * jnp.where(first, gates[0:1, :], gates[1:2, :])
    stores = []
    for half, (weight, source_ref) in enumerate(((table, tokens_ref), (gated, cotan_ref))):
        loads[2 + half].wait()
        picked = jnp.dot(
            weight.astype(jnp.bfloat16), source_ref[...], preferred_element_type=jnp.float32
        )
        for e in range(EXPERTS):
            rows_ref[half, e] = picked[e * CAP : (e + 1) * CAP].astype(jnp.bfloat16)
        for piece in range(half, send_ref.shape[1], 2):
            store = pltpu.make_async_copy(
                rows_ref.at[half], send_ref.at[:, piece], out_sems.at[piece]
            )
            store.start()
            stores.append(store)
    for store in stores:
        store.wait()


def chunk_grads(width, lanes, core, pre, activation, inputs, cotan, out_ref):
    for chunk in range(out_ref.shape[0]):
        start = (chunk * 2 + core) * width
        part = jnp.concatenate(
            [
                jnp.dot(pre, inputs[:, start : start + lanes], preferred_element_type=jnp.float32),
                jnp.dot(
                    activation, cotan[:, start : start + lanes], preferred_element_type=jnp.float32
                ),
            ],
            axis=0,
        )
        out_ref[chunk] = part.astype(jnp.bfloat16)


def flatten(rows_ref, lanes):
    sources, cap, features = rows_ref.shape
    flat = rows_ref[...].reshape(sources * cap, features)
    beyond = jnp.zeros((sources * cap, lanes - features), jnp.bfloat16)
    return jnp.concatenate([flat, beyond], axis=1)


def project(weight_ref, rows):
    across = (((1,), (1,)), ((), ()))
    features = weight_ref.shape[1]
    return lax.dot_general(
        weight_ref[...], rows[:, :features], across, preferred_element_type=jnp.float32
    )


def first_kernel(
    odd_ref, rows_ref, gate_ref, up_hbm, down_hbm, flat_ref, up_ref, down_ref, forward_ref, back_ref,
    sems,
):
    load_up = pltpu.make_async_copy(up_hbm, up_ref, sems.at[0])
    load_down = pltpu.make_async_copy(down_hbm, down_ref, sems.at[1])
    load_up.start()
    load_down.start()
    flat_ref[...] = flatten(rows_ref, flat_ref.shape[1])

    @pl.when(odd_ref[0] == 0)
    def _():
        forward_ref[0] = project(gate_ref, flat_ref)

    load_up.wait()
    load_down.wait()

    @pl.when(odd_ref[0] == 0)
    def _():
        forward_ref[1] = project(up_ref, flat_ref)

    @pl.when(odd_ref[0] == 1)
    def _():
        back_ref[...] = project(down_ref, flat_ref)


def passes_kernel(
    width, core_ref, odd_ref, first_ref, low_ref, high_ref, gate_ref, up_ref, down_ref, done_forward_ref,
    done_back_ref, other_ref, pre_ref, act_ref, flat_ref, forward_ref, back_ref,
):
    lanes = other_ref.shape[2]
    half = flat_ref.shape[1] // 2
    odd = odd_ref[0]
    flat_ref[odd] = first_ref[...]
    flat_ref[1 - odd, :half] = flatten(low_ref, flat_ref.shape[2])
    flat_ref[1 - odd, half:] = flatten(high_ref, flat_ref.shape[2])

    @pl.when(odd == 0)
    def _():
        forward_ref[...] = done_forward_ref[...]
        back_ref[...] = project(down_ref, flat_ref.at[1])

    @pl.when(odd == 1)
    def _():
        forward_ref[0] = project(gate_ref, flat_ref.at[0])
        forward_ref[1] = project(up_ref, flat_ref.at[0])
        back_ref[...] = done_back_ref[...]

    gate_pre, up_pre, hidden = forward_ref[0], forward_ref[1], back_ref[...]
    sig = 1.0 / (1.0 + jnp.exp(-gate_pre))
    activation = (gate_pre * sig * up_pre).astype(jnp.bfloat16)
    grad_up = hidden * gate_pre * sig
    grad_gate = hidden * up_pre * sig * (1.0 + gate_pre * (1.0 - sig))
    pre = jnp.concatenate([grad_gate, grad_up], axis=0).astype(jnp.bfloat16)
    pre_ref[...] = pre
    act_ref[...] = activation
    for core in range(2):

        @pl.when(core_ref[0] == core)
        def _():
            chunk_grads(
                width, lanes, 1 - core, pre, activation, flat_ref[0], flat_ref[1], other_ref
            )


def own_kernel(width, core_ref, pre_ref, act_ref, flat_ref, mine_ref):
    lanes = mine_ref.shape[2]
    for core in range(2):

        @pl.when(core_ref[0] == core)
        def _():
            chunk_grads(
                width, lanes, core, pre_ref[...], act_ref[...], flat_ref[0], flat_ref[1], mine_ref
            )


def shards(tokens, cotangent, gates, route_ids, w_gate, w_up, w_down):
    device_count = lax.axis_size("expert")
    replicas = lax.axis_size("dp")
    pieces = device_count // EXPERTS
    token_count, feature_count = tokens.shape
    hidden = w_gate.shape[0]
    chips = replicas // 2
    width = feature_count // replicas
    lanes = -(-width // 128) * 128
    rows = device_count * CAP
    vmem = pl.BlockSpec(memory_space=pltpu.VMEM)
    smem = pl.BlockSpec(memory_space=pltpu.SMEM)
    hbm = pl.BlockSpec(memory_space=pltpu.HBM)
    in_hbm = functools.partial(pltpu.with_memory_space_constraint, memory_space=pltpu.HBM)
    send, table = pl.pallas_call(
        select_kernel,
        out_shape=(
            pltpu.HBM((EXPERTS, pieces, CAP, feature_count), jnp.bfloat16),
            jax.ShapeDtypeStruct((EXPERTS * CAP, token_count), jnp.bfloat16),
        ),
        in_specs=[hbm] * 4,
        out_specs=(hbm, vmem),
        scratch_shapes=[
            pltpu.VMEM((2, token_count), jnp.int32),
            pltpu.VMEM((2, token_count), jnp.bfloat16),
            pltpu.VMEM((token_count, feature_count), jnp.bfloat16),
            pltpu.VMEM((token_count, feature_count), jnp.bfloat16),
            pltpu.VMEM((2, EXPERTS, CAP, feature_count), jnp.bfloat16),
            pltpu.SemaphoreType.DMA((4,)),
            pltpu.SemaphoreType.DMA((pieces,)),
        ],
        compiler_params=pltpu.CompilerParams(vmem_limit_bytes=16 * 2**20),
    )(in_hbm(route_ids.T), in_hbm(gates.T), in_hbm(tokens), in_hbm(cotangent))
    arrived = lax.all_to_all(
        send.reshape(device_count, CAP, feature_count),
        "expert",
        split_axis=0,
        concat_axis=0,
        tiled=True,
    )
    ring = pieces // 2
    after = [(i, i // ring * ring + (i + 1) % ring) for i in range(device_count)]
    before = [(i, i // ring * ring + (i - 1) % ring) for i in range(device_count)]
    low = lax.ppermute(arrived[: device_count // 2], "expert", after)
    high = lax.ppermute(arrived[device_count // 2 :], "expert", before)
    odd = (lax.axis_index("expert") & 1).astype(jnp.int32).reshape(1)
    core = (lax.axis_index("dp") & 1).astype(jnp.int32).reshape(1)
    flat_lanes = feature_count + lanes // 2
    weight_shape = jax.ShapeDtypeStruct((hidden, feature_count), jnp.bfloat16)
    forward_shape = jax.ShapeDtypeStruct((2, hidden, rows), jnp.float32)
    back_shape = jax.ShapeDtypeStruct((hidden, rows), jnp.float32)
    first, up_here, down_here, forward, back = pl.pallas_call(
        first_kernel,
        out_shape=(
            jax.ShapeDtypeStruct((rows, flat_lanes), jnp.bfloat16),
            weight_shape,
            weight_shape,
            forward_shape,
            back_shape,
        ),
        in_specs=[smem, vmem, vmem, hbm, hbm],
        out_specs=(vmem,) * 5,
        scratch_shapes=[pltpu.SemaphoreType.DMA((2,))],
        compiler_params=pltpu.CompilerParams(vmem_limit_bytes=32 * 2**20),
        cost_estimate=pl.CostEstimate(
            flops=4 * hidden * rows * feature_count, bytes_accessed=8 * 2**20, transcendentals=0
        ),
    )(odd, arrived, w_gate, in_hbm(w_up), in_hbm(w_down))
    grads_shape = jax.ShapeDtypeStruct((chips, 3 * hidden, lanes), jnp.bfloat16)
    other, pre, activation, flat = pl.pallas_call(
        functools.partial(passes_kernel, width),
        out_shape=(
            grads_shape,
            jax.ShapeDtypeStruct((2 * hidden, rows), jnp.bfloat16),
            jax.ShapeDtypeStruct((hidden, rows), jnp.bfloat16),
            jax.ShapeDtypeStruct((2, rows, flat_lanes), jnp.bfloat16),
        ),
        in_specs=[smem, smem] + [vmem] * 8,
        out_specs=(vmem,) * 4,
        scratch_shapes=[
            pltpu.VMEM((2, hidden, rows), jnp.float32),
            pltpu.VMEM((hidden, rows), jnp.float32),
        ],
        compiler_params=pltpu.CompilerParams(vmem_limit_bytes=32 * 2**20),
    )(core, odd, first, low, high, w_gate, up_here, down_here, forward, back)
    swap = [(i, i ^ 1) for i in range(replicas)]
    theirs = lax.ppermute(other, "dp", swap)
    mine = pl.pallas_call(
        functools.partial(own_kernel, width),
        out_shape=grads_shape,
        in_specs=[smem] + [vmem] * 3,
        out_specs=vmem,
        compiler_params=pltpu.CompilerParams(vmem_limit_bytes=32 * 2**20),
        cost_estimate=pl.CostEstimate(
            flops=6 * hidden * rows * feature_count, bytes_accessed=4 * 2**20, transcendentals=0
        ),
    )(core, pre, activation, flat)
    chip_sum = (mine.astype(jnp.float32) + theirs.astype(jnp.float32)).astype(jnp.bfloat16)
    chip_sum, pre = lax.optimization_barrier((chip_sum, pre))
    same_core = [[2 * x + c for x in range(chips)] for c in range(2)]
    summed = lax.psum_scatter(
        chip_sum.reshape(chips * 3 * hidden, lanes),
        "dp",
        scatter_dimension=0,
        axis_index_groups=same_core,
        tiled=True,
    )
    down_first = (((0,), (0,)), ((), ()))
    partial = lax.dot_general(pre[:hidden], w_gate, down_first, preferred_element_type=jnp.float32)
    partial = partial + lax.dot_general(
        pre[hidden:], w_up, down_first, preferred_element_type=jnp.float32
    )
    piece_grad = partial.astype(jnp.bfloat16).reshape(device_count, CAP, feature_count)
    returned = lax.all_to_all(piece_grad, "expert", split_axis=0, concat_axis=0, tiled=True)
    returned_rows = returned.reshape(device_count * CAP, feature_count)
    pair_table = jnp.broadcast_to(
        table.reshape(EXPERTS, 1, CAP, token_count), (EXPERTS, pieces, CAP, token_count)
    ).reshape(device_count * CAP, token_count)
    grad_tokens = jnp.dot(pair_table.T, returned_rows, preferred_element_type=jnp.float32).astype(
        jnp.bfloat16
    )
    return (
        grad_tokens,
        summed[:hidden, :width],
        summed[hidden : 2 * hidden, :width],
        summed[2 * hidden :, :width],
    )


def solution(mesh):
    in_specs = (
        P(("expert", "dp"), None),
        P(("expert", "dp"), None),
        P(("expert", "dp"), None),
        P(("expert", "dp"), None),
        P("expert", None),
        P("expert", None),
        P("expert", None),
    )
    out_specs = (P(("expert", "dp"), None), P("expert", "dp"), P("expert", "dp"), P("expert", "dp"))
    return jax.shard_map(shards, mesh=mesh, in_specs=in_specs, out_specs=out_specs, check_vma=False)
```

time: 149 us -> 138 us (0.926)
  blocking collectives: 34.5 us -> 86.2 us
  waiting for transfers between devices: 54.3 us -> 9.64 us
  starting transfers between devices: 25.5 us -> 9 us
  local copies, waits for them, and re-layouts: 10.6 us -> 6.56 us
    all_to_all x0 -> x1, blocking collectives: none -> 50.6 us  [shards(): lax.all_to_all(send.reshape(device_count, CAP, feature_count), 'expert',...]
    all_to_all x1 -> x0, waiting for transfers between devices: 47 us -> none  [shards(): lax.all_to_all(send.reshape(device_count, CAP, 2 * feature_count), 'exper...]
    all_to_all x1 -> x0, starting transfers between devices: 23.5 us -> none  [shards(): lax.all_to_all(send.reshape(device_count, CAP, 2 * feature_count), 'exper...]
    unnamed x18 -> x4, local copies, waits for them, and re-layouts: 8.24 us -> 0.8 us
    ppermute x0 -> x2, starting transfers between devices: none -> 7.04 us  [the longest x1 4.01 us: shards(): high = lax.ppermute(arrived[device_count // 2:], 'expert', before)]
    ppermute x0 -> x2, waiting for transfers between devices: none -> 5.93 us  [the longest x1 4.15 us: shards(): low = lax.ppermute(arrived[:device_count // 2], 'expert', after)]
    reduce_scatter x1, waiting for transfers between devices: 3.5 us -> 0.59 us  [shards(): lax.psum_scatter(chip_sum.reshape(chips * 3 * hidden, lanes), 'dp', scatt...]
    reshape x1, local copies, waits for them, and re-layouts: 0.35 us -> 2.34 us  [shards(): partial.astype(jnp.bfloat16).reshape(device_count, CAP, feature_count)]
  transfers between devices with their start and end apart: 3 -> 4, of which waited for: 3 -> 4; matrix products, arithmetic and copies ran while one was open for 2% -> 4% of each run, Pallas kernels for 0% -> 2%
where the time goes in v2:
time: 138 us; the launch traced here: 137 us
  blocking collectives  86.2 us (62%)
  between operations  14.1 us (10%)
  waiting for transfers between devices  9.64 us (7%)
  starting transfers between devices  9 us (7%)
  Pallas kernels  6.85 us (5%)
  local copies, waits for them, and re-layouts  6.56 us (5%)
  matrix products  3.15 us (2%)
  other arithmetic  1.86 us (1%)
    all_to_all x1, blocking collectives, shards(): lax.all_to_all(send.reshape(device_count, CAP, feature_count), 'expert',...  50.6 us
    all_to_all x1, blocking collectives, shards(): lax.all_to_all(piece_grad, 'expert', split_axis=0, concat_axis=0, tiled=T...  35.6 us
    ppermute x1, waiting for transfers between devices, shards(): low = lax.ppermute(arrived[:device_count // 2], 'expert', after)  4.15 us
    ppermute x1, starting transfers between devices, shards(): high = lax.ppermute(arrived[device_count // 2:], 'expert', before)  4.01 us
    ppermute x1, waiting for transfers between devices, shards(): theirs = lax.ppermute(other, 'dp', swap)  3.1 us
    ppermute x1, starting transfers between devices, shards(): low = lax.ppermute(arrived[:device_count // 2], 'expert', after)  3.03 us
  transfers between devices with their start and end apart: 4, of which 4 were waited for; matrix products, arithmetic and copies ran while one was open for 4% of the time, Pallas kernels for 2%

profile of v2, /device:TPU:6, one launch (start us, length us, event | category | flops | bytes accessed | tf_op | source)
XLA Modules:
  0.0 137.4 jit_solution(15892914109239897596)
XLA Ops:
  7.2 0.0 reduce-scatter.2.cloned.1.call-start
  7.2 2.7 %shard_map.102 = (bf16[4,16,2,3584]{3,2,1,0:T(2,128)(2,1)}, bf16[8,128]{1,0:T(8,128)(2,1)S(1)}) custom-call(s32[2,128]{1,0:T(2,128)} %bitcast.16, bf16[2,128]{1,0:T(2,128)(2,1)} %bitcast.17, bf16[128,3584]{1,0:T(8,128)(2,1)} %tokens_hbm.1, bf16[128,3584]{1,0:T(8,128)(2,1)} %cotan_hbm.1), custom_call_target="tpu_custom_call" | custom-call | tf_op jit(solution)/shard_map/pallas_call | solution.py:186
  9.9 0.0 copy-start
  9.9 50.6 %all_to_all.10.rows_ref = bf16[64,2,3584]{2,1,0:T(2,128)(2,1)S(1)} all-to-all(bf16[64,2,3584]{2,1,0:T(2,128)(2,1)} %bitcast.14), channel_id=1, replica_groups=mesh['expert'=64,'dp'=16] {'expert'}, dimensions={0} | all-to-all | bytes 1835008 | tf_op jit(solution)/shard_map/all_to_all | solution.py:205
  60.4 1.4 %fusion.4 = (bf16[32,2,3584]{2,1,0:T(2,128)(2,1)S(1)}, bf16[32,2,3584]{2,1,0:T(2,128)(2,1)}) fusion(bf16[64,2,3584]{2,1,0:T(2,128)(2,1)S(1)} %all_to_all.10.rows_ref), kind=kLoop, calls=%fused_computation.7 | loop fusion | bytes 1835008 | tf_op jit(solution)/shard_map/slice | solution.py:216
  61.8 3.0 %collective-permute-start = (bf16[32,2,3584]{2,1,0:T(2,128)(2,1)}, bf16[32,2,3584]{2,1,0:T(2,128)(2,1)S(1)}, u32[]{:S(2)}, u32[]{:S(2)}) collective-permute-start(bf16[32,2,3584]{2,1,0:T(2,128)(2,1)} %get-tuple-element.31), channel_id=1, source_target_pairs={{0,16},{16,32},{32,48},{48,64},{64,80},{80,96},{96,112},{112,0},{1... | collective-permute-start | bytes 1376264 | tf_op jit(solution)/shard_map/ppermute | solution.py:215
  64.9 4.0 %collective-permute-start.1 = (bf16[32,2,3584]{2,1,0:T(2,128)(2,1)S(1)}, bf16[32,2,3584]{2,1,0:T(2,128)(2,1)S(1)}, u32[]{:S(2)}, u32[]{:S(2)}) collective-permute-start(bf16[32,2,3584]{2,1,0:T(2,128)(2,1)S(1)} %get-tuple-element.30), channel_id=1, source_target_pairs={{0,112},{16,0},{32,16},{48,32},{64,48},{80,64},{96,80},{112,96},{1... | collective-permute-start | bytes 1376264 | tf_op jit(solution)/shard_map/ppermute | solution.py:216
  68.9 0.0 copy-done
  68.9 2.0 %shard_map.103 = (bf16[128,3712]{1,0:T(8,128)(2,1)S(1)}, bf16[152,3584]{1,0:T(8,128)(2,1)S(1)}, bf16[152,3584]{1,0:T(8,128)(2,1)S(1)}, f32[2,152,128]{2,1,0:T(8,128)S(1)}, f32[152,128]{1,0:T(8,128)S(1)}) custom-call(s32[1]{0:T(128)} %bitcast.5.odd_ref, bf16[64,2,3584]{2,1,0:T(2,128)(2,1)S(1)} %all_to_all.10.rows_ref, bf16[152,3584]{1,0:T(8,128)(2,1)S(1)} %copy-done, ...), custom_call_target="tpu_custom_call" | custom-call | flops 278921216 | bytes 8388608 | tf_op jit(solution)/shard_map/pallas_call | solution.py:223
  71.0 4.1 %collective-permute-done.low_ref = bf16[32,2,3584]{2,1,0:T(2,128)(2,1)S(1)} collective-permute-done((bf16[32,2,3584]{2,1,0:T(2,128)(2,1)}, bf16[32,2,3584]{2,1,0:T(2,128)(2,1)S(1)}, u32[]{:S(2)}, u32[]{:S(2)}) %collective-permute-start) | collective-permute-done | bytes 458784 | tf_op jit(solution)/shard_map/ppermute | solution.py:215
  75.1 1.8 %collective-permute-done.1.high_ref = bf16[32,2,3584]{2,1,0:T(2,128)(2,1)S(1)} collective-permute-done((bf16[32,2,3584]{2,1,0:T(2,128)(2,1)S(1)}, bf16[32,2,3584]{2,1,0:T(2,128)(2,1)S(1)}, u32[]{:S(2)}, u32[]{:S(2)}) %collective-permute-start.1) | collective-permute-done | bytes 458784 | tf_op jit(solution)/shard_map/ppermute | solution.py:216
  76.9 1.5 %shard_map.104 = (bf16[8,456,256]{2,1,0:T(8,128)(2,1)S(1)}, bf16[304,128]{1,0:T(8,128)(2,1)S(1)}, bf16[152,128]{1,0:T(8,128)(2,1)S(1)}, bf16[2,128,3712]{2,1,0:T(8,128)(2,1)S(1)}) custom-call(s32[1]{0:T(128)} %bitcast.4.core_ref, s32[1]{0:T(128)} %bitcast.5.odd_ref, bf16[128,3712]{1,0:T(8,128)(2,1)S(1)} %get-tuple-element.19.first_ref, ...), custom_call_target="tpu_custom_call" | custom-call | tf_op jit(solution)/shard_map/pallas_call | solution.py:241
  78.4 1.9 %collective-permute-start.2 = (bf16[8,456,256]{2,1,0:T(8,128)(2,1)S(1)}, bf16[8,456,256]{2,1,0:T(8,128)(2,1)S(1)}, u32[]{:S(2)}, u32[]{:S(2)}) collective-permute-start(bf16[8,456,256]{2,1,0:T(8,128)(2,1)S(1)} %get-tuple-element.27), channel_id=1, source_target_pairs={{0,1},{1,0},{2,3},{3,2},{4,5},{5,4},{6,7},{7,6},{8,9},{9,8},{10,11... | collective-permute-start | bytes 5603336 | tf_op jit(solution)/shard_map/ppermute | solution.py:258
  80.3 0.7 shard_map.105
  81.0 3.1 %collective-permute-done.2 = bf16[8,456,256]{2,1,0:T(8,128)(2,1)S(1)} collective-permute-done((bf16[8,456,256]{2,1,0:T(8,128)(2,1)S(1)}, bf16[8,456,256]{2,1,0:T(8,128)(2,1)S(1)}, u32[]{:S(2)}, u32[]{:S(2)}) %collective-permute-start.2) | collective-permute-done | bytes 1867808 | tf_op jit(solution)/shard_map/ppermute | solution.py:258
  84.1 1.9 %add_convert_fusion = bf16[8,456,256]{2,1,0:T(8,128)(2,1)} fusion(bf16[8,456,256]{2,1,0:T(8,128)(2,1)S(1)} %collective-permute-done.2, bf16[8,456,256]{2,1,0:T(8,128)(2,1)S(1)} %shard_map.105), kind=kLoop, calls=%fused_computation.3 | loop fusion | flops 3735552 | bytes 5603328 | tf_op jit(solution)/shard_map/convert_element_type | solution.py:269
  86.0 0.0 reduce-scatter.2.cloned.1.call-update
  86.0 0.0 copy-start.1
  86.0 0.4 fusion.2
  86.4 0.8 copy-done.1
  87.2 1.4 fusion
  88.6 2.3 %reshape.35 = bf16[64,2,3584]{2,1,0:T(2,128)(2,1)S(1)} reshape(bf16[128,3584]{1,0:T(8,128)(2,1)} %fusion) | data formatting | bytes 1835008 | tf_op jit(solution)/shard_map/reshape | solution.py:284
  90.9 35.6 %all_to_all.11 = bf16[64,2,3584]{2,1,0:T(2,128)(2,1)S(1)} all-to-all(bf16[64,2,3584]{2,1,0:T(2,128)(2,1)S(1)} %reshape.35), channel_id=1, replica_groups=mesh['expert'=64,'dp'=16] {'expert'}, dimensions={0} | all-to-all | bytes 1835008 | tf_op jit(solution)/shard_map/all_to_all | solution.py:285
  126.5 0.3 reshape.36
  126.9 1.4 convolution_convert_fusion
  128.3 0.6 reduce-scatter.2.cloned.1.call-done
  128.9 1.6 %fusion.5 = (bf16[152,224]{1,0:T(8,128)(2,1)}, bf16[152,224]{1,0:T(8,128)(2,1)}, bf16[152,224]{1,0:T(8,128)(2,1)}) fusion(bf16[456,256]{1,0:T(8,128)(2,1)} %reduce-scatter.2.cloned.1.call-done), kind=kLoop, calls=%fused_computation.8 | loop fusion | bytes 408576 | tf_op jit(solution)/shard_map/slice | solution.py:297
  (1 shorter events, 0.0 us)
Async XLA Ops:
  7.2 121.7 %reduce-scatter.2.cloned.1.call-start = ((), (), s32[]{:S(2)}) async-start(), calls=%async_computation.3 | async-start | bytes 2101248 | tf_op jit(solution)/shard_map/reduce_scatter | solution.py:272
  9.9 59.0 %copy-start = (bf16[152,3584]{1,0:T(8,128)(2,1)S(1)}, bf16[152,3584]{1,0:T(8,128)(2,1)}, u32[]{:S(2)}) copy-start(bf16[152,3584]{1,0:T(8,128)(2,1)} %gate_ref.3) | copy-start | bytes 3268612
  61.8 13.3 %collective-permute-start = (bf16[32,2,3584]{2,1,0:T(2,128)(2,1)}, bf16[32,2,3584]{2,1,0:T(2,128)(2,1)S(1)}, u32[]{:S(2)}, u32[]{:S(2)}) collective-permute-start(bf16[32,2,3584]{2,1,0:T(2,128)(2,1)} %get-tuple-element.31), channel_id=1, source_target_pairs={{0,16},{16,32},{32,48},{48,64},{64,80},{80,96},{96,112},{112,0},{1... | collective-permute-start | bytes 1376264 | tf_op jit(solution)/shard_map/ppermute | solution.py:215
  64.9 12.0 %collective-permute-start.1 = (bf16[32,2,3584]{2,1,0:T(2,128)(2,1)S(1)}, bf16[32,2,3584]{2,1,0:T(2,128)(2,1)S(1)}, u32[]{:S(2)}, u32[]{:S(2)}) collective-permute-start(bf16[32,2,3584]{2,1,0:T(2,128)(2,1)S(1)} %get-tuple-element.30), channel_id=1, source_target_pairs={{0,112},{16,0},{32,16},{48,32},{64,48},{80,64},{96,80},{112,96},{1... | collective-permute-start | bytes 1376264 | tf_op jit(solution)/shard_map/ppermute | solution.py:216
  78.4 5.7 %collective-permute-start.2 = (bf16[8,456,256]{2,1,0:T(8,128)(2,1)S(1)}, bf16[8,456,256]{2,1,0:T(8,128)(2,1)S(1)}, u32[]{:S(2)}, u32[]{:S(2)}) collective-permute-start(bf16[8,456,256]{2,1,0:T(8,128)(2,1)S(1)} %get-tuple-element.27), channel_id=1, source_target_pairs={{0,1},{1,0},{2,3},{3,2},{4,5},{5,4},{6,7},{7,6},{8,9},{9,8},{10,11... | collective-permute-start | bytes 5603336 | tf_op jit(solution)/shard_map/ppermute | solution.py:258
  86.0 1.2 copy-start.1
Sparse Core Ops, SparseCore 0:
  86.1 42.7 reduce-scatter.1

commit v3 on v2

--- a/solution.py
+++ b/solution.py
@@ -15,7 +15,7 @@
     ids_hbm, gates_hbm, tokens_hbm, cotan_hbm, send_ref, table_ref, ids_ref, gates_ref, tokens_ref,
     cotan_ref, rows_ref, in_sems, out_sems,
 ):
-    slots, tokens = table_ref.shape
+    slots, tokens = EXPERTS * CAP, table_ref.shape[1]
     loads = [
         pltpu.make_async_copy(source, target, in_sems.at[index])
         for index, (source, target) in enumerate(
@@ -41,7 +41,14 @@
     named = jnp.where(first | second, 1.0, 0.0)
     before = jnp.dot(named.astype(jnp.bfloat16), earlier, preferred_element_type=jnp.float32)
     table = jnp.where(before == place.astype(jnp.float32), named, 0.0)
-    table_ref[...] = table.astype(jnp.bfloat16)
+    sub = lax.broadcasted_iota(jnp.int32, table_ref.shape, 0)
+    per_expert = table_ref.shape[0] // EXPERTS
+    repeated = jnp.zeros(table_ref.shape, jnp.float32)
+    for e in range(EXPERTS):
+        for p in range(CAP):
+            here = (sub // per_expert == e) & (sub % CAP == p)
+            repeated = jnp.where(here, table[e * CAP + p : e * CAP + p + 1, :], repeated)
+    table_ref[...] = repeated.astype(jnp.bfloat16)
     loads[1].wait()
     gates = gates_ref[...].astype(jnp.float32)
     gated = table * jnp.where(first, gates[0:1, :], gates[1:2, :])
@@ -63,8 +70,9 @@
         store.wait()
 
 
-def chunk_grads(width, lanes, core, pre, activation, inputs, cotan, out_ref):
-    for chunk in range(out_ref.shape[0]):
+def chunk_grads(width, core, pre, activation, inputs, cotan, out_ref):
+    chunks, _, lanes = out_ref.shape
+    for chunk in range(chunks):
         start = (chunk * 2 + core) * width
         part = jnp.concatenate(
             [
@@ -78,6 +86,12 @@
         out_ref[chunk] = part.astype(jnp.bfloat16)
 
 
+def halve_kernel(rows_ref, low_ref, high_ref):
+    half = low_ref.shape[0]
+    low_ref[...] = rows_ref[:half]
+    high_ref[...] = rows_ref[half:]
+
+
 def flatten(rows_ref, lanes):
     sources, cap, features = rows_ref.shape
     flat = rows_ref[...].reshape(sources * cap, features)
@@ -94,7 +108,7 @@
 
 
 def first_kernel(
-    odd_ref, rows_ref, gate_ref, up_hbm, down_hbm, flat_ref, up_ref, down_ref, forward_ref, back_ref,
+    piece_at_ref, rows_ref, gate_ref, up_hbm, down_hbm, flat_ref, up_ref, down_ref, forward_ref, back_ref,
     sems,
 ):
     load_up = pltpu.make_async_copy(up_hbm, up_ref, sems.at[0])
@@ -103,29 +117,28 @@
     load_down.start()
     flat_ref[...] = flatten(rows_ref, flat_ref.shape[1])
 
-    @pl.when(odd_ref[0] == 0)
+    @pl.when(piece_at_ref[0] & 1 == 0)
     def _():
         forward_ref[0] = project(gate_ref, flat_ref)
 
     load_up.wait()
     load_down.wait()
 
-    @pl.when(odd_ref[0] == 0)
+    @pl.when(piece_at_ref[0] & 1 == 0)
     def _():
         forward_ref[1] = project(up_ref, flat_ref)
 
-    @pl.when(odd_ref[0] == 1)
+    @pl.when(piece_at_ref[0] & 1 == 1)
     def _():
         back_ref[...] = project(down_ref, flat_ref)
 
 
 def passes_kernel(
-    width, core_ref, odd_ref, first_ref, low_ref, high_ref, gate_ref, up_ref, down_ref, done_forward_ref,
+    width, replica_ref, piece_at_ref, first_ref, low_ref, high_ref, gate_ref, up_ref, down_ref, done_forward_ref,
     done_back_ref, other_ref, pre_ref, act_ref, flat_ref, forward_ref, back_ref,
 ):
-    lanes = other_ref.shape[2]
     half = flat_ref.shape[1] // 2
-    odd = odd_ref[0]
+    odd = piece_at_ref[0] & 1
     flat_ref[odd] = first_ref[...]
     flat_ref[1 - odd, :half] = flatten(low_ref, flat_ref.shape[2])
     flat_ref[1 - odd, half:] = flatten(high_ref, flat_ref.shape[2])
@@ -151,22 +164,64 @@
     act_ref[...] = activation
     for core in range(2):
 
-        @pl.when(core_ref[0] == core)
+        @pl.when(replica_ref[0] & 1 == core)
         def _():
-            chunk_grads(
-                width, lanes, 1 - core, pre, activation, flat_ref[0], flat_ref[1], other_ref
-            )
-
-
-def own_kernel(width, core_ref, pre_ref, act_ref, flat_ref, mine_ref):
-    lanes = mine_ref.shape[2]
+            chunk_grads(width, 1 - core, pre, activation, flat_ref[0], flat_ref[1], other_ref)
+
+
+def own_kernel(width, replica_ref, pre_ref, act_ref, flat_ref, mine_ref):
     for core in range(2):
 
-        @pl.when(core_ref[0] == core)
+        @pl.when(replica_ref[0] & 1 == core)
         def _():
-            chunk_grads(
-                width, lanes, core, pre_ref[...], act_ref[...], flat_ref[0], flat_ref[1], mine_ref
-            )
+            chunk_grads(width, core, pre_ref[...], act_ref[...], flat_ref[0], flat_ref[1], mine_ref)
+
+
+def piece_kernel(pre_ref, gate_ref, up_ref, piece_hbm, piece_ref, sem):
+    hidden = gate_ref.shape[0]
+    pre = pre_ref[...].astype(jnp.float32)
+    down = (((0,), (0,)), ((), ()))
+    piece = lax.dot_general(
+        pre[:hidden].astype(jnp.bfloat16), gate_ref[...], down, preferred_element_type=jnp.float32
+    ) + lax.dot_general(
+        pre[hidden:].astype(jnp.bfloat16), up_ref[...], down, preferred_element_type=jnp.float32
+    )
+    piece_ref[...] = piece.astype(jnp.bfloat16).reshape(piece_ref.shape)
+    store = pltpu.make_async_copy(piece_ref, piece_hbm, sem)
+    store.start()
+    store.wait()
+
+
+def combine_kernel(table_ref, rows_ref, tokens_ref):
+    flat = rows_ref[...].reshape(table_ref.shape[0], tokens_ref.shape[1])
+    total = lax.dot_general(
+        table_ref[...], flat, (((0,), (0,)), ((), ())), preferred_element_type=jnp.float32
+    )
+    tokens_ref[...] = total.astype(jnp.bfloat16)
+
+
+def added(first, second):
+    return (first.astype(jnp.float32) + second.astype(jnp.float32)).astype(jnp.bfloat16)
+
+
+def chip_kernel(replica_ref, mine_ref, theirs_ref, *out_refs):
+    chips = len(out_refs)
+    for distance, out_ref in enumerate(out_refs):
+        chunk = ((replica_ref[0] >> 1) + distance) & (chips - 1)
+        out_ref[...] = added(mine_ref[chunk], theirs_ref[chunk])
+
+
+def add_kernel(got_ref, own_ref, sum_ref):
+    sum_ref[...] = added(got_ref[...], own_ref[...])
+
+
+def total_kernel(up_ring_ref, down_ring_ref, own_ref, gate_ref, up_ref, down_ref):
+    hidden, width = gate_ref.shape
+    total = up_ring_ref[...].astype(jnp.float32) + down_ring_ref[...].astype(jnp.float32)
+    total = total + own_ref[...].astype(jnp.float32)
+    for index, out_ref in enumerate((gate_ref, up_ref, down_ref)):
+        rows = total[index * hidden : (index + 1) * hidden]
+        out_ref[...] = rows[:, :width].astype(jnp.bfloat16)
 
 
 def shards(tokens, cotangent, gates, route_ids, w_gate, w_up, w_down):
@@ -187,7 +242,7 @@
         select_kernel,
         out_shape=(
             pltpu.HBM((EXPERTS, pieces, CAP, feature_count), jnp.bfloat16),
-            jax.ShapeDtypeStruct((EXPERTS * CAP, token_count), jnp.bfloat16),
+            jax.ShapeDtypeStruct((rows, token_count), jnp.bfloat16),
         ),
         in_specs=[hbm] * 4,
         out_specs=(hbm, vmem),
@@ -212,10 +267,18 @@
     ring = pieces // 2
     after = [(i, i // ring * ring + (i + 1) % ring) for i in range(device_count)]
     before = [(i, i // ring * ring + (i - 1) % ring) for i in range(device_count)]
-    low = lax.ppermute(arrived[: device_count // 2], "expert", after)
-    high = lax.ppermute(arrived[device_count // 2 :], "expert", before)
-    odd = (lax.axis_index("expert") & 1).astype(jnp.int32).reshape(1)
-    core = (lax.axis_index("dp") & 1).astype(jnp.int32).reshape(1)
+    half_shape = jax.ShapeDtypeStruct((device_count // 2, CAP, feature_count), jnp.bfloat16)
+    low, high = pl.pallas_call(
+        halve_kernel,
+        out_shape=(half_shape, half_shape),
+        in_specs=[vmem],
+        out_specs=(vmem, vmem),
+        compiler_params=pltpu.CompilerParams(vmem_limit_bytes=12 * 2**20),
+    )(arrived)
+    low = lax.ppermute(low, "expert", after)
+    high = lax.ppermute(high, "expert", before)
+    piece_at = lax.axis_index("expert").astype(jnp.int32).reshape(1)
+    replica = lax.axis_index("dp").astype(jnp.int32).reshape(1)
     flat_lanes = feature_count + lanes // 2
     weight_shape = jax.ShapeDtypeStruct((hidden, feature_count), jnp.bfloat16)
     forward_shape = jax.ShapeDtypeStruct((2, hidden, rows), jnp.float32)
@@ -232,11 +295,11 @@
         in_specs=[smem, vmem, vmem, hbm, hbm],
         out_specs=(vmem,) * 5,
         scratch_shapes=[pltpu.SemaphoreType.DMA((2,))],
-        compiler_params=pltpu.CompilerParams(vmem_limit_bytes=32 * 2**20),
+        compiler_params=pltpu.CompilerParams(vmem_limit_bytes=12 * 2**20),
         cost_estimate=pl.CostEstimate(
             flops=4 * hidden * rows * feature_count, bytes_accessed=8 * 2**20, transcendentals=0
         ),
-    )(odd, arrived, w_gate, in_hbm(w_up), in_hbm(w_down))
+    )(piece_at, arrived, w_gate, in_hbm(w_up), in_hbm(w_down))
     grads_shape = jax.ShapeDtypeStruct((chips, 3 * hidden, lanes), jnp.bfloat16)
     other, pre, activation, flat = pl.pallas_call(
         functools.partial(passes_kernel, width),
@@ -252,8 +315,8 @@
             pltpu.VMEM((2, hidden, rows), jnp.float32),
             pltpu.VMEM((hidden, rows), jnp.float32),
         ],
-        compiler_params=pltpu.CompilerParams(vmem_limit_bytes=32 * 2**20),
-    )(core, odd, first, low, high, w_gate, up_here, down_here, forward, back)
+        compiler_params=pltpu.CompilerParams(vmem_limit_bytes=12 * 2**20),
+    )(replica, piece_at, first, low, high, w_gate, up_here, down_here, forward, back)
     swap = [(i, i ^ 1) for i in range(replicas)]
     theirs = lax.ppermute(other, "dp", swap)
     mine = pl.pallas_call(
@@ -261,41 +324,75 @@
         out_shape=grads_shape,
         in_specs=[smem] + [vmem] * 3,
         out_specs=vmem,
-        compiler_params=pltpu.CompilerParams(vmem_limit_bytes=32 * 2**20),
+        compiler_params=pltpu.CompilerParams(vmem_limit_bytes=12 * 2**20),
         cost_estimate=pl.CostEstimate(
             flops=6 * hidden * rows * feature_count, bytes_accessed=4 * 2**20, transcendentals=0
         ),
-    )(core, pre, activation, flat)
-    chip_sum = (mine.astype(jnp.float32) + theirs.astype(jnp.float32)).astype(jnp.bfloat16)
-    chip_sum, pre = lax.optimization_barrier((chip_sum, pre))
-    same_core = [[2 * x + c for x in range(chips)] for c in range(2)]
-    summed = lax.psum_scatter(
-        chip_sum.reshape(chips * 3 * hidden, lanes),
-        "dp",
-        scatter_dimension=0,
-        axis_index_groups=same_core,
-        tiled=True,
-    )
-    down_first = (((0,), (0,)), ((), ()))
-    partial = lax.dot_general(pre[:hidden], w_gate, down_first, preferred_element_type=jnp.float32)
-    partial = partial + lax.dot_general(
-        pre[hidden:], w_up, down_first, preferred_element_type=jnp.float32
-    )
-    piece_grad = partial.astype(jnp.bfloat16).reshape(device_count, CAP, feature_count)
+    )(replica, pre, activation, flat)
+    chunk_shape = jax.ShapeDtypeStruct((3 * hidden, lanes), jnp.bfloat16)
+    small = pltpu.CompilerParams(vmem_limit_bytes=12 * 2**20)
+    chunks = pl.pallas_call(
+        chip_kernel,
+        out_shape=(chunk_shape,) * chips,
+        in_specs=[smem, vmem, vmem],
+        out_specs=(vmem,) * chips,
+        compiler_params=small,
+    )(replica, mine, theirs)
+    add = pl.pallas_call(
+        add_kernel,
+        out_shape=chunk_shape,
+        in_specs=[vmem, vmem],
+        out_specs=vmem,
+        compiler_params=small,
+    )
+    far = chips // 2
+    chunks = list(chunks)
+    chunks[far], pre = lax.optimization_barrier((chunks[far], pre))
+    piece_grad = pl.pallas_call(
+        piece_kernel,
+        out_shape=pltpu.HBM((device_count, CAP, feature_count), jnp.bfloat16),
+        in_specs=[vmem] * 3,
+        out_specs=hbm,
+        scratch_shapes=[
+            pltpu.VMEM((device_count, CAP, feature_count), jnp.bfloat16),
+            pltpu.SemaphoreType.DMA(()),
+        ],
+        compiler_params=pltpu.CompilerParams(vmem_limit_bytes=12 * 2**20),
+        cost_estimate=pl.CostEstimate(
+            flops=4 * hidden * rows * feature_count, bytes_accessed=4 * 2**20, transcendentals=0
+        ),
+    )(pre, w_gate, up_here)
+    ahead = [(i, (i + 2) % replicas) for i in range(replicas)]
+    back = [(i, (i - 2) % replicas) for i in range(replicas)]
+    rising = lax.ppermute(chunks[far], "dp", ahead)
+    falling = lax.ppermute(chunks[chips - far + 1], "dp", back)
+    for distance in range(far - 1, 0, -1):
+        rising = lax.ppermute(add(rising, chunks[distance]), "dp", ahead)
+        if distance > 1:
+            falling = lax.ppermute(add(falling, chunks[chips - distance + 1]), "dp", back)
     returned = lax.all_to_all(piece_grad, "expert", split_axis=0, concat_axis=0, tiled=True)
-    returned_rows = returned.reshape(device_count * CAP, feature_count)
-    pair_table = jnp.broadcast_to(
-        table.reshape(EXPERTS, 1, CAP, token_count), (EXPERTS, pieces, CAP, token_count)
-    ).reshape(device_count * CAP, token_count)
-    grad_tokens = jnp.dot(pair_table.T, returned_rows, preferred_element_type=jnp.float32).astype(
-        jnp.bfloat16
-    )
-    return (
-        grad_tokens,
-        summed[:hidden, :width],
-        summed[hidden : 2 * hidden, :width],
-        summed[2 * hidden :, :width],
-    )
+    grad_tokens = pl.pallas_call(
+        combine_kernel,
+        out_shape=jax.ShapeDtypeStruct((token_count, feature_count), jnp.bfloat16),
+        in_specs=[vmem, vmem],
+        out_specs=vmem,
+        compiler_params=small,
+        cost_estimate=pl.CostEstimate(
+            flops=2 * rows * token_count * feature_count,
+            bytes_accessed=2 * 2**20,
+            transcendentals=0,
+        ),
+    )(table, returned)
+    rising, grad_tokens = lax.optimization_barrier((rising, grad_tokens))
+    owned = jax.ShapeDtypeStruct((hidden, width), jnp.bfloat16)
+    grads = pl.pallas_call(
+        total_kernel,
+        out_shape=(owned,) * 3,
+        in_specs=[vmem] * 3,
+        out_specs=(vmem,) * 3,
+        compiler_params=small,
+    )(rising, falling, chunks[0])
+    return (grad_tokens, *grads)
 
 
 def solution(mesh):

time: 138 us -> 133 us (0.964)
  starting transfers between devices: 9 us -> 44.8 us
  blocking collectives: 86.2 us -> 50.6 us
  waiting for transfers between devices: 9.64 us -> 23.6 us
  between operations: 14.1 us -> 0.82 us
  local copies, waits for them, and re-layouts: 6.56 us -> 0.01 us
  Pallas kernels: 6.85 us -> 12.1 us
  matrix products: 3.15 us -> 0 us
  other arithmetic: 1.86 us -> 0 us
    all_to_all x1 -> x0, blocking collectives: 35.6 us -> none  [shards(): lax.all_to_all(piece_grad, 'expert', split_axis=0, concat_axis=0, tiled=T...]
    ppermute x2 -> x9, starting transfers between devices: 7.04 us -> 34.2 us  [the longest x3 16.8 us: shards(): rising = lax.ppermute(add(rising, chunks[distance]), 'dp', ahead)]
    ppermute x2 -> x9, waiting for transfers between devices: 5.93 us -> 20.5 us  [the longest x2 5.7 us: shards(): lax.ppermute(add(falling, chunks[chips - distance + 1]), 'dp', back)]
    all_to_all x0 -> x1, starting transfers between devices: none -> 8.71 us  [shards(): lax.all_to_all(piece_grad, 'expert', split_axis=0, concat_axis=0, tiled=T...]
    pallas_call x0 -> x10, Pallas kernels: none -> 5.22 us  [the longest x1 1.6 us: shards(): pl.pallas_call(piece_kernel, out_shape=pltpu.HBM((device_count, CAP, feat...]
    dot_general x3 -> x0, matrix products: 3.15 us -> none  [the longest x1 1.36 us: shards(): lax.dot_general(pre[hidden:], w_up, down_first, preferred_element_type=jn...]
    slice x2 -> x0, local copies, waits for them, and re-layouts: 3.05 us -> none  [the longest x1 1.65 us: shards(): summed[2 * hidden:, :width]]
    reshape x2 -> x0, local copies, waits for them, and re-layouts: 2.69 us -> none  [the longest x1 2.34 us: shards(): partial.astype(jnp.bfloat16).reshape(device_count, CAP, feature_count)]
  transfers between devices with their start and end apart: 4 -> 11, of which waited for: 4 -> 8; matrix products, arithmetic and copies ran while one was open for 4% -> 0% of each run, Pallas kernels for 2% -> 3%
where the time goes in v3:
time: 133 us; the launch traced here: 132 us
  blocking collectives  50.6 us (38%)
  starting transfers between devices  44.8 us (34%)
  waiting for transfers between devices  23.6 us (18%)
  Pallas kernels  12.1 us (9%)
    all_to_all x1, blocking collectives, shards(): lax.all_to_all(send.reshape(device_count, CAP, feature_count), 'expert',...  50.6 us
    ppermute x3, starting transfers between devices, shards(): rising = lax.ppermute(add(rising, chunks[distance]), 'dp', ahead)  16.8 us
    all_to_all x1, starting transfers between devices, shards(): lax.all_to_all(piece_grad, 'expert', split_axis=0, concat_axis=0, tiled=T...  8.71 us
    ppermute x2, waiting for transfers between devices, shards(): lax.ppermute(add(falling, chunks[chips - distance + 1]), 'dp', back)  5.7 us
    ppermute x1, waiting for transfers between devices, shards(): rising = lax.ppermute(chunks[far], 'dp', ahead)  4.95 us
    ppermute x1, starting transfers between devices, shards(): rising = lax.ppermute(chunks[far], 'dp', ahead)  4.61 us
    ppermute x1, waiting for transfers between devices, shards(): low = lax.ppermute(low, 'expert', after)  4.15 us
    ppermute x1, starting transfers between devices, shards(): high = lax.ppermute(high, 'expert', before)  4.01 us
  transfers between devices with their start and end apart: 11, of which 8 were waited for; matrix products, arithmetic and copies ran while one was open for 0% of the time, Pallas kernels for 3%

profile of v3, /device:TPU:6, one launch (start us, length us, event | category | flops | bytes accessed | tf_op | source)
XLA Modules:
  0.0 131.9 jit_solution(4422583292831590796)
XLA Ops:
  0.6 2.7 %shard_map.102 = (bf16[4,16,2,3584]{3,2,1,0:T(2,128)(2,1)}, bf16[128,128]{1,0:T(8,128)(2,1)S(1)}) custom-call(s32[2,128]{1,0:T(2,128)} %bitcast.6, bf16[2,128]{1,0:T(2,128)(2,1)} %bitcast.7, bf16[128,3584]{1,0:T(8,128)(2,1)} %tokens_hbm.1, bf16[128,3584]{1,0:T(8,128)(2,1)} %cotan_hbm.1), custom_call_target="tpu_custom_call" | custom-call | tf_op jit(solution)/shard_map/pallas_call | solution.py:241
  3.3 0.0 copy-start
  3.3 50.6 %all_to_all.10.rows_ref = bf16[64,2,3584]{2,1,0:T(2,128)(2,1)S(1)} all-to-all(bf16[64,2,3584]{2,1,0:T(2,128)(2,1)} %bitcast.5), channel_id=1, replica_groups=mesh['expert'=64,'dp'=16] {'expert'}, dimensions={0} | all-to-all | bytes 1835008 | tf_op jit(solution)/shard_map/all_to_all | solution.py:260
  53.9 0.8 shard_map.104
  54.7 3.0 %collective-permute-start = (bf16[32,2,3584]{2,1,0:T(2,128)(2,1)}, bf16[32,2,3584]{2,1,0:T(2,128)(2,1)S(1)}, u32[]{:S(2)}, u32[]{:S(2)}) collective-permute-start(bf16[32,2,3584]{2,1,0:T(2,128)(2,1)} %get-tuple-element.34), channel_id=1, source_target_pairs={{0,16},{16,32},{32,48},{48,64},{64,80},{80,96},{96,112},{112,0},{1... | collective-permute-start | bytes 1376264 | tf_op jit(solution)/shard_map/ppermute | solution.py:278
  57.7 4.0 %collective-permute-start.1 = (bf16[32,2,3584]{2,1,0:T(2,128)(2,1)S(1)}, bf16[32,2,3584]{2,1,0:T(2,128)(2,1)S(1)}, u32[]{:S(2)}, u32[]{:S(2)}) collective-permute-start(bf16[32,2,3584]{2,1,0:T(2,128)(2,1)S(1)} %get-tuple-element.35), channel_id=1, source_target_pairs={{0,112},{16,0},{32,16},{48,32},{64,48},{80,64},{96,80},{112,96},{1... | collective-permute-start | bytes 1376264 | tf_op jit(solution)/shard_map/ppermute | solution.py:279
  61.8 0.0 copy-done
  61.8 2.0 %shard_map.103 = (bf16[128,3712]{1,0:T(8,128)(2,1)S(1)}, bf16[152,3584]{1,0:T(8,128)(2,1)S(1)}, bf16[152,3584]{1,0:T(8,128)(2,1)S(1)}, f32[2,152,128]{2,1,0:T(8,128)S(1)}, f32[152,128]{1,0:T(8,128)S(1)}) custom-call(s32[1]{0:T(128)} %bitcast.1.piece_at_ref, bf16[64,2,3584]{2,1,0:T(2,128)(2,1)S(1)} %all_to_all.10.rows_ref, bf16[152,3584]{1,0:T(8,128)(2,1)S(1)} %copy-done, ...), custom_call_target="tpu_custom_call" | custom-call | flops 278921216 | bytes 8388608 | tf_op jit(solution)/shard_map/pallas_call | solution.py:286
  63.8 4.1 %collective-permute-done.low_ref = bf16[32,2,3584]{2,1,0:T(2,128)(2,1)S(1)} collective-permute-done((bf16[32,2,3584]{2,1,0:T(2,128)(2,1)}, bf16[32,2,3584]{2,1,0:T(2,128)(2,1)S(1)}, u32[]{:S(2)}, u32[]{:S(2)}) %collective-permute-start) | collective-permute-done | bytes 458784 | tf_op jit(solution)/shard_map/ppermute | solution.py:278
  68.0 1.8 %collective-permute-done.1.high_ref = bf16[32,2,3584]{2,1,0:T(2,128)(2,1)S(1)} collective-permute-done((bf16[32,2,3584]{2,1,0:T(2,128)(2,1)S(1)}, bf16[32,2,3584]{2,1,0:T(2,128)(2,1)S(1)}, u32[]{:S(2)}, u32[]{:S(2)}) %collective-permute-start.1) | collective-permute-done | bytes 458784 | tf_op jit(solution)/shard_map/ppermute | solution.py:279
  69.8 1.5 %shard_map.105 = (bf16[8,456,256]{2,1,0:T(8,128)(2,1)S(1)}, bf16[304,128]{1,0:T(8,128)(2,1)S(1)}, bf16[152,128]{1,0:T(8,128)(2,1)S(1)}, bf16[2,128,3712]{2,1,0:T(8,128)(2,1)S(1)}) custom-call(s32[1]{0:T(128)} %bitcast.replica_ref, s32[1]{0:T(128)} %bitcast.1.piece_at_ref, bf16[128,3712]{1,0:T(8,128)(2,1)S(1)} %get-tuple-element.33.first_ref, ...), custom_call_target="tpu_custom_call" | custom-call | tf_op jit(solution)/shard_map/pallas_call | solution.py:304
  71.2 1.9 %collective-permute-start.2 = (bf16[8,456,256]{2,1,0:T(8,128)(2,1)S(1)}, bf16[8,456,256]{2,1,0:T(8,128)(2,1)S(1)}, u32[]{:S(2)}, u32[]{:S(2)}) collective-permute-start(bf16[8,456,256]{2,1,0:T(8,128)(2,1)S(1)} %get-tuple-element.43), channel_id=1, source_target_pairs={{0,1},{1,0},{2,3},{3,2},{4,5},{5,4},{6,7},{7,6},{8,9},{9,8},{10,11... | collective-permute-start | bytes 5603336 | tf_op jit(solution)/shard_map/ppermute | solution.py:321
  73.2 0.7 shard_map.106.mine_ref
  73.9 3.1 %collective-permute-done.2.theirs_ref = bf16[8,456,256]{2,1,0:T(8,128)(2,1)S(1)} collective-permute-done((bf16[8,456,256]{2,1,0:T(8,128)(2,1)S(1)}, bf16[8,456,256]{2,1,0:T(8,128)(2,1)S(1)}, u32[]{:S(2)}, u32[]{:S(2)}) %collective-permute-start.2) | collective-permute-done | bytes 1867808 | tf_op jit(solution)/shard_map/ppermute | solution.py:321
  77.0 0.4 shard_map.107
  77.4 1.6 %shard_map.111 = bf16[64,2,3584]{2,1,0:T(2,128)(2,1)} custom-call(bf16[304,128]{1,0:T(8,128)(2,1)S(1)} %get-tuple-element.50.pre_ref, bf16[152,3584]{1,0:T(8,128)(2,1)S(1)} %copy-done, bf16[152,3584]{1,0:T(8,128)(2,1)S(1)} %get-tuple-element.36.up_ref), custom_call_target="tpu_custom_call" | custom-call | flops 278921216 | bytes 4194304 | tf_op jit(solution)/shard_map/pallas_call | solution.py:351
  79.0 8.7 %all-to-all-start.1 = ((bf16[64,2,3584]{2,1,0:T(2,128)(2,1)}), bf16[64,2,3584]{2,1,0:T(2,128)(2,1)S(1)}, u32[]{:S(2)}, u32[]{:S(2)}) async-start(bf16[64,2,3584]{2,1,0:T(2,128)(2,1)} %shard_map.111), calls=%async_computation.1 | async-start | bytes 1835008 | tf_op jit(solution)/shard_map/all_to_all | solution.py:373
  87.7 4.6 %collective-permute-start.3 = (bf16[456,256]{1,0:T(8,128)(2,1)S(1)}, bf16[456,256]{1,0:T(8,128)(2,1)S(1)}, u32[]{:S(2)}, u32[]{:S(2)}) collective-permute-start(bf16[456,256]{1,0:T(8,128)(2,1)S(1)} %get-tuple-element.45), channel_id=1, source_target_pairs={{0,2},{1,3},{2,4},{3,5},{4,6},{5,7},{6,8},{7,9},{8,10},{9,11},{10,... | collective-permute-start | bytes 700424 | tf_op jit(solution)/shard_map/ppermute | solution.py:367
  92.3 4.9 %collective-permute-done.3.got_ref = bf16[456,256]{1,0:T(8,128)(2,1)S(1)} collective-permute-done((bf16[456,256]{1,0:T(8,128)(2,1)S(1)}, bf16[456,256]{1,0:T(8,128)(2,1)S(1)}, u32[]{:S(2)}, u32[]{:S(2)}) %collective-permute-start.3) | collective-permute-done | bytes 233504 | tf_op jit(solution)/shard_map/ppermute | solution.py:367
  97.3 0.1 shard_map.108
  97.3 5.6 %collective-permute-start.4 = (bf16[456,256]{1,0:T(8,128)(2,1)S(1)}, bf16[456,256]{1,0:T(8,128)(2,1)S(1)}, u32[]{:S(2)}, u32[]{:S(2)}) collective-permute-start(bf16[456,256]{1,0:T(8,128)(2,1)S(1)} %shard_map.108), channel_id=1, source_target_pairs={{0,2},{1,3},{2,4},{3,5},{4,6},{5,7},{6,8},{7,9},{8,10},{9,11},{10,... | collective-permute-start | bytes 700424 | tf_op jit(solution)/shard_map/ppermute | solution.py:370
  102.9 1.9 %collective-permute-start.7 = (bf16[456,256]{1,0:T(8,128)(2,1)S(1)}, bf16[456,256]{1,0:T(8,128)(2,1)S(1)}, u32[]{:S(2)}, u32[]{:S(2)}) collective-permute-start(bf16[456,256]{1,0:T(8,128)(2,1)S(1)} %get-tuple-element.53), channel_id=1, source_target_pairs={{0,14},{1,15},{2,0},{3,1},{4,2},{5,3},{6,4},{7,5},{8,6},{9,7},{10,... | collective-permute-start | bytes 700424 | tf_op jit(solution)/shard_map/ppermute | solution.py:368
  104.9 2.1 %collective-permute-done.4.got_ref = bf16[456,256]{1,0:T(8,128)(2,1)S(1)} collective-permute-done((bf16[456,256]{1,0:T(8,128)(2,1)S(1)}, bf16[456,256]{1,0:T(8,128)(2,1)S(1)}, u32[]{:S(2)}, u32[]{:S(2)}) %collective-permute-start.4) | collective-permute-done | bytes 233504 | tf_op jit(solution)/shard_map/ppermute | solution.py:370
  107.0 0.1 shard_map.109
  107.1 5.6 %collective-permute-start.5 = (bf16[456,256]{1,0:T(8,128)(2,1)S(1)}, bf16[456,256]{1,0:T(8,128)(2,1)S(1)}, u32[]{:S(2)}, u32[]{:S(2)}) collective-permute-start(bf16[456,256]{1,0:T(8,128)(2,1)S(1)} %shard_map.109), channel_id=1, source_target_pairs={{0,2},{1,3},{2,4},{3,5},{4,6},{5,7},{6,8},{7,9},{8,10},{9,11},{10,... | collective-permute-start | bytes 700424 | tf_op jit(solution)/shard_map/ppermute | solution.py:370
  112.7 0.0 collective-permute-done.7.got_ref
  112.7 0.1 shard_map.113
  112.8 1.9 %collective-permute-start.8 = (bf16[456,256]{1,0:T(8,128)(2,1)S(1)}, bf16[456,256]{1,0:T(8,128)(2,1)S(1)}, u32[]{:S(2)}, u32[]{:S(2)}) collective-permute-start(bf16[456,256]{1,0:T(8,128)(2,1)S(1)} %shard_map.113), channel_id=1, source_target_pairs={{0,14},{1,15},{2,0},{3,1},{4,2},{5,3},{6,4},{7,5},{8,6},{9,7},{10,... | collective-permute-start | bytes 700424 | tf_op jit(solution)/shard_map/ppermute | solution.py:372
  114.7 1.6 %collective-permute-done.5.got_ref = bf16[456,256]{1,0:T(8,128)(2,1)S(1)} collective-permute-done((bf16[456,256]{1,0:T(8,128)(2,1)S(1)}, bf16[456,256]{1,0:T(8,128)(2,1)S(1)}, u32[]{:S(2)}, u32[]{:S(2)}) %collective-permute-start.5) | collective-permute-done | bytes 233504 | tf_op jit(solution)/shard_map/ppermute | solution.py:370
  116.2 0.1 shard_map.110
  116.3 5.6 %collective-permute-start.6 = (bf16[456,256]{1,0:T(8,128)(2,1)S(1)}, bf16[456,256]{1,0:T(8,128)(2,1)S(1)}, u32[]{:S(2)}, u32[]{:S(2)}) collective-permute-start(bf16[456,256]{1,0:T(8,128)(2,1)S(1)} %shard_map.110), channel_id=1, source_target_pairs={{0,2},{1,3},{2,4},{3,5},{4,6},{5,7},{6,8},{7,9},{8,10},{9,11},{10,... | collective-permute-start | bytes 700424 | tf_op jit(solution)/shard_map/ppermute | solution.py:370
  121.9 0.0 collective-permute-done.8.got_ref
  121.9 0.1 shard_map.114
  122.0 1.9 %collective-permute-start.9 = (bf16[456,256]{1,0:T(8,128)(2,1)S(1)}, bf16[456,256]{1,0:T(8,128)(2,1)S(1)}, u32[]{:S(2)}, u32[]{:S(2)}) collective-permute-start(bf16[456,256]{1,0:T(8,128)(2,1)S(1)} %shard_map.114), channel_id=1, source_target_pairs={{0,14},{1,15},{2,0},{3,1},{4,2},{5,3},{6,4},{7,5},{8,6},{9,7},{10,... | collective-permute-start | bytes 700424 | tf_op jit(solution)/shard_map/ppermute | solution.py:372
  123.9 0.0 all-to-all-done.1.rows_ref
  123.9 1.4 %shard_map.112 = bf16[128,3584]{1,0:T(8,128)(2,1)} custom-call(bf16[128,128]{1,0:T(8,128)(2,1)S(1)} %get-tuple-element.49.table_ref, bf16[64,2,3584]{2,1,0:T(2,128)(2,1)S(1)} %all-to-all-done.1.rows_ref), custom_call_target="tpu_custom_call" | custom-call | flops 117440512 | bytes 2097152 | tf_op jit(solution)/shard_map/pallas_call | solution.py:374
  125.3 0.2 collective-permute-done.6.up_ring_ref
  125.5 5.7 %collective-permute-done.9.down_ring_ref = bf16[456,256]{1,0:T(8,128)(2,1)S(1)} collective-permute-done((bf16[456,256]{1,0:T(8,128)(2,1)S(1)}, bf16[456,256]{1,0:T(8,128)(2,1)S(1)}, u32[]{:S(2)}, u32[]{:S(2)}) %collective-permute-start.9) | collective-permute-done | bytes 233504 | tf_op jit(solution)/shard_map/ppermute | solution.py:372
  131.2 0.7 shard_map.115
Async XLA Ops:
  3.3 58.5 %copy-start = (bf16[152,3584]{1,0:T(8,128)(2,1)S(1)}, bf16[152,3584]{1,0:T(8,128)(2,1)}, u32[]{:S(2)}) copy-start(bf16[152,3584]{1,0:T(8,128)(2,1)} %gate_ref.5) | copy-start | bytes 3268612
  54.7 13.3 %collective-permute-start = (bf16[32,2,3584]{2,1,0:T(2,128)(2,1)}, bf16[32,2,3584]{2,1,0:T(2,128)(2,1)S(1)}, u32[]{:S(2)}, u32[]{:S(2)}) collective-permute-start(bf16[32,2,3584]{2,1,0:T(2,128)(2,1)} %get-tuple-element.34), channel_id=1, source_target_pairs={{0,16},{16,32},{32,48},{48,64},{64,80},{80,96},{96,112},{112,0},{1... | collective-permute-start | bytes 1376264 | tf_op jit(solution)/shard_map/ppermute | solution.py:278
  57.7 12.0 %collective-permute-start.1 = (bf16[32,2,3584]{2,1,0:T(2,128)(2,1)S(1)}, bf16[32,2,3584]{2,1,0:T(2,128)(2,1)S(1)}, u32[]{:S(2)}, u32[]{:S(2)}) collective-permute-start(bf16[32,2,3584]{2,1,0:T(2,128)(2,1)S(1)} %get-tuple-element.35), channel_id=1, source_target_pairs={{0,112},{16,0},{32,16},{48,32},{64,48},{80,64},{96,80},{112,96},{1... | collective-permute-start | bytes 1376264 | tf_op jit(solution)/shard_map/ppermute | solution.py:279
  71.2 5.7 %collective-permute-start.2 = (bf16[8,456,256]{2,1,0:T(8,128)(2,1)S(1)}, bf16[8,456,256]{2,1,0:T(8,128)(2,1)S(1)}, u32[]{:S(2)}, u32[]{:S(2)}) collective-permute-start(bf16[8,456,256]{2,1,0:T(8,128)(2,1)S(1)} %get-tuple-element.43), channel_id=1, source_target_pairs={{0,1},{1,0},{2,3},{3,2},{4,5},{5,4},{6,7},{7,6},{8,9},{9,8},{10,11... | collective-permute-start | bytes 5603336 | tf_op jit(solution)/shard_map/ppermute | solution.py:321
  79.0 44.9 %all-to-all-start.1 = ((bf16[64,2,3584]{2,1,0:T(2,128)(2,1)}), bf16[64,2,3584]{2,1,0:T(2,128)(2,1)S(1)}, u32[]{:S(2)}, u32[]{:S(2)}) async-start(bf16[64,2,3584]{2,1,0:T(2,128)(2,1)} %shard_map.111), calls=%async_computation.1 | async-start | bytes 1835008 | tf_op jit(solution)/shard_map/all_to_all | solution.py:373
  87.7 9.6 %collective-permute-start.3 = (bf16[456,256]{1,0:T(8,128)(2,1)S(1)}, bf16[456,256]{1,0:T(8,128)(2,1)S(1)}, u32[]{:S(2)}, u32[]{:S(2)}) collective-permute-start(bf16[456,256]{1,0:T(8,128)(2,1)S(1)} %get-tuple-element.45), channel_id=1, source_target_pairs={{0,2},{1,3},{2,4},{3,5},{4,6},{5,7},{6,8},{7,9},{8,10},{9,11},{10,... | collective-permute-start | bytes 700424 | tf_op jit(solution)/shard_map/ppermute | solution.py:367
  97.3 9.7 %collective-permute-start.4 = (bf16[456,256]{1,0:T(8,128)(2,1)S(1)}, bf16[456,256]{1,0:T(8,128)(2,1)S(1)}, u32[]{:S(2)}, u32[]{:S(2)}) collective-permute-start(bf16[456,256]{1,0:T(8,128)(2,1)S(1)} %shard_map.108), channel_id=1, source_target_pairs={{0,2},{1,3},{2,4},{3,5},{4,6},{5,7},{6,8},{7,9},{8,10},{9,11},{10,... | collective-permute-start | bytes 700424 | tf_op jit(solution)/shard_map/ppermute | solution.py:370
  102.9 9.7 %collective-permute-start.7 = (bf16[456,256]{1,0:T(8,128)(2,1)S(1)}, bf16[456,256]{1,0:T(8,128)(2,1)S(1)}, u32[]{:S(2)}, u32[]{:S(2)}) collective-permute-start(bf16[456,256]{1,0:T(8,128)(2,1)S(1)} %get-tuple-element.53), channel_id=1, source_target_pairs={{0,14},{1,15},{2,0},{3,1},{4,2},{5,3},{6,4},{7,5},{8,6},{9,7},{10,... | collective-permute-start | bytes 700424 | tf_op jit(solution)/shard_map/ppermute | solution.py:368
  107.1 9.2 %collective-permute-start.5 = (bf16[456,256]{1,0:T(8,128)(2,1)S(1)}, bf16[456,256]{1,0:T(8,128)(2,1)S(1)}, u32[]{:S(2)}, u32[]{:S(2)}) collective-permute-start(bf16[456,256]{1,0:T(8,128)(2,1)S(1)} %shard_map.109), channel_id=1, source_target_pairs={{0,2},{1,3},{2,4},{3,5},{4,6},{5,7},{6,8},{7,9},{8,10},{9,11},{10,... | collective-permute-start | bytes 700424 | tf_op jit(solution)/shard_map/ppermute | solution.py:370
  112.8 9.2 %collective-permute-start.8 = (bf16[456,256]{1,0:T(8,128)(2,1)S(1)}, bf16[456,256]{1,0:T(8,128)(2,1)S(1)}, u32[]{:S(2)}, u32[]{:S(2)}) collective-permute-start(bf16[456,256]{1,0:T(8,128)(2,1)S(1)} %shard_map.113), channel_id=1, source_target_pairs={{0,14},{1,15},{2,0},{3,1},{4,2},{5,3},{6,4},{7,5},{8,6},{9,7},{10,... | collective-permute-start | bytes 700424 | tf_op jit(solution)/shard_map/ppermute | solution.py:372
  116.3 9.2 %collective-permute-start.6 = (bf16[456,256]{1,0:T(8,128)(2,1)S(1)}, bf16[456,256]{1,0:T(8,128)(2,1)S(1)}, u32[]{:S(2)}, u32[]{:S(2)}) collective-permute-start(bf16[456,256]{1,0:T(8,128)(2,1)S(1)} %shard_map.110), channel_id=1, source_target_pairs={{0,2},{1,3},{2,4},{3,5},{4,6},{5,7},{6,8},{7,9},{8,10},{9,11},{10,... | collective-permute-start | bytes 700424 | tf_op jit(solution)/shard_map/ppermute | solution.py:370
  122.0 9.2 %collective-permute-start.9 = (bf16[456,256]{1,0:T(8,128)(2,1)S(1)}, bf16[456,256]{1,0:T(8,128)(2,1)S(1)}, u32[]{:S(2)}, u32[]{:S(2)}) collective-permute-start(bf16[456,256]{1,0:T(8,128)(2,1)S(1)} %shard_map.114), channel_id=1, source_target_pairs={{0,14},{1,15},{2,0},{3,1},{4,2},{5,3},{6,4},{7,5},{8,6},{9,7},{10,... | collective-permute-start | bytes 700424 | tf_op jit(solution)/shard_map/ppermute | solution.py:372

commit v4 on v3

--- a/solution.py
+++ b/solution.py
@@ -86,10 +86,8 @@
         out_ref[chunk] = part.astype(jnp.bfloat16)
 
 
-def halve_kernel(rows_ref, low_ref, high_ref):
-    half = low_ref.shape[0]
-    low_ref[...] = rows_ref[:half]
-    high_ref[...] = rows_ref[half:]
+def part_kernel(start, rows_ref, part_ref):
+    part_ref[...] = rows_ref[start : start + part_ref.shape[0]]
 
 
 def flatten(rows_ref, lanes):
@@ -137,7 +135,7 @@
     width, replica_ref, piece_at_ref, first_ref, low_ref, high_ref, gate_ref, up_ref, down_ref, done_forward_ref,
     done_back_ref, other_ref, pre_ref, act_ref, flat_ref, forward_ref, back_ref,
 ):
-    half = flat_ref.shape[1] // 2
+    half = CAP * low_ref.shape[0]
     odd = piece_at_ref[0] & 1
     flat_ref[odd] = first_ref[...]
     flat_ref[1 - odd, :half] = flatten(low_ref, flat_ref.shape[2])
@@ -267,14 +265,18 @@
     ring = pieces // 2
     after = [(i, i // ring * ring + (i + 1) % ring) for i in range(device_count)]
     before = [(i, i // ring * ring + (i - 1) % ring) for i in range(device_count)]
-    half_shape = jax.ShapeDtypeStruct((device_count // 2, CAP, feature_count), jnp.bfloat16)
-    low, high = pl.pallas_call(
-        halve_kernel,
-        out_shape=(half_shape, half_shape),
-        in_specs=[vmem],
-        out_specs=(vmem, vmem),
-        compiler_params=pltpu.CompilerParams(vmem_limit_bytes=12 * 2**20),
-    )(arrived)
+    split = device_count * 5 // 8
+
+    def part(start, size):
+        return pl.pallas_call(
+            functools.partial(part_kernel, start),
+            out_shape=jax.ShapeDtypeStruct((size, CAP, feature_count), jnp.bfloat16),
+            in_specs=[vmem],
+            out_specs=vmem,
+            compiler_params=pltpu.CompilerParams(vmem_limit_bytes=12 * 2**20),
+        )(arrived)
+
+    low, high = part(0, split), part(split, device_count - split)
     low = lax.ppermute(low, "expert", after)
     high = lax.ppermute(high, "expert", before)
     piece_at = lax.axis_index("expert").astype(jnp.int32).reshape(1)
@@ -347,7 +349,6 @@
     )
     far = chips // 2
     chunks = list(chunks)
-    chunks[far], pre = lax.optimization_barrier((chunks[far], pre))
     piece_grad = pl.pallas_call(
         piece_kernel,
         out_shape=pltpu.HBM((device_count, CAP, feature_count), jnp.bfloat16),
@@ -362,6 +363,7 @@
             flops=4 * hidden * rows * feature_count, bytes_accessed=4 * 2**20, transcendentals=0
         ),
     )(pre, w_gate, up_here)
+    chunks[far], piece_grad = lax.optimization_barrier((chunks[far], piece_grad))
     ahead = [(i, (i + 2) % replicas) for i in range(replicas)]
     back = [(i, (i - 2) % replicas) for i in range(replicas)]
     rising = lax.ppermute(chunks[far], "dp", ahead)
@@ -383,7 +385,7 @@
             transcendentals=0,
         ),
     )(table, returned)
-    rising, grad_tokens = lax.optimization_barrier((rising, grad_tokens))
+    falling, grad_tokens = lax.optimization_barrier((falling, grad_tokens))
     owned = jax.ShapeDtypeStruct((hidden, width), jnp.bfloat16)
     grads = pl.pallas_call(
         total_kernel,

time: 133 us -> 126 us (0.947)
  the two profiles are of different devices: /device:TPU:6 before, /device:TPU:8 now
where the time goes in v4:
time: 126 us; the launch traced here: 125 us
  blocking collectives  50.4 us (40%)
  starting transfers between devices  39.6 us (31%)
  waiting for transfers between devices  21.8 us (17%)
  Pallas kernels  12.3 us (10%)
    all_to_all x1, blocking collectives, shards(): lax.all_to_all(send.reshape(device_count, CAP, feature_count), 'expert',...  50.4 us
    ppermute x3, waiting for transfers between devices, shards(): rising = lax.ppermute(add(rising, chunks[distance]), 'dp', ahead)  10.4 us
    ppermute x2, starting transfers between devices, shards(): lax.ppermute(add(falling, chunks[chips - distance + 1]), 'dp', back)  10.3 us
    all_to_all x1, starting transfers between devices, shards(): lax.all_to_all(piece_grad, 'expert', split_axis=0, concat_axis=0, tiled=T...  7.46 us
    ppermute x3, starting transfers between devices, shards(): rising = lax.ppermute(add(rising, chunks[distance]), 'dp', ahead)  5.76 us
    ppermute x1, starting transfers between devices, shards(): falling = lax.ppermute(chunks[chips - far + 1], 'dp', back)  4.56 us
    ppermute x1, starting transfers between devices, shards(): high = lax.ppermute(high, 'expert', before)  4.01 us
    ppermute x1, waiting for transfers between devices, shards(): high = lax.ppermute(high, 'expert', before)  3.58 us
  transfers between devices with their start and end apart: 11, of which 7 were waited for; matrix products, arithmetic and copies ran while one was open for 0% of the time, Pallas kernels for 5%

profile of v4, /device:TPU:8, one launch (start us, length us, event | category | flops | bytes accessed | tf_op | source)
XLA Modules:
  0.0 125.0 jit_solution(2364462944972643512)
XLA Ops:
  0.6 2.7 %shard_map.102 = (bf16[4,16,2,3584]{3,2,1,0:T(2,128)(2,1)}, bf16[128,128]{1,0:T(8,128)(2,1)S(1)}) custom-call(s32[2,128]{1,0:T(2,128)} %bitcast.6, bf16[2,128]{1,0:T(2,128)(2,1)} %bitcast.7, bf16[128,3584]{1,0:T(8,128)(2,1)} %tokens_hbm.1, bf16[128,3584]{1,0:T(8,128)(2,1)} %cotan_hbm.1), custom_call_target="tpu_custom_call" | custom-call | tf_op jit(solution)/shard_map/pallas_call | solution.py:239
  3.3 50.4 %all_to_all.10.rows_ref = bf16[64,2,3584]{2,1,0:T(2,128)(2,1)S(1)} all-to-all(bf16[64,2,3584]{2,1,0:T(2,128)(2,1)} %bitcast.5), channel_id=1, replica_groups=mesh['expert'=64,'dp'=16] {'expert'}, dimensions={0} | all-to-all | bytes 1835008 | tf_op jit(solution)/shard_map/all_to_all | solution.py:258
  53.7 0.0 copy-start
  53.8 3.2 %collective-permute-start = (bf16[40,2,3584]{2,1,0:T(2,128)(2,1)S(1)}, bf16[40,2,3584]{2,1,0:T(2,128)(2,1)S(1)}, u32[]{:S(2)}, u32[]{:S(2)}) collective-permute-start(bf16[40,2,3584]{2,1,0:T(2,128)(2,1)S(1)} %shard_map.104), channel_id=1, source_target_pairs={{0,16},{16,32},{32,48},{48,64},{64,80},{80,96},{96,112},{112,0},{1... | collective-permute-start | bytes 1720328 | tf_op jit(solution)/shard_map/ppermute | solution.py:280
  57.0 4.0 %collective-permute-start.1 = (bf16[24,2,3584]{2,1,0:T(2,128)(2,1)S(1)}, bf16[24,2,3584]{2,1,0:T(2,128)(2,1)}, u32[]{:S(2)}, u32[]{:S(2)}) collective-permute-start(bf16[24,2,3584]{2,1,0:T(2,128)(2,1)S(1)} %shard_map.105), channel_id=1, source_target_pairs={{0,112},{16,0},{32,16},{48,32},{64,48},{80,64},{96,80},{112,96},{1... | collective-permute-start | bytes 1032200 | tf_op jit(solution)/shard_map/ppermute | solution.py:281
  61.0 0.0 copy-done
  61.0 2.0 %shard_map.103 = (bf16[128,3712]{1,0:T(8,128)(2,1)S(1)}, bf16[152,3584]{1,0:T(8,128)(2,1)S(1)}, bf16[152,3584]{1,0:T(8,128)(2,1)S(1)}, f32[2,152,128]{2,1,0:T(8,128)S(1)}, f32[152,128]{1,0:T(8,128)S(1)}) custom-call(s32[1]{0:T(128)} %bitcast.1.piece_at_ref, bf16[64,2,3584]{2,1,0:T(2,128)(2,1)S(1)} %all_to_all.10.rows_ref, bf16[152,3584]{1,0:T(8,128)(2,1)S(1)} %copy-done, ...), custom_call_target="tpu_custom_call" | custom-call | flops 278921216 | bytes 8388608 | tf_op jit(solution)/shard_map/pallas_call | solution.py:288
  63.1 3.6 %collective-permute-done.1.high_ref = bf16[24,2,3584]{2,1,0:T(2,128)(2,1)} collective-permute-done((bf16[24,2,3584]{2,1,0:T(2,128)(2,1)S(1)}, bf16[24,2,3584]{2,1,0:T(2,128)(2,1)}, u32[]{:S(2)}, u32[]{:S(2)}) %collective-permute-start.1) | collective-permute-done | bytes 344096 | tf_op jit(solution)/shard_map/ppermute | solution.py:281
  66.7 2.8 %collective-permute-done.low_ref = bf16[40,2,3584]{2,1,0:T(2,128)(2,1)S(1)} collective-permute-done((bf16[40,2,3584]{2,1,0:T(2,128)(2,1)S(1)}, bf16[40,2,3584]{2,1,0:T(2,128)(2,1)S(1)}, u32[]{:S(2)}, u32[]{:S(2)}) %collective-permute-start) | collective-permute-done | bytes 573472 | tf_op jit(solution)/shard_map/ppermute | solution.py:280
  69.4 2.4 %shard_map.106 = (bf16[8,456,256]{2,1,0:T(8,128)(2,1)S(1)}, bf16[304,128]{1,0:T(8,128)(2,1)S(1)}, bf16[152,128]{1,0:T(8,128)(2,1)S(1)}, bf16[2,128,3712]{2,1,0:T(8,128)(2,1)S(1)}) custom-call(s32[1]{0:T(128)} %bitcast.replica_ref, s32[1]{0:T(128)} %bitcast.1.piece_at_ref, bf16[128,3712]{1,0:T(8,128)(2,1)S(1)} %get-tuple-element.31.first_ref, ...), custom_call_target="tpu_custom_call" | custom-call | tf_op jit(solution)/shard_map/pallas_call | solution.py:306
  71.9 1.9 %collective-permute-start.2 = (bf16[8,456,256]{2,1,0:T(8,128)(2,1)S(1)}, bf16[8,456,256]{2,1,0:T(8,128)(2,1)S(1)}, u32[]{:S(2)}, u32[]{:S(2)}) collective-permute-start(bf16[8,456,256]{2,1,0:T(8,128)(2,1)S(1)} %get-tuple-element.39), channel_id=1, source_target_pairs={{0,1},{1,0},{2,3},{3,2},{4,5},{5,4},{6,7},{7,6},{8,9},{9,8},{10,11... | collective-permute-start | bytes 5603336 | tf_op jit(solution)/shard_map/ppermute | solution.py:323
  73.8 1.6 %shard_map.111 = bf16[64,2,3584]{2,1,0:T(2,128)(2,1)} custom-call(bf16[304,128]{1,0:T(8,128)(2,1)S(1)} %get-tuple-element.36.pre_ref, bf16[152,3584]{1,0:T(8,128)(2,1)S(1)} %copy-done, bf16[152,3584]{1,0:T(8,128)(2,1)S(1)} %get-tuple-element.32.up_ref), custom_call_target="tpu_custom_call" | custom-call | flops 278921216 | bytes 4194304 | tf_op jit(solution)/shard_map/pallas_call | solution.py:352
  75.4 0.7 shard_map.107.mine_ref
  76.1 1.5 %collective-permute-done.2.theirs_ref = bf16[8,456,256]{2,1,0:T(8,128)(2,1)S(1)} collective-permute-done((bf16[8,456,256]{2,1,0:T(8,128)(2,1)S(1)}, bf16[8,456,256]{2,1,0:T(8,128)(2,1)S(1)}, u32[]{:S(2)}, u32[]{:S(2)}) %collective-permute-start.2) | collective-permute-done | bytes 1867808 | tf_op jit(solution)/shard_map/ppermute | solution.py:323
  77.6 0.4 shard_map.108
  78.0 7.5 %all-to-all-start.1 = ((bf16[64,2,3584]{2,1,0:T(2,128)(2,1)}), bf16[64,2,3584]{2,1,0:T(2,128)(2,1)S(1)}, u32[]{:S(2)}, u32[]{:S(2)}) async-start(bf16[64,2,3584]{2,1,0:T(2,128)(2,1)} %shard_map.111), calls=%async_computation.1 | async-start | bytes 1835008 | tf_op jit(solution)/shard_map/all_to_all | solution.py:375
  85.5 2.5 %collective-permute-start.6 = (bf16[456,256]{1,0:T(8,128)(2,1)S(1)}, bf16[456,256]{1,0:T(8,128)(2,1)S(1)}, u32[]{:S(2)}, u32[]{:S(2)}) collective-permute-start(bf16[456,256]{1,0:T(8,128)(2,1)S(1)} %get-tuple-element.47), channel_id=1, source_target_pairs={{0,2},{1,3},{2,4},{3,5},{4,6},{5,7},{6,8},{7,9},{8,10},{9,11},{10,... | collective-permute-start | bytes 700424 | tf_op jit(solution)/shard_map/ppermute | solution.py:369
  88.0 4.6 %collective-permute-start.3 = (bf16[456,256]{1,0:T(8,128)(2,1)S(1)}, bf16[456,256]{1,0:T(8,128)(2,1)S(1)}, u32[]{:S(2)}, u32[]{:S(2)}) collective-permute-start(bf16[456,256]{1,0:T(8,128)(2,1)S(1)} %get-tuple-element.40), channel_id=1, source_target_pairs={{0,14},{1,15},{2,0},{3,1},{4,2},{5,3},{6,4},{7,5},{8,6},{9,7},{10,... | collective-permute-start | bytes 700424 | tf_op jit(solution)/shard_map/ppermute | solution.py:370
  92.6 3.5 %collective-permute-done.6.got_ref = bf16[456,256]{1,0:T(8,128)(2,1)S(1)} collective-permute-done((bf16[456,256]{1,0:T(8,128)(2,1)S(1)}, bf16[456,256]{1,0:T(8,128)(2,1)S(1)}, u32[]{:S(2)}, u32[]{:S(2)}) %collective-permute-start.6) | collective-permute-done | bytes 233504 | tf_op jit(solution)/shard_map/ppermute | solution.py:369
  96.1 0.1 shard_map.113
  96.1 1.9 %collective-permute-start.7 = (bf16[456,256]{1,0:T(8,128)(2,1)S(1)}, bf16[456,256]{1,0:T(8,128)(2,1)S(1)}, u32[]{:S(2)}, u32[]{:S(2)}) collective-permute-start(bf16[456,256]{1,0:T(8,128)(2,1)S(1)} %shard_map.113), channel_id=1, source_target_pairs={{0,2},{1,3},{2,4},{3,5},{4,6},{5,7},{6,8},{7,9},{8,10},{9,11},{10,... | collective-permute-start | bytes 700424 | tf_op jit(solution)/shard_map/ppermute | solution.py:372
  98.1 0.0 collective-permute-done.3.got_ref
  98.1 0.1 shard_map.109
  98.1 5.1 %collective-permute-start.4 = (bf16[456,256]{1,0:T(8,128)(2,1)S(1)}, bf16[456,256]{1,0:T(8,128)(2,1)S(1)}, u32[]{:S(2)}, u32[]{:S(2)}) collective-permute-start(bf16[456,256]{1,0:T(8,128)(2,1)S(1)} %shard_map.109), channel_id=1, source_target_pairs={{0,14},{1,15},{2,0},{3,1},{4,2},{5,3},{6,4},{7,5},{8,6},{9,7},{10,... | collective-permute-start | bytes 700424 | tf_op jit(solution)/shard_map/ppermute | solution.py:374
  103.3 2.5 %collective-permute-done.7.got_ref = bf16[456,256]{1,0:T(8,128)(2,1)S(1)} collective-permute-done((bf16[456,256]{1,0:T(8,128)(2,1)S(1)}, bf16[456,256]{1,0:T(8,128)(2,1)S(1)}, u32[]{:S(2)}, u32[]{:S(2)}) %collective-permute-start.7) | collective-permute-done | bytes 233504 | tf_op jit(solution)/shard_map/ppermute | solution.py:372
  105.8 0.1 shard_map.114
  105.9 1.9 %collective-permute-start.8 = (bf16[456,256]{1,0:T(8,128)(2,1)S(1)}, bf16[456,256]{1,0:T(8,128)(2,1)S(1)}, u32[]{:S(2)}, u32[]{:S(2)}) collective-permute-start(bf16[456,256]{1,0:T(8,128)(2,1)S(1)} %shard_map.114), channel_id=1, source_target_pairs={{0,2},{1,3},{2,4},{3,5},{4,6},{5,7},{6,8},{7,9},{8,10},{9,11},{10,... | collective-permute-start | bytes 700424 | tf_op jit(solution)/shard_map/ppermute | solution.py:372
  107.8 0.0 collective-permute-done.4.got_ref
  107.8 0.1 shard_map.110
  107.9 5.1 %collective-permute-start.5 = (bf16[456,256]{1,0:T(8,128)(2,1)S(1)}, bf16[456,256]{1,0:T(8,128)(2,1)S(1)}, u32[]{:S(2)}, u32[]{:S(2)}) collective-permute-start(bf16[456,256]{1,0:T(8,128)(2,1)S(1)} %shard_map.110), channel_id=1, source_target_pairs={{0,14},{1,15},{2,0},{3,1},{4,2},{5,3},{6,4},{7,5},{8,6},{9,7},{10,... | collective-permute-start | bytes 700424 | tf_op jit(solution)/shard_map/ppermute | solution.py:374
  113.0 2.0 %collective-permute-done.8.got_ref = bf16[456,256]{1,0:T(8,128)(2,1)S(1)} collective-permute-done((bf16[456,256]{1,0:T(8,128)(2,1)S(1)}, bf16[456,256]{1,0:T(8,128)(2,1)S(1)}, u32[]{:S(2)}, u32[]{:S(2)}) %collective-permute-start.8) | collective-permute-done | bytes 233504 | tf_op jit(solution)/shard_map/ppermute | solution.py:372
  115.0 0.1 shard_map.115
  115.1 1.9 %collective-permute-start.9 = (bf16[456,256]{1,0:T(8,128)(2,1)S(1)}, bf16[456,256]{1,0:T(8,128)(2,1)S(1)}, u32[]{:S(2)}, u32[]{:S(2)}) collective-permute-start(bf16[456,256]{1,0:T(8,128)(2,1)S(1)} %shard_map.115), channel_id=1, source_target_pairs={{0,2},{1,3},{2,4},{3,5},{4,6},{5,7},{6,8},{7,9},{8,10},{9,11},{10,... | collective-permute-start | bytes 700424 | tf_op jit(solution)/shard_map/ppermute | solution.py:372
  117.0 0.0 all-to-all-done.1.rows_ref
  117.0 1.4 %shard_map.112 = bf16[128,3584]{1,0:T(8,128)(2,1)} custom-call(bf16[128,128]{1,0:T(8,128)(2,1)S(1)} %get-tuple-element.43.table_ref, bf16[64,2,3584]{2,1,0:T(2,128)(2,1)S(1)} %all-to-all-done.1.rows_ref), custom_call_target="tpu_custom_call" | custom-call | flops 117440512 | bytes 2097152 | tf_op jit(solution)/shard_map/pallas_call | solution.py:376
  118.4 0.0 collective-permute-done.5.down_ring_ref
  118.4 5.9 %collective-permute-done.9.up_ring_ref = bf16[456,256]{1,0:T(8,128)(2,1)S(1)} collective-permute-done((bf16[456,256]{1,0:T(8,128)(2,1)S(1)}, bf16[456,256]{1,0:T(8,128)(2,1)S(1)}, u32[]{:S(2)}, u32[]{:S(2)}) %collective-permute-start.9) | collective-permute-done | bytes 233504 | tf_op jit(solution)/shard_map/ppermute | solution.py:372
  124.3 0.7 shard_map.116
  (2 shorter events, 0.1 us)
Async XLA Ops:
  53.7 7.3 %copy-start = (bf16[152,3584]{1,0:T(8,128)(2,1)S(1)}, bf16[152,3584]{1,0:T(8,128)(2,1)}, u32[]{:S(2)}) copy-start(bf16[152,3584]{1,0:T(8,128)(2,1)} %gate_ref.5) | copy-start | bytes 3268612
  53.8 15.7 %collective-permute-start = (bf16[40,2,3584]{2,1,0:T(2,128)(2,1)S(1)}, bf16[40,2,3584]{2,1,0:T(2,128)(2,1)S(1)}, u32[]{:S(2)}, u32[]{:S(2)}) collective-permute-start(bf16[40,2,3584]{2,1,0:T(2,128)(2,1)S(1)} %shard_map.104), channel_id=1, source_target_pairs={{0,16},{16,32},{32,48},{48,64},{64,80},{80,96},{96,112},{112,0},{1... | collective-permute-start | bytes 1720328 | tf_op jit(solution)/shard_map/ppermute | solution.py:280
  57.0 9.7 %collective-permute-start.1 = (bf16[24,2,3584]{2,1,0:T(2,128)(2,1)S(1)}, bf16[24,2,3584]{2,1,0:T(2,128)(2,1)}, u32[]{:S(2)}, u32[]{:S(2)}) collective-permute-start(bf16[24,2,3584]{2,1,0:T(2,128)(2,1)S(1)} %shard_map.105), channel_id=1, source_target_pairs={{0,112},{16,0},{32,16},{48,32},{64,48},{80,64},{96,80},{112,96},{1... | collective-permute-start | bytes 1032200 | tf_op jit(solution)/shard_map/ppermute | solution.py:281
  71.9 5.7 %collective-permute-start.2 = (bf16[8,456,256]{2,1,0:T(8,128)(2,1)S(1)}, bf16[8,456,256]{2,1,0:T(8,128)(2,1)S(1)}, u32[]{:S(2)}, u32[]{:S(2)}) collective-permute-start(bf16[8,456,256]{2,1,0:T(8,128)(2,1)S(1)} %get-tuple-element.39), channel_id=1, source_target_pairs={{0,1},{1,0},{2,3},{3,2},{4,5},{5,4},{6,7},{7,6},{8,9},{9,8},{10,11... | collective-permute-start | bytes 5603336 | tf_op jit(solution)/shard_map/ppermute | solution.py:323
  78.0 39.0 %all-to-all-start.1 = ((bf16[64,2,3584]{2,1,0:T(2,128)(2,1)}), bf16[64,2,3584]{2,1,0:T(2,128)(2,1)S(1)}, u32[]{:S(2)}, u32[]{:S(2)}) async-start(bf16[64,2,3584]{2,1,0:T(2,128)(2,1)} %shard_map.111), calls=%async_computation.1 | async-start | bytes 1835008 | tf_op jit(solution)/shard_map/all_to_all | solution.py:375
  85.5 10.6 %collective-permute-start.6 = (bf16[456,256]{1,0:T(8,128)(2,1)S(1)}, bf16[456,256]{1,0:T(8,128)(2,1)S(1)}, u32[]{:S(2)}, u32[]{:S(2)}) collective-permute-start(bf16[456,256]{1,0:T(8,128)(2,1)S(1)} %get-tuple-element.47), channel_id=1, source_target_pairs={{0,2},{1,3},{2,4},{3,5},{4,6},{5,7},{6,8},{7,9},{8,10},{9,11},{10,... | collective-permute-start | bytes 700424 | tf_op jit(solution)/shard_map/ppermute | solution.py:369
  88.0 10.1 %collective-permute-start.3 = (bf16[456,256]{1,0:T(8,128)(2,1)S(1)}, bf16[456,256]{1,0:T(8,128)(2,1)S(1)}, u32[]{:S(2)}, u32[]{:S(2)}) collective-permute-start(bf16[456,256]{1,0:T(8,128)(2,1)S(1)} %get-tuple-element.40), channel_id=1, source_target_pairs={{0,14},{1,15},{2,0},{3,1},{4,2},{5,3},{6,4},{7,5},{8,6},{9,7},{10,... | collective-permute-start | bytes 700424 | tf_op jit(solution)/shard_map/ppermute | solution.py:370
  96.1 9.7 %collective-permute-start.7 = (bf16[456,256]{1,0:T(8,128)(2,1)S(1)}, bf16[456,256]{1,0:T(8,128)(2,1)S(1)}, u32[]{:S(2)}, u32[]{:S(2)}) collective-permute-start(bf16[456,256]{1,0:T(8,128)(2,1)S(1)} %shard_map.113), channel_id=1, source_target_pairs={{0,2},{1,3},{2,4},{3,5},{4,6},{5,7},{6,8},{7,9},{8,10},{9,11},{10,... | collective-permute-start | bytes 700424 | tf_op jit(solution)/shard_map/ppermute | solution.py:372
  98.1 9.7 %collective-permute-start.4 = (bf16[456,256]{1,0:T(8,128)(2,1)S(1)}, bf16[456,256]{1,0:T(8,128)(2,1)S(1)}, u32[]{:S(2)}, u32[]{:S(2)}) collective-permute-start(bf16[456,256]{1,0:T(8,128)(2,1)S(1)} %shard_map.109), channel_id=1, source_target_pairs={{0,14},{1,15},{2,0},{3,1},{4,2},{5,3},{6,4},{7,5},{8,6},{9,7},{10,... | collective-permute-start | bytes 700424 | tf_op jit(solution)/shard_map/ppermute | solution.py:374
  105.9 9.2 %collective-permute-start.8 = (bf16[456,256]{1,0:T(8,128)(2,1)S(1)}, bf16[456,256]{1,0:T(8,128)(2,1)S(1)}, u32[]{:S(2)}, u32[]{:S(2)}) collective-permute-start(bf16[456,256]{1,0:T(8,128)(2,1)S(1)} %shard_map.114), channel_id=1, source_target_pairs={{0,2},{1,3},{2,4},{3,5},{4,6},{5,7},{6,8},{7,9},{8,10},{9,11},{10,... | collective-permute-start | bytes 700424 | tf_op jit(solution)/shard_map/ppermute | solution.py:372
  107.9 10.5 %collective-permute-start.5 = (bf16[456,256]{1,0:T(8,128)(2,1)S(1)}, bf16[456,256]{1,0:T(8,128)(2,1)S(1)}, u32[]{:S(2)}, u32[]{:S(2)}) collective-permute-start(bf16[456,256]{1,0:T(8,128)(2,1)S(1)} %shard_map.110), channel_id=1, source_target_pairs={{0,14},{1,15},{2,0},{3,1},{4,2},{5,3},{6,4},{7,5},{8,6},{9,7},{10,... | collective-permute-start | bytes 700424 | tf_op jit(solution)/shard_map/ppermute | solution.py:374
  115.1 9.2 %collective-permute-start.9 = (bf16[456,256]{1,0:T(8,128)(2,1)S(1)}, bf16[456,256]{1,0:T(8,128)(2,1)S(1)}, u32[]{:S(2)}, u32[]{:S(2)}) collective-permute-start(bf16[456,256]{1,0:T(8,128)(2,1)S(1)} %shard_map.115), channel_id=1, source_target_pairs={{0,2},{1,3},{2,4},{3,5},{4,6},{5,7},{6,8},{7,9},{8,10},{9,11},{10,... | collective-permute-start | bytes 700424 | tf_op jit(solution)/shard_map/ppermute | solution.py:372

commit v5 on v4

--- a/solution.py
+++ b/solution.py
@@ -9,33 +9,41 @@
 
 EXPERTS = 4
 CAP = 2
+LOADS = 4
 
 
 def select_kernel(
     ids_hbm, gates_hbm, tokens_hbm, cotan_hbm, send_ref, table_ref, ids_ref, gates_ref, tokens_ref,
-    cotan_ref, rows_ref, in_sems, out_sems,
+    cotan_ref, rows_ref, in_sems, row_sems, out_sems,
 ):
     slots, tokens = EXPERTS * CAP, table_ref.shape[1]
+    load_ids = pltpu.make_async_copy(ids_hbm, ids_ref, in_sems.at[0])
+    load_gates = pltpu.make_async_copy(gates_hbm, gates_ref, in_sems.at[1])
+    load_ids.start()
+    load_gates.start()
+    tall = tokens_ref.shape[0] // LOADS
     loads = [
-        pltpu.make_async_copy(source, target, in_sems.at[index])
+        [
+            pltpu.make_async_copy(
+                source.at[pl.ds(part * tall, tall)],
+                target.at[pl.ds(part * tall, tall)],
+                row_sems.at[index, part],
+            )
+            for part in range(LOADS)
+        ]
         for index, (source, target) in enumerate(
-            (
-                (ids_hbm, ids_ref),
-                (gates_hbm, gates_ref),
-                (tokens_hbm, tokens_ref),
-                (cotan_hbm, cotan_ref),
-            )
+            ((tokens_hbm, tokens_ref), (cotan_hbm, cotan_ref))
         )
     ]
-    for load in loads:
-        load.start()
+    for part in loads[0] + loads[1]:
+        part.start()
     slot = lax.broadcasted_iota(jnp.int32, (slots, tokens), 0)
     expert, place = slot // CAP, slot % CAP
     earlier = lax.broadcasted_iota(jnp.int32, (tokens, tokens), 0) < lax.broadcasted_iota(
         jnp.int32, (tokens, tokens), 1
     )
     earlier = jnp.where(earlier, 1.0, 0.0).astype(jnp.bfloat16)
-    loads[0].wait()
+    load_ids.wait()
     first = ids_ref[0:1, :] == expert
     second = ids_ref[1:2, :] == expert
     named = jnp.where(first | second, 1.0, 0.0)
@@ -49,12 +57,13 @@
             here = (sub // per_expert == e) & (sub % CAP == p)
             repeated = jnp.where(here, table[e * CAP + p : e * CAP + p + 1, :], repeated)
     table_ref[...] = repeated.astype(jnp.bfloat16)
-    loads[1].wait()
+    load_gates.wait()
     gates = gates_ref[...].astype(jnp.float32)
     gated = table * jnp.where(first, gates[0:1, :], gates[1:2, :])
     stores = []
     for half, (weight, source_ref) in enumerate(((table, tokens_ref), (gated, cotan_ref))):
-        loads[2 + half].wait()
+        for part in loads[half]:
+            part.wait()
         picked = jnp.dot(
             weight.astype(jnp.bfloat16), source_ref[...], preferred_element_type=jnp.float32
         )
@@ -250,7 +259,8 @@
             pltpu.VMEM((token_count, feature_count), jnp.bfloat16),
             pltpu.VMEM((token_count, feature_count), jnp.bfloat16),
             pltpu.VMEM((2, EXPERTS, CAP, feature_count), jnp.bfloat16),
-            pltpu.SemaphoreType.DMA((4,)),
+            pltpu.SemaphoreType.DMA((2,)),
+            pltpu.SemaphoreType.DMA((2, LOADS)),
             pltpu.SemaphoreType.DMA((pieces,)),
         ],
         compiler_params=pltpu.CompilerParams(vmem_limit_bytes=16 * 2**20),
@@ -265,7 +275,7 @@
     ring = pieces // 2
     after = [(i, i // ring * ring + (i + 1) % ring) for i in range(device_count)]
     before = [(i, i // ring * ring + (i - 1) % ring) for i in range(device_count)]
-    split = device_count * 5 // 8
+    split = device_count // 2
 
     def part(start, size):
         return pl.pallas_call(

time: 126 us -> 127 us (level)
  starting transfers between devices: 39.6 us -> 40.9 us
where the time goes in v5:
time: 127 us; the launch traced here: 126 us
  blocking collectives  50.4 us (40%)
  starting transfers between devices  40.9 us (32%)
  waiting for transfers between devices  21.6 us (17%)
  Pallas kernels  12.3 us (10%)
    all_to_all x1, blocking collectives, shards(): lax.all_to_all(send.reshape(device_count, CAP, feature_count), 'expert',...  50.4 us
    ppermute x3, waiting for transfers between devices, shards(): rising = lax.ppermute(add(rising, chunks[distance]), 'dp', ahead)  10.4 us
    ppermute x2, starting transfers between devices, shards(): lax.ppermute(add(falling, chunks[chips - distance + 1]), 'dp', back)  10.3 us
    all_to_all x1, starting transfers between devices, shards(): lax.all_to_all(piece_grad, 'expert', split_axis=0, concat_axis=0, tiled=T...  8.72 us
    ppermute x3, starting transfers between devices, shards(): rising = lax.ppermute(add(rising, chunks[distance]), 'dp', ahead)  5.76 us
    ppermute x1, starting transfers between devices, shards(): falling = lax.ppermute(chunks[chips - far + 1], 'dp', back)  4.56 us
    ppermute x1, starting transfers between devices, shards(): high = lax.ppermute(high, 'expert', before)  4 us
    ppermute x1, waiting for transfers between devices, shards(): rising = lax.ppermute(chunks[far], 'dp', ahead)  3.49 us
  transfers between devices with their start and end apart: 11, of which 7 were waited for; matrix products, arithmetic and copies ran while one was open for 0% of the time, Pallas kernels for 5%

profile of v5, /device:TPU:8, one launch (start us, length us, event | category | flops | bytes accessed | tf_op | source)
XLA Modules:
  0.0 126.0 jit_solution(8704160472902121023)
XLA Ops:
  0.6 2.8 %shard_map.102 = (bf16[4,16,2,3584]{3,2,1,0:T(2,128)(2,1)}, bf16[128,128]{1,0:T(8,128)(2,1)S(1)}) custom-call(s32[2,128]{1,0:T(2,128)} %bitcast.6, bf16[2,128]{1,0:T(2,128)(2,1)} %bitcast.7, bf16[128,3584]{1,0:T(8,128)(2,1)} %tokens_hbm.1, bf16[128,3584]{1,0:T(8,128)(2,1)} %cotan_hbm.1), custom_call_target="tpu_custom_call" | custom-call | tf_op jit(solution)/shard_map/pallas_call | solution.py:248
  3.5 50.4 %all_to_all.10.rows_ref = bf16[64,2,3584]{2,1,0:T(2,128)(2,1)S(1)} all-to-all(bf16[64,2,3584]{2,1,0:T(2,128)(2,1)} %bitcast.5), channel_id=1, replica_groups=mesh['expert'=64,'dp'=16] {'expert'}, dimensions={0} | all-to-all | bytes 1835008 | tf_op jit(solution)/shard_map/all_to_all | solution.py:268
  53.9 0.0 copy-start
  53.9 3.2 %collective-permute-start = (bf16[32,2,3584]{2,1,0:T(2,128)(2,1)S(1)}, bf16[32,2,3584]{2,1,0:T(2,128)(2,1)S(1)}, u32[]{:S(2)}, u32[]{:S(2)}) collective-permute-start(bf16[32,2,3584]{2,1,0:T(2,128)(2,1)S(1)} %shard_map.104), channel_id=1, source_target_pairs={{0,16},{16,32},{32,48},{48,64},{64,80},{80,96},{96,112},{112,0},{1... | collective-permute-start | bytes 1376264 | tf_op jit(solution)/shard_map/ppermute | solution.py:290
  57.1 0.8 shard_map.105
  57.9 4.0 %collective-permute-start.1 = (bf16[32,2,3584]{2,1,0:T(2,128)(2,1)}, bf16[32,2,3584]{2,1,0:T(2,128)(2,1)S(1)}, u32[]{:S(2)}, u32[]{:S(2)}) collective-permute-start(bf16[32,2,3584]{2,1,0:T(2,128)(2,1)} %shard_map.105), channel_id=1, source_target_pairs={{0,112},{16,0},{32,16},{48,32},{64,48},{80,64},{96,80},{112,96},{1... | collective-permute-start | bytes 1376264 | tf_op jit(solution)/shard_map/ppermute | solution.py:291
  61.9 0.0 copy-done
  61.9 2.0 %shard_map.103 = (bf16[128,3712]{1,0:T(8,128)(2,1)S(1)}, bf16[152,3584]{1,0:T(8,128)(2,1)S(1)}, bf16[152,3584]{1,0:T(8,128)(2,1)S(1)}, f32[2,152,128]{2,1,0:T(8,128)S(1)}, f32[152,128]{1,0:T(8,128)S(1)}) custom-call(s32[1]{0:T(128)} %bitcast.1.piece_at_ref, bf16[64,2,3584]{2,1,0:T(2,128)(2,1)S(1)} %all_to_all.10.rows_ref, bf16[152,3584]{1,0:T(8,128)(2,1)S(1)} %copy-done, ...), custom_call_target="tpu_custom_call" | custom-call | flops 278921216 | bytes 8388608 | tf_op jit(solution)/shard_map/pallas_call | solution.py:298
  64.0 3.1 %collective-permute-done.low_ref = bf16[32,2,3584]{2,1,0:T(2,128)(2,1)S(1)} collective-permute-done((bf16[32,2,3584]{2,1,0:T(2,128)(2,1)S(1)}, bf16[32,2,3584]{2,1,0:T(2,128)(2,1)S(1)}, u32[]{:S(2)}, u32[]{:S(2)}) %collective-permute-start) | collective-permute-done | bytes 458784 | tf_op jit(solution)/shard_map/ppermute | solution.py:290
  67.1 3.0 %collective-permute-done.1.high_ref = bf16[32,2,3584]{2,1,0:T(2,128)(2,1)S(1)} collective-permute-done((bf16[32,2,3584]{2,1,0:T(2,128)(2,1)}, bf16[32,2,3584]{2,1,0:T(2,128)(2,1)S(1)}, u32[]{:S(2)}, u32[]{:S(2)}) %collective-permute-start.1) | collective-permute-done | bytes 458784 | tf_op jit(solution)/shard_map/ppermute | solution.py:291
  70.1 1.5 %shard_map.106 = (bf16[8,456,256]{2,1,0:T(8,128)(2,1)S(1)}, bf16[304,128]{1,0:T(8,128)(2,1)S(1)}, bf16[152,128]{1,0:T(8,128)(2,1)S(1)}, bf16[2,128,3712]{2,1,0:T(8,128)(2,1)S(1)}) custom-call(s32[1]{0:T(128)} %bitcast.replica_ref, s32[1]{0:T(128)} %bitcast.1.piece_at_ref, bf16[128,3712]{1,0:T(8,128)(2,1)S(1)} %get-tuple-element.31.first_ref, ...), custom_call_target="tpu_custom_call" | custom-call | tf_op jit(solution)/shard_map/pallas_call | solution.py:316
  71.6 1.9 %collective-permute-start.2 = (bf16[8,456,256]{2,1,0:T(8,128)(2,1)S(1)}, bf16[8,456,256]{2,1,0:T(8,128)(2,1)S(1)}, u32[]{:S(2)}, u32[]{:S(2)}) collective-permute-start(bf16[8,456,256]{2,1,0:T(8,128)(2,1)S(1)} %get-tuple-element.39), channel_id=1, source_target_pairs={{0,1},{1,0},{2,3},{3,2},{4,5},{5,4},{6,7},{7,6},{8,9},{9,8},{10,11... | collective-permute-start | bytes 5603336 | tf_op jit(solution)/shard_map/ppermute | solution.py:333
  73.5 1.6 %shard_map.111 = bf16[64,2,3584]{2,1,0:T(2,128)(2,1)} custom-call(bf16[304,128]{1,0:T(8,128)(2,1)S(1)} %get-tuple-element.36.pre_ref, bf16[152,3584]{1,0:T(8,128)(2,1)S(1)} %copy-done, bf16[152,3584]{1,0:T(8,128)(2,1)S(1)} %get-tuple-element.32.up_ref), custom_call_target="tpu_custom_call" | custom-call | flops 278921216 | bytes 4194304 | tf_op jit(solution)/shard_map/pallas_call | solution.py:362
  75.2 0.7 shard_map.107.mine_ref
  75.9 1.5 %collective-permute-done.2.theirs_ref = bf16[8,456,256]{2,1,0:T(8,128)(2,1)S(1)} collective-permute-done((bf16[8,456,256]{2,1,0:T(8,128)(2,1)S(1)}, bf16[8,456,256]{2,1,0:T(8,128)(2,1)S(1)}, u32[]{:S(2)}, u32[]{:S(2)}) %collective-permute-start.2) | collective-permute-done | bytes 1867808 | tf_op jit(solution)/shard_map/ppermute | solution.py:333
  77.3 0.4 shard_map.108
  77.8 8.7 %all-to-all-start.1 = ((bf16[64,2,3584]{2,1,0:T(2,128)(2,1)}), bf16[64,2,3584]{2,1,0:T(2,128)(2,1)S(1)}, u32[]{:S(2)}, u32[]{:S(2)}) async-start(bf16[64,2,3584]{2,1,0:T(2,128)(2,1)} %shard_map.111), calls=%async_computation.1 | async-start | bytes 1835008 | tf_op jit(solution)/shard_map/all_to_all | solution.py:385
  86.5 2.5 %collective-permute-start.6 = (bf16[456,256]{1,0:T(8,128)(2,1)S(1)}, bf16[456,256]{1,0:T(8,128)(2,1)S(1)}, u32[]{:S(2)}, u32[]{:S(2)}) collective-permute-start(bf16[456,256]{1,0:T(8,128)(2,1)S(1)} %get-tuple-element.47), channel_id=1, source_target_pairs={{0,2},{1,3},{2,4},{3,5},{4,6},{5,7},{6,8},{7,9},{8,10},{9,11},{10,... | collective-permute-start | bytes 700424 | tf_op jit(solution)/shard_map/ppermute | solution.py:379
  89.0 4.6 %collective-permute-start.3 = (bf16[456,256]{1,0:T(8,128)(2,1)S(1)}, bf16[456,256]{1,0:T(8,128)(2,1)S(1)}, u32[]{:S(2)}, u32[]{:S(2)}) collective-permute-start(bf16[456,256]{1,0:T(8,128)(2,1)S(1)} %get-tuple-element.40), channel_id=1, source_target_pairs={{0,14},{1,15},{2,0},{3,1},{4,2},{5,3},{6,4},{7,5},{8,6},{9,7},{10,... | collective-permute-start | bytes 700424 | tf_op jit(solution)/shard_map/ppermute | solution.py:380
  93.6 3.5 %collective-permute-done.6.got_ref = bf16[456,256]{1,0:T(8,128)(2,1)S(1)} collective-permute-done((bf16[456,256]{1,0:T(8,128)(2,1)S(1)}, bf16[456,256]{1,0:T(8,128)(2,1)S(1)}, u32[]{:S(2)}, u32[]{:S(2)}) %collective-permute-start.6) | collective-permute-done | bytes 233504 | tf_op jit(solution)/shard_map/ppermute | solution.py:379
  97.1 0.1 shard_map.113
  97.1 1.9 %collective-permute-start.7 = (bf16[456,256]{1,0:T(8,128)(2,1)S(1)}, bf16[456,256]{1,0:T(8,128)(2,1)S(1)}, u32[]{:S(2)}, u32[]{:S(2)}) collective-permute-start(bf16[456,256]{1,0:T(8,128)(2,1)S(1)} %shard_map.113), channel_id=1, source_target_pairs={{0,2},{1,3},{2,4},{3,5},{4,6},{5,7},{6,8},{7,9},{8,10},{9,11},{10,... | collective-permute-start | bytes 700424 | tf_op jit(solution)/shard_map/ppermute | solution.py:382
  99.0 0.0 collective-permute-done.3.got_ref
  99.1 0.1 shard_map.109
  99.1 5.1 %collective-permute-start.4 = (bf16[456,256]{1,0:T(8,128)(2,1)S(1)}, bf16[456,256]{1,0:T(8,128)(2,1)S(1)}, u32[]{:S(2)}, u32[]{:S(2)}) collective-permute-start(bf16[456,256]{1,0:T(8,128)(2,1)S(1)} %shard_map.109), channel_id=1, source_target_pairs={{0,14},{1,15},{2,0},{3,1},{4,2},{5,3},{6,4},{7,5},{8,6},{9,7},{10,... | collective-permute-start | bytes 700424 | tf_op jit(solution)/shard_map/ppermute | solution.py:384
  104.3 2.5 %collective-permute-done.7.got_ref = bf16[456,256]{1,0:T(8,128)(2,1)S(1)} collective-permute-done((bf16[456,256]{1,0:T(8,128)(2,1)S(1)}, bf16[456,256]{1,0:T(8,128)(2,1)S(1)}, u32[]{:S(2)}, u32[]{:S(2)}) %collective-permute-start.7) | collective-permute-done | bytes 233504 | tf_op jit(solution)/shard_map/ppermute | solution.py:382
  106.8 0.1 shard_map.114
  106.9 1.9 %collective-permute-start.8 = (bf16[456,256]{1,0:T(8,128)(2,1)S(1)}, bf16[456,256]{1,0:T(8,128)(2,1)S(1)}, u32[]{:S(2)}, u32[]{:S(2)}) collective-permute-start(bf16[456,256]{1,0:T(8,128)(2,1)S(1)} %shard_map.114), channel_id=1, source_target_pairs={{0,2},{1,3},{2,4},{3,5},{4,6},{5,7},{6,8},{7,9},{8,10},{9,11},{10,... | collective-permute-start | bytes 700424 | tf_op jit(solution)/shard_map/ppermute | solution.py:382
  108.8 0.0 collective-permute-done.4.got_ref
  108.8 0.1 shard_map.110
  108.9 5.1 %collective-permute-start.5 = (bf16[456,256]{1,0:T(8,128)(2,1)S(1)}, bf16[456,256]{1,0:T(8,128)(2,1)S(1)}, u32[]{:S(2)}, u32[]{:S(2)}) collective-permute-start(bf16[456,256]{1,0:T(8,128)(2,1)S(1)} %shard_map.110), channel_id=1, source_target_pairs={{0,14},{1,15},{2,0},{3,1},{4,2},{5,3},{6,4},{7,5},{8,6},{9,7},{10,... | collective-permute-start | bytes 700424 | tf_op jit(solution)/shard_map/ppermute | solution.py:384
  114.0 2.0 %collective-permute-done.8.got_ref = bf16[456,256]{1,0:T(8,128)(2,1)S(1)} collective-permute-done((bf16[456,256]{1,0:T(8,128)(2,1)S(1)}, bf16[456,256]{1,0:T(8,128)(2,1)S(1)}, u32[]{:S(2)}, u32[]{:S(2)}) %collective-permute-start.8) | collective-permute-done | bytes 233504 | tf_op jit(solution)/shard_map/ppermute | solution.py:382
  116.0 0.1 shard_map.115
  116.1 1.9 %collective-permute-start.9 = (bf16[456,256]{1,0:T(8,128)(2,1)S(1)}, bf16[456,256]{1,0:T(8,128)(2,1)S(1)}, u32[]{:S(2)}, u32[]{:S(2)}) collective-permute-start(bf16[456,256]{1,0:T(8,128)(2,1)S(1)} %shard_map.115), channel_id=1, source_target_pairs={{0,2},{1,3},{2,4},{3,5},{4,6},{5,7},{6,8},{7,9},{8,10},{9,11},{10,... | collective-permute-start | bytes 700424 | tf_op jit(solution)/shard_map/ppermute | solution.py:382
  118.0 0.0 all-to-all-done.1.rows_ref
  118.0 1.4 %shard_map.112 = bf16[128,3584]{1,0:T(8,128)(2,1)} custom-call(bf16[128,128]{1,0:T(8,128)(2,1)S(1)} %get-tuple-element.43.table_ref, bf16[64,2,3584]{2,1,0:T(2,128)(2,1)S(1)} %all-to-all-done.1.rows_ref), custom_call_target="tpu_custom_call" | custom-call | flops 117440512 | bytes 2097152 | tf_op jit(solution)/shard_map/pallas_call | solution.py:386
  119.4 0.0 collective-permute-done.5.down_ring_ref
  119.4 5.9 %collective-permute-done.9.up_ring_ref = bf16[456,256]{1,0:T(8,128)(2,1)S(1)} collective-permute-done((bf16[456,256]{1,0:T(8,128)(2,1)S(1)}, bf16[456,256]{1,0:T(8,128)(2,1)S(1)}, u32[]{:S(2)}, u32[]{:S(2)}) %collective-permute-start.9) | collective-permute-done | bytes 233504 | tf_op jit(solution)/shard_map/ppermute | solution.py:382
  125.3 0.7 shard_map.116
  (1 shorter events, 0.0 us)
Async XLA Ops:
  53.9 8.0 %copy-start = (bf16[152,3584]{1,0:T(8,128)(2,1)S(1)}, bf16[152,3584]{1,0:T(8,128)(2,1)}, u32[]{:S(2)}) copy-start(bf16[152,3584]{1,0:T(8,128)(2,1)} %gate_ref.5) | copy-start | bytes 3268612
  53.9 13.2 %collective-permute-start = (bf16[32,2,3584]{2,1,0:T(2,128)(2,1)S(1)}, bf16[32,2,3584]{2,1,0:T(2,128)(2,1)S(1)}, u32[]{:S(2)}, u32[]{:S(2)}) collective-permute-start(bf16[32,2,3584]{2,1,0:T(2,128)(2,1)S(1)} %shard_map.104), channel_id=1, source_target_pairs={{0,16},{16,32},{32,48},{48,64},{64,80},{80,96},{96,112},{112,0},{1... | collective-permute-start | bytes 1376264 | tf_op jit(solution)/shard_map/ppermute | solution.py:290
  57.9 12.2 %collective-permute-start.1 = (bf16[32,2,3584]{2,1,0:T(2,128)(2,1)}, bf16[32,2,3584]{2,1,0:T(2,128)(2,1)S(1)}, u32[]{:S(2)}, u32[]{:S(2)}) collective-permute-start(bf16[32,2,3584]{2,1,0:T(2,128)(2,1)} %shard_map.105), channel_id=1, source_target_pairs={{0,112},{16,0},{32,16},{48,32},{64,48},{80,64},{96,80},{112,96},{1... | collective-permute-start | bytes 1376264 | tf_op jit(solution)/shard_map/ppermute | solution.py:291
  71.6 5.7 %collective-permute-start.2 = (bf16[8,456,256]{2,1,0:T(8,128)(2,1)S(1)}, bf16[8,456,256]{2,1,0:T(8,128)(2,1)S(1)}, u32[]{:S(2)}, u32[]{:S(2)}) collective-permute-start(bf16[8,456,256]{2,1,0:T(8,128)(2,1)S(1)} %get-tuple-element.39), channel_id=1, source_target_pairs={{0,1},{1,0},{2,3},{3,2},{4,5},{5,4},{6,7},{7,6},{8,9},{9,8},{10,11... | collective-permute-start | bytes 5603336 | tf_op jit(solution)/shard_map/ppermute | solution.py:333
  77.8 40.3 %all-to-all-start.1 = ((bf16[64,2,3584]{2,1,0:T(2,128)(2,1)}), bf16[64,2,3584]{2,1,0:T(2,128)(2,1)S(1)}, u32[]{:S(2)}, u32[]{:S(2)}) async-start(bf16[64,2,3584]{2,1,0:T(2,128)(2,1)} %shard_map.111), calls=%async_computation.1 | async-start | bytes 1835008 | tf_op jit(solution)/shard_map/all_to_all | solution.py:385
  86.5 10.6 %collective-permute-start.6 = (bf16[456,256]{1,0:T(8,128)(2,1)S(1)}, bf16[456,256]{1,0:T(8,128)(2,1)S(1)}, u32[]{:S(2)}, u32[]{:S(2)}) collective-permute-start(bf16[456,256]{1,0:T(8,128)(2,1)S(1)} %get-tuple-element.47), channel_id=1, source_target_pairs={{0,2},{1,3},{2,4},{3,5},{4,6},{5,7},{6,8},{7,9},{8,10},{9,11},{10,... | collective-permute-start | bytes 700424 | tf_op jit(solution)/shard_map/ppermute | solution.py:379
  89.0 10.1 %collective-permute-start.3 = (bf16[456,256]{1,0:T(8,128)(2,1)S(1)}, bf16[456,256]{1,0:T(8,128)(2,1)S(1)}, u32[]{:S(2)}, u32[]{:S(2)}) collective-permute-start(bf16[456,256]{1,0:T(8,128)(2,1)S(1)} %get-tuple-element.40), channel_id=1, source_target_pairs={{0,14},{1,15},{2,0},{3,1},{4,2},{5,3},{6,4},{7,5},{8,6},{9,7},{10,... | collective-permute-start | bytes 700424 | tf_op jit(solution)/shard_map/ppermute | solution.py:380
  97.1 9.7 %collective-permute-start.7 = (bf16[456,256]{1,0:T(8,128)(2,1)S(1)}, bf16[456,256]{1,0:T(8,128)(2,1)S(1)}, u32[]{:S(2)}, u32[]{:S(2)}) collective-permute-start(bf16[456,256]{1,0:T(8,128)(2,1)S(1)} %shard_map.113), channel_id=1, source_target_pairs={{0,2},{1,3},{2,4},{3,5},{4,6},{5,7},{6,8},{7,9},{8,10},{9,11},{10,... | collective-permute-start | bytes 700424 | tf_op jit(solution)/shard_map/ppermute | solution.py:382
  99.1 9.7 %collective-permute-start.4 = (bf16[456,256]{1,0:T(8,128)(2,1)S(1)}, bf16[456,256]{1,0:T(8,128)(2,1)S(1)}, u32[]{:S(2)}, u32[]{:S(2)}) collective-permute-start(bf16[456,256]{1,0:T(8,128)(2,1)S(1)} %shard_map.109), channel_id=1, source_target_pairs={{0,14},{1,15},{2,0},{3,1},{4,2},{5,3},{6,4},{7,5},{8,6},{9,7},{10,... | collective-permute-start | bytes 700424 | tf_op jit(solution)/shard_map/ppermute | solution.py:384
  106.9 9.2 %collective-permute-start.8 = (bf16[456,256]{1,0:T(8,128)(2,1)S(1)}, bf16[456,256]{1,0:T(8,128)(2,1)S(1)}, u32[]{:S(2)}, u32[]{:S(2)}) collective-permute-start(bf16[456,256]{1,0:T(8,128)(2,1)S(1)} %shard_map.114), channel_id=1, source_target_pairs={{0,2},{1,3},{2,4},{3,5},{4,6},{5,7},{6,8},{7,9},{8,10},{9,11},{10,... | collective-permute-start | bytes 700424 | tf_op jit(solution)/shard_map/ppermute | solution.py:382
  108.9 10.5 %collective-permute-start.5 = (bf16[456,256]{1,0:T(8,128)(2,1)S(1)}, bf16[456,256]{1,0:T(8,128)(2,1)S(1)}, u32[]{:S(2)}, u32[]{:S(2)}) collective-permute-start(bf16[456,256]{1,0:T(8,128)(2,1)S(1)} %shard_map.110), channel_id=1, source_target_pairs={{0,14},{1,15},{2,0},{3,1},{4,2},{5,3},{6,4},{7,5},{8,6},{9,7},{10,... | collective-permute-start | bytes 700424 | tf_op jit(solution)/shard_map/ppermute | solution.py:384
  116.1 9.2 %collective-permute-start.9 = (bf16[456,256]{1,0:T(8,128)(2,1)S(1)}, bf16[456,256]{1,0:T(8,128)(2,1)S(1)}, u32[]{:S(2)}, u32[]{:S(2)}) collective-permute-start(bf16[456,256]{1,0:T(8,128)(2,1)S(1)} %shard_map.115), channel_id=1, source_target_pairs={{0,2},{1,3},{2,4},{3,5},{4,6},{5,7},{6,8},{7,9},{8,10},{9,11},{10,... | collective-permute-start | bytes 700424 | tf_op jit(solution)/shard_map/ppermute | solution.py:382

commit v6 on v4

--- a/solution.py
+++ b/solution.py
@@ -90,9 +90,9 @@
     part_ref[...] = rows_ref[start : start + part_ref.shape[0]]
 
 
-def flatten(rows_ref, lanes):
-    sources, cap, features = rows_ref.shape
-    flat = rows_ref[...].reshape(sources * cap, features)
+def flatten(rows, lanes):
+    sources, cap, features = rows.shape
+    flat = rows.reshape(sources * cap, features)
     beyond = jnp.zeros((sources * cap, lanes - features), jnp.bfloat16)
     return jnp.concatenate([flat, beyond], axis=1)
 
@@ -113,7 +113,7 @@
     load_down = pltpu.make_async_copy(down_hbm, down_ref, sems.at[1])
     load_up.start()
     load_down.start()
-    flat_ref[...] = flatten(rows_ref, flat_ref.shape[1])
+    flat_ref[...] = flatten(rows_ref[...], flat_ref.shape[1])
 
     @pl.when(piece_at_ref[0] & 1 == 0)
     def _():
@@ -135,11 +135,10 @@
     width, replica_ref, piece_at_ref, first_ref, low_ref, high_ref, gate_ref, up_ref, down_ref, done_forward_ref,
     done_back_ref, other_ref, pre_ref, act_ref, flat_ref, forward_ref, back_ref,
 ):
-    half = CAP * low_ref.shape[0]
     odd = piece_at_ref[0] & 1
     flat_ref[odd] = first_ref[...]
-    flat_ref[1 - odd, :half] = flatten(low_ref, flat_ref.shape[2])
-    flat_ref[1 - odd, half:] = flatten(high_ref, flat_ref.shape[2])
+    traded = jnp.concatenate([low_ref[...], high_ref[...]], axis=0)
+    flat_ref[1 - odd] = flatten(traded, flat_ref.shape[2])
 
     @pl.when(odd == 0)
     def _():

time: 126 us -> 126 us (level)
  no operation moved by 1% of the time
where the time goes in v6:
time: 126 us; the launch traced here: 125 us
  blocking collectives  50.4 us (40%)
  starting transfers between devices  39.6 us (31%)
  waiting for transfers between devices  21.8 us (17%)
  Pallas kernels  12.3 us (10%)
    all_to_all x1, blocking collectives, shards(): lax.all_to_all(send.reshape(device_count, CAP, feature_count), 'expert',...  50.4 us
    ppermute x3, waiting for transfers between devices, shards(): rising = lax.ppermute(add(rising, chunks[distance]), 'dp', ahead)  10.4 us
    ppermute x2, starting transfers between devices, shards(): lax.ppermute(add(falling, chunks[chips - distance + 1]), 'dp', back)  10.3 us
    all_to_all x1, starting transfers between devices, shards(): lax.all_to_all(piece_grad, 'expert', split_axis=0, concat_axis=0, tiled=T...  7.46 us
    ppermute x3, starting transfers between devices, shards(): rising = lax.ppermute(add(rising, chunks[distance]), 'dp', ahead)  5.76 us
    ppermute x1, starting transfers between devices, shards(): falling = lax.ppermute(chunks[chips - far + 1], 'dp', back)  4.56 us
    ppermute x1, starting transfers between devices, shards(): high = lax.ppermute(high, 'expert', before)  4.01 us
    ppermute x1, waiting for transfers between devices, shards(): high = lax.ppermute(high, 'expert', before)  3.58 us
  transfers between devices with their start and end apart: 11, of which 7 were waited for; matrix products, arithmetic and copies ran while one was open for 0% of the time, Pallas kernels for 5%

profile of v6, /device:TPU:8, one launch (start us, length us, event | category | flops | bytes accessed | tf_op | source)
XLA Modules:
  0.0 125.0 jit_solution(2364462944972643512)
XLA Ops:
  0.6 2.7 %shard_map.102 = (bf16[4,16,2,3584]{3,2,1,0:T(2,128)(2,1)}, bf16[128,128]{1,0:T(8,128)(2,1)S(1)}) custom-call(s32[2,128]{1,0:T(2,128)} %bitcast.6, bf16[2,128]{1,0:T(2,128)(2,1)} %bitcast.7, bf16[128,3584]{1,0:T(8,128)(2,1)} %tokens_hbm.1, bf16[128,3584]{1,0:T(8,128)(2,1)} %cotan_hbm.1), custom_call_target="tpu_custom_call" | custom-call | tf_op jit(solution)/shard_map/pallas_call | solution.py:238
  3.3 50.4 %all_to_all.10.rows_ref = bf16[64,2,3584]{2,1,0:T(2,128)(2,1)S(1)} all-to-all(bf16[64,2,3584]{2,1,0:T(2,128)(2,1)} %bitcast.5), channel_id=1, replica_groups=mesh['expert'=64,'dp'=16] {'expert'}, dimensions={0} | all-to-all | bytes 1835008 | tf_op jit(solution)/shard_map/all_to_all | solution.py:257
  53.7 0.0 copy-start
  53.8 3.2 %collective-permute-start = (bf16[40,2,3584]{2,1,0:T(2,128)(2,1)S(1)}, bf16[40,2,3584]{2,1,0:T(2,128)(2,1)S(1)}, u32[]{:S(2)}, u32[]{:S(2)}) collective-permute-start(bf16[40,2,3584]{2,1,0:T(2,128)(2,1)S(1)} %shard_map.104), channel_id=1, source_target_pairs={{0,16},{16,32},{32,48},{48,64},{64,80},{80,96},{96,112},{112,0},{1... | collective-permute-start | bytes 1720328 | tf_op jit(solution)/shard_map/ppermute | solution.py:279
  57.0 4.0 %collective-permute-start.1 = (bf16[24,2,3584]{2,1,0:T(2,128)(2,1)S(1)}, bf16[24,2,3584]{2,1,0:T(2,128)(2,1)}, u32[]{:S(2)}, u32[]{:S(2)}) collective-permute-start(bf16[24,2,3584]{2,1,0:T(2,128)(2,1)S(1)} %shard_map.105), channel_id=1, source_target_pairs={{0,112},{16,0},{32,16},{48,32},{64,48},{80,64},{96,80},{112,96},{1... | collective-permute-start | bytes 1032200 | tf_op jit(solution)/shard_map/ppermute | solution.py:280
  61.0 0.0 copy-done
  61.0 2.0 %shard_map.103 = (bf16[128,3712]{1,0:T(8,128)(2,1)S(1)}, bf16[152,3584]{1,0:T(8,128)(2,1)S(1)}, bf16[152,3584]{1,0:T(8,128)(2,1)S(1)}, f32[2,152,128]{2,1,0:T(8,128)S(1)}, f32[152,128]{1,0:T(8,128)S(1)}) custom-call(s32[1]{0:T(128)} %bitcast.1.piece_at_ref, bf16[64,2,3584]{2,1,0:T(2,128)(2,1)S(1)} %all_to_all.10.rows_ref, bf16[152,3584]{1,0:T(8,128)(2,1)S(1)} %copy-done, ...), custom_call_target="tpu_custom_call" | custom-call | flops 278921216 | bytes 8388608 | tf_op jit(solution)/shard_map/pallas_call | solution.py:287
  63.1 3.6 %collective-permute-done.1.high_ref = bf16[24,2,3584]{2,1,0:T(2,128)(2,1)} collective-permute-done((bf16[24,2,3584]{2,1,0:T(2,128)(2,1)S(1)}, bf16[24,2,3584]{2,1,0:T(2,128)(2,1)}, u32[]{:S(2)}, u32[]{:S(2)}) %collective-permute-start.1) | collective-permute-done | bytes 344096 | tf_op jit(solution)/shard_map/ppermute | solution.py:280
  66.7 2.8 %collective-permute-done.low_ref = bf16[40,2,3584]{2,1,0:T(2,128)(2,1)S(1)} collective-permute-done((bf16[40,2,3584]{2,1,0:T(2,128)(2,1)S(1)}, bf16[40,2,3584]{2,1,0:T(2,128)(2,1)S(1)}, u32[]{:S(2)}, u32[]{:S(2)}) %collective-permute-start) | collective-permute-done | bytes 573472 | tf_op jit(solution)/shard_map/ppermute | solution.py:279
  69.4 2.4 %shard_map.106 = (bf16[8,456,256]{2,1,0:T(8,128)(2,1)S(1)}, bf16[304,128]{1,0:T(8,128)(2,1)S(1)}, bf16[152,128]{1,0:T(8,128)(2,1)S(1)}, bf16[2,128,3712]{2,1,0:T(8,128)(2,1)S(1)}) custom-call(s32[1]{0:T(128)} %bitcast.replica_ref, s32[1]{0:T(128)} %bitcast.1.piece_at_ref, bf16[128,3712]{1,0:T(8,128)(2,1)S(1)} %get-tuple-element.31.first_ref, ...), custom_call_target="tpu_custom_call" | custom-call | tf_op jit(solution)/shard_map/pallas_call | solution.py:305
  71.9 1.9 %collective-permute-start.2 = (bf16[8,456,256]{2,1,0:T(8,128)(2,1)S(1)}, bf16[8,456,256]{2,1,0:T(8,128)(2,1)S(1)}, u32[]{:S(2)}, u32[]{:S(2)}) collective-permute-start(bf16[8,456,256]{2,1,0:T(8,128)(2,1)S(1)} %get-tuple-element.39), channel_id=1, source_target_pairs={{0,1},{1,0},{2,3},{3,2},{4,5},{5,4},{6,7},{7,6},{8,9},{9,8},{10,11... | collective-permute-start | bytes 5603336 | tf_op jit(solution)/shard_map/ppermute | solution.py:322
  73.8 1.6 %shard_map.111 = bf16[64,2,3584]{2,1,0:T(2,128)(2,1)} custom-call(bf16[304,128]{1,0:T(8,128)(2,1)S(1)} %get-tuple-element.36.pre_ref, bf16[152,3584]{1,0:T(8,128)(2,1)S(1)} %copy-done, bf16[152,3584]{1,0:T(8,128)(2,1)S(1)} %get-tuple-element.32.up_ref), custom_call_target="tpu_custom_call" | custom-call | flops 278921216 | bytes 4194304 | tf_op jit(solution)/shard_map/pallas_call | solution.py:351
  75.4 0.7 shard_map.107.mine_ref
  76.1 1.5 %collective-permute-done.2.theirs_ref = bf16[8,456,256]{2,1,0:T(8,128)(2,1)S(1)} collective-permute-done((bf16[8,456,256]{2,1,0:T(8,128)(2,1)S(1)}, bf16[8,456,256]{2,1,0:T(8,128)(2,1)S(1)}, u32[]{:S(2)}, u32[]{:S(2)}) %collective-permute-start.2) | collective-permute-done | bytes 1867808 | tf_op jit(solution)/shard_map/ppermute | solution.py:322
  77.6 0.4 shard_map.108
  78.0 7.5 %all-to-all-start.1 = ((bf16[64,2,3584]{2,1,0:T(2,128)(2,1)}), bf16[64,2,3584]{2,1,0:T(2,128)(2,1)S(1)}, u32[]{:S(2)}, u32[]{:S(2)}) async-start(bf16[64,2,3584]{2,1,0:T(2,128)(2,1)} %shard_map.111), calls=%async_computation.1 | async-start | bytes 1835008 | tf_op jit(solution)/shard_map/all_to_all | solution.py:374
  85.5 2.5 %collective-permute-start.6 = (bf16[456,256]{1,0:T(8,128)(2,1)S(1)}, bf16[456,256]{1,0:T(8,128)(2,1)S(1)}, u32[]{:S(2)}, u32[]{:S(2)}) collective-permute-start(bf16[456,256]{1,0:T(8,128)(2,1)S(1)} %get-tuple-element.47), channel_id=1, source_target_pairs={{0,2},{1,3},{2,4},{3,5},{4,6},{5,7},{6,8},{7,9},{8,10},{9,11},{10,... | collective-permute-start | bytes 700424 | tf_op jit(solution)/shard_map/ppermute | solution.py:368
  88.0 4.6 %collective-permute-start.3 = (bf16[456,256]{1,0:T(8,128)(2,1)S(1)}, bf16[456,256]{1,0:T(8,128)(2,1)S(1)}, u32[]{:S(2)}, u32[]{:S(2)}) collective-permute-start(bf16[456,256]{1,0:T(8,128)(2,1)S(1)} %get-tuple-element.40), channel_id=1, source_target_pairs={{0,14},{1,15},{2,0},{3,1},{4,2},{5,3},{6,4},{7,5},{8,6},{9,7},{10,... | collective-permute-start | bytes 700424 | tf_op jit(solution)/shard_map/ppermute | solution.py:369
  92.6 3.5 %collective-permute-done.6.got_ref = bf16[456,256]{1,0:T(8,128)(2,1)S(1)} collective-permute-done((bf16[456,256]{1,0:T(8,128)(2,1)S(1)}, bf16[456,256]{1,0:T(8,128)(2,1)S(1)}, u32[]{:S(2)}, u32[]{:S(2)}) %collective-permute-start.6) | collective-permute-done | bytes 233504 | tf_op jit(solution)/shard_map/ppermute | solution.py:368
  96.1 0.1 shard_map.113
  96.1 1.9 %collective-permute-start.7 = (bf16[456,256]{1,0:T(8,128)(2,1)S(1)}, bf16[456,256]{1,0:T(8,128)(2,1)S(1)}, u32[]{:S(2)}, u32[]{:S(2)}) collective-permute-start(bf16[456,256]{1,0:T(8,128)(2,1)S(1)} %shard_map.113), channel_id=1, source_target_pairs={{0,2},{1,3},{2,4},{3,5},{4,6},{5,7},{6,8},{7,9},{8,10},{9,11},{10,... | collective-permute-start | bytes 700424 | tf_op jit(solution)/shard_map/ppermute | solution.py:371
  98.1 0.0 collective-permute-done.3.got_ref
  98.1 0.1 shard_map.109
  98.1 5.1 %collective-permute-start.4 = (bf16[456,256]{1,0:T(8,128)(2,1)S(1)}, bf16[456,256]{1,0:T(8,128)(2,1)S(1)}, u32[]{:S(2)}, u32[]{:S(2)}) collective-permute-start(bf16[456,256]{1,0:T(8,128)(2,1)S(1)} %shard_map.109), channel_id=1, source_target_pairs={{0,14},{1,15},{2,0},{3,1},{4,2},{5,3},{6,4},{7,5},{8,6},{9,7},{10,... | collective-permute-start | bytes 700424 | tf_op jit(solution)/shard_map/ppermute | solution.py:373
  103.3 2.5 %collective-permute-done.7.got_ref = bf16[456,256]{1,0:T(8,128)(2,1)S(1)} collective-permute-done((bf16[456,256]{1,0:T(8,128)(2,1)S(1)}, bf16[456,256]{1,0:T(8,128)(2,1)S(1)}, u32[]{:S(2)}, u32[]{:S(2)}) %collective-permute-start.7) | collective-permute-done | bytes 233504 | tf_op jit(solution)/shard_map/ppermute | solution.py:371
  105.8 0.1 shard_map.114
  105.9 1.9 %collective-permute-start.8 = (bf16[456,256]{1,0:T(8,128)(2,1)S(1)}, bf16[456,256]{1,0:T(8,128)(2,1)S(1)}, u32[]{:S(2)}, u32[]{:S(2)}) collective-permute-start(bf16[456,256]{1,0:T(8,128)(2,1)S(1)} %shard_map.114), channel_id=1, source_target_pairs={{0,2},{1,3},{2,4},{3,5},{4,6},{5,7},{6,8},{7,9},{8,10},{9,11},{10,... | collective-permute-start | bytes 700424 | tf_op jit(solution)/shard_map/ppermute | solution.py:371
  107.8 0.0 collective-permute-done.4.got_ref
  107.8 0.1 shard_map.110
  107.9 5.1 %collective-permute-start.5 = (bf16[456,256]{1,0:T(8,128)(2,1)S(1)}, bf16[456,256]{1,0:T(8,128)(2,1)S(1)}, u32[]{:S(2)}, u32[]{:S(2)}) collective-permute-start(bf16[456,256]{1,0:T(8,128)(2,1)S(1)} %shard_map.110), channel_id=1, source_target_pairs={{0,14},{1,15},{2,0},{3,1},{4,2},{5,3},{6,4},{7,5},{8,6},{9,7},{10,... | collective-permute-start | bytes 700424 | tf_op jit(solution)/shard_map/ppermute | solution.py:373
  113.0 2.0 %collective-permute-done.8.got_ref = bf16[456,256]{1,0:T(8,128)(2,1)S(1)} collective-permute-done((bf16[456,256]{1,0:T(8,128)(2,1)S(1)}, bf16[456,256]{1,0:T(8,128)(2,1)S(1)}, u32[]{:S(2)}, u32[]{:S(2)}) %collective-permute-start.8) | collective-permute-done | bytes 233504 | tf_op jit(solution)/shard_map/ppermute | solution.py:371
  115.0 0.1 shard_map.115
  115.1 1.9 %collective-permute-start.9 = (bf16[456,256]{1,0:T(8,128)(2,1)S(1)}, bf16[456,256]{1,0:T(8,128)(2,1)S(1)}, u32[]{:S(2)}, u32[]{:S(2)}) collective-permute-start(bf16[456,256]{1,0:T(8,128)(2,1)S(1)} %shard_map.115), channel_id=1, source_target_pairs={{0,2},{1,3},{2,4},{3,5},{4,6},{5,7},{6,8},{7,9},{8,10},{9,11},{10,... | collective-permute-start | bytes 700424 | tf_op jit(solution)/shard_map/ppermute | solution.py:371
  117.0 0.0 all-to-all-done.1.rows_ref
  117.0 1.4 %shard_map.112 = bf16[128,3584]{1,0:T(8,128)(2,1)} custom-call(bf16[128,128]{1,0:T(8,128)(2,1)S(1)} %get-tuple-element.43.table_ref, bf16[64,2,3584]{2,1,0:T(2,128)(2,1)S(1)} %all-to-all-done.1.rows_ref), custom_call_target="tpu_custom_call" | custom-call | flops 117440512 | bytes 2097152 | tf_op jit(solution)/shard_map/pallas_call | solution.py:375
  118.4 0.0 collective-permute-done.5.down_ring_ref
  118.4 5.9 %collective-permute-done.9.up_ring_ref = bf16[456,256]{1,0:T(8,128)(2,1)S(1)} collective-permute-done((bf16[456,256]{1,0:T(8,128)(2,1)S(1)}, bf16[456,256]{1,0:T(8,128)(2,1)S(1)}, u32[]{:S(2)}, u32[]{:S(2)}) %collective-permute-start.9) | collective-permute-done | bytes 233504 | tf_op jit(solution)/shard_map/ppermute | solution.py:371
  124.3 0.7 shard_map.116
  (2 shorter events, 0.1 us)
Async XLA Ops:
  53.7 7.3 %copy-start = (bf16[152,3584]{1,0:T(8,128)(2,1)S(1)}, bf16[152,3584]{1,0:T(8,128)(2,1)}, u32[]{:S(2)}) copy-start(bf16[152,3584]{1,0:T(8,128)(2,1)} %gate_ref.5) | copy-start | bytes 3268612
  53.8 15.7 %collective-permute-start = (bf16[40,2,3584]{2,1,0:T(2,128)(2,1)S(1)}, bf16[40,2,3584]{2,1,0:T(2,128)(2,1)S(1)}, u32[]{:S(2)}, u32[]{:S(2)}) collective-permute-start(bf16[40,2,3584]{2,1,0:T(2,128)(2,1)S(1)} %shard_map.104), channel_id=1, source_target_pairs={{0,16},{16,32},{32,48},{48,64},{64,80},{80,96},{96,112},{112,0},{1... | collective-permute-start | bytes 1720328 | tf_op jit(solution)/shard_map/ppermute | solution.py:279
  57.0 9.7 %collective-permute-start.1 = (bf16[24,2,3584]{2,1,0:T(2,128)(2,1)S(1)}, bf16[24,2,3584]{2,1,0:T(2,128)(2,1)}, u32[]{:S(2)}, u32[]{:S(2)}) collective-permute-start(bf16[24,2,3584]{2,1,0:T(2,128)(2,1)S(1)} %shard_map.105), channel_id=1, source_target_pairs={{0,112},{16,0},{32,16},{48,32},{64,48},{80,64},{96,80},{112,96},{1... | collective-permute-start | bytes 1032200 | tf_op jit(solution)/shard_map/ppermute | solution.py:280
  71.9 5.7 %collective-permute-start.2 = (bf16[8,456,256]{2,1,0:T(8,128)(2,1)S(1)}, bf16[8,456,256]{2,1,0:T(8,128)(2,1)S(1)}, u32[]{:S(2)}, u32[]{:S(2)}) collective-permute-start(bf16[8,456,256]{2,1,0:T(8,128)(2,1)S(1)} %get-tuple-element.39), channel_id=1, source_target_pairs={{0,1},{1,0},{2,3},{3,2},{4,5},{5,4},{6,7},{7,6},{8,9},{9,8},{10,11... | collective-permute-start | bytes 5603336 | tf_op jit(solution)/shard_map/ppermute | solution.py:322
  78.0 39.0 %all-to-all-start.1 = ((bf16[64,2,3584]{2,1,0:T(2,128)(2,1)}), bf16[64,2,3584]{2,1,0:T(2,128)(2,1)S(1)}, u32[]{:S(2)}, u32[]{:S(2)}) async-start(bf16[64,2,3584]{2,1,0:T(2,128)(2,1)} %shard_map.111), calls=%async_computation.1 | async-start | bytes 1835008 | tf_op jit(solution)/shard_map/all_to_all | solution.py:374
  85.5 10.6 %collective-permute-start.6 = (bf16[456,256]{1,0:T(8,128)(2,1)S(1)}, bf16[456,256]{1,0:T(8,128)(2,1)S(1)}, u32[]{:S(2)}, u32[]{:S(2)}) collective-permute-start(bf16[456,256]{1,0:T(8,128)(2,1)S(1)} %get-tuple-element.47), channel_id=1, source_target_pairs={{0,2},{1,3},{2,4},{3,5},{4,6},{5,7},{6,8},{7,9},{8,10},{9,11},{10,... | collective-permute-start | bytes 700424 | tf_op jit(solution)/shard_map/ppermute | solution.py:368
  88.0 10.1 %collective-permute-start.3 = (bf16[456,256]{1,0:T(8,128)(2,1)S(1)}, bf16[456,256]{1,0:T(8,128)(2,1)S(1)}, u32[]{:S(2)}, u32[]{:S(2)}) collective-permute-start(bf16[456,256]{1,0:T(8,128)(2,1)S(1)} %get-tuple-element.40), channel_id=1, source_target_pairs={{0,14},{1,15},{2,0},{3,1},{4,2},{5,3},{6,4},{7,5},{8,6},{9,7},{10,... | collective-permute-start | bytes 700424 | tf_op jit(solution)/shard_map/ppermute | solution.py:369
  96.1 9.7 %collective-permute-start.7 = (bf16[456,256]{1,0:T(8,128)(2,1)S(1)}, bf16[456,256]{1,0:T(8,128)(2,1)S(1)}, u32[]{:S(2)}, u32[]{:S(2)}) collective-permute-start(bf16[456,256]{1,0:T(8,128)(2,1)S(1)} %shard_map.113), channel_id=1, source_target_pairs={{0,2},{1,3},{2,4},{3,5},{4,6},{5,7},{6,8},{7,9},{8,10},{9,11},{10,... | collective-permute-start | bytes 700424 | tf_op jit(solution)/shard_map/ppermute | solution.py:371
  98.1 9.7 %collective-permute-start.4 = (bf16[456,256]{1,0:T(8,128)(2,1)S(1)}, bf16[456,256]{1,0:T(8,128)(2,1)S(1)}, u32[]{:S(2)}, u32[]{:S(2)}) collective-permute-start(bf16[456,256]{1,0:T(8,128)(2,1)S(1)} %shard_map.109), channel_id=1, source_target_pairs={{0,14},{1,15},{2,0},{3,1},{4,2},{5,3},{6,4},{7,5},{8,6},{9,7},{10,... | collective-permute-start | bytes 700424 | tf_op jit(solution)/shard_map/ppermute | solution.py:373
  105.9 9.2 %collective-permute-start.8 = (bf16[456,256]{1,0:T(8,128)(2,1)S(1)}, bf16[456,256]{1,0:T(8,128)(2,1)S(1)}, u32[]{:S(2)}, u32[]{:S(2)}) collective-permute-start(bf16[456,256]{1,0:T(8,128)(2,1)S(1)} %shard_map.114), channel_id=1, source_target_pairs={{0,2},{1,3},{2,4},{3,5},{4,6},{5,7},{6,8},{7,9},{8,10},{9,11},{10,... | collective-permute-start | bytes 700424 | tf_op jit(solution)/shard_map/ppermute | solution.py:371
  107.9 10.5 %collective-permute-start.5 = (bf16[456,256]{1,0:T(8,128)(2,1)S(1)}, bf16[456,256]{1,0:T(8,128)(2,1)S(1)}, u32[]{:S(2)}, u32[]{:S(2)}) collective-permute-start(bf16[456,256]{1,0:T(8,128)(2,1)S(1)} %shard_map.110), channel_id=1, source_target_pairs={{0,14},{1,15},{2,0},{3,1},{4,2},{5,3},{6,4},{7,5},{8,6},{9,7},{10,... | collective-permute-start | bytes 700424 | tf_op jit(solution)/shard_map/ppermute | solution.py:373
  115.1 9.2 %collective-permute-start.9 = (bf16[456,256]{1,0:T(8,128)(2,1)S(1)}, bf16[456,256]{1,0:T(8,128)(2,1)S(1)}, u32[]{:S(2)}, u32[]{:S(2)}) collective-permute-start(bf16[456,256]{1,0:T(8,128)(2,1)S(1)} %shard_map.115), channel_id=1, source_target_pairs={{0,2},{1,3},{2,4},{3,5},{4,6},{5,7},{6,8},{7,9},{8,10},{9,11},{10,... | collective-permute-start | bytes 700424 | tf_op jit(solution)/shard_map/ppermute | solution.py:371

commit v7 on v6

--- a/solution.py
+++ b/solution.py
@@ -264,7 +264,7 @@
     ring = pieces // 2
     after = [(i, i // ring * ring + (i + 1) % ring) for i in range(device_count)]
     before = [(i, i // ring * ring + (i - 1) % ring) for i in range(device_count)]
-    split = device_count * 5 // 8
+    split = device_count * 9 // 16
 
     def part(start, size):
         return pl.pallas_call(

time: 126 us -> 125 us (level)
  waiting for transfers between devices: 21.8 us -> 20.4 us
  starting transfers between devices: 39.6 us -> 40.9 us
    ppermute x1, waiting for transfers between devices: 2.77 us -> 0.01 us  [shards(): low = lax.ppermute(low, 'expert', after)]
    ppermute x1, waiting for transfers between devices: 3.58 us -> 4.91 us  [shards(): high = lax.ppermute(high, 'expert', before)]
  transfers between devices with their start and end apart: 11 -> 11, of which waited for: 7 -> 6; matrix products, arithmetic and copies ran while one was open for 0% -> 0% of each run, Pallas kernels for 5% -> 5%
where the time goes in v7:
time: 125 us
  blocking collectives  50.4 us (40%)
  starting transfers between devices  40.9 us (33%)
  waiting for transfers between devices  20.4 us (16%)
  Pallas kernels  12.1 us (10%)
    all_to_all x1, blocking collectives, shards(): lax.all_to_all(send.reshape(device_count, CAP, feature_count), 'expert',...  50.4 us
    ppermute x3, waiting for transfers between devices, shards(): rising = lax.ppermute(add(rising, chunks[distance]), 'dp', ahead)  10.4 us
    ppermute x2, starting transfers between devices, shards(): lax.ppermute(add(falling, chunks[chips - distance + 1]), 'dp', back)  10.3 us
    all_to_all x1, starting transfers between devices, shards(): lax.all_to_all(piece_grad, 'expert', split_axis=0, concat_axis=0, tiled=T...  8.71 us
    ppermute x3, starting transfers between devices, shards(): rising = lax.ppermute(add(rising, chunks[distance]), 'dp', ahead)  5.76 us
    ppermute x1, waiting for transfers between devices, shards(): high = lax.ppermute(high, 'expert', before)  4.91 us
    ppermute x1, starting transfers between devices, shards(): falling = lax.ppermute(chunks[chips - far + 1], 'dp', back)  4.55 us
    ppermute x1, starting transfers between devices, shards(): high = lax.ppermute(high, 'expert', before)  4 us
  transfers between devices with their start and end apart: 11, of which 6 were waited for; matrix products, arithmetic and copies ran while one was open for 0% of the time, Pallas kernels for 5%

profile of v7, /device:TPU:8, one launch (start us, length us, event | category | flops | bytes accessed | tf_op | source)
XLA Modules:
  0.0 124.6 jit_solution(17768196783056215032)
XLA Ops:
  0.6 2.7 %shard_map.102 = (bf16[4,16,2,3584]{3,2,1,0:T(2,128)(2,1)}, bf16[128,128]{1,0:T(8,128)(2,1)S(1)}) custom-call(s32[2,128]{1,0:T(2,128)} %bitcast.6, bf16[2,128]{1,0:T(2,128)(2,1)} %bitcast.7, bf16[128,3584]{1,0:T(8,128)(2,1)} %tokens_hbm.1, bf16[128,3584]{1,0:T(8,128)(2,1)} %cotan_hbm.1), custom_call_target="tpu_custom_call" | custom-call | tf_op jit(solution)/shard_map/pallas_call | solution.py:238
  3.3 50.4 %all_to_all.10.rows_ref = bf16[64,2,3584]{2,1,0:T(2,128)(2,1)S(1)} all-to-all(bf16[64,2,3584]{2,1,0:T(2,128)(2,1)} %bitcast.5), channel_id=1, replica_groups=mesh['expert'=64,'dp'=16] {'expert'}, dimensions={0} | all-to-all | bytes 1835008 | tf_op jit(solution)/shard_map/all_to_all | solution.py:257
  53.7 0.0 copy-start
  53.8 3.2 %collective-permute-start = (bf16[36,2,3584]{2,1,0:T(2,128)(2,1)S(1)}, bf16[36,2,3584]{2,1,0:T(2,128)(2,1)S(1)}, u32[]{:S(2)}, u32[]{:S(2)}) collective-permute-start(bf16[36,2,3584]{2,1,0:T(2,128)(2,1)S(1)} %shard_map.104), channel_id=1, source_target_pairs={{0,16},{16,32},{32,48},{48,64},{64,80},{80,96},{96,112},{112,0},{1... | collective-permute-start | bytes 1548296 | tf_op jit(solution)/shard_map/ppermute | solution.py:279
  56.9 0.8 shard_map.105
  57.7 4.0 %collective-permute-start.1 = (bf16[28,2,3584]{2,1,0:T(2,128)(2,1)}, bf16[28,2,3584]{2,1,0:T(2,128)(2,1)S(1)}, u32[]{:S(2)}, u32[]{:S(2)}) collective-permute-start(bf16[28,2,3584]{2,1,0:T(2,128)(2,1)} %shard_map.105), channel_id=1, source_target_pairs={{0,112},{16,0},{32,16},{48,32},{64,48},{80,64},{96,80},{112,96},{1... | collective-permute-start | bytes 1204232 | tf_op jit(solution)/shard_map/ppermute | solution.py:280
  61.7 0.0 copy-done
  61.7 2.0 %shard_map.103 = (bf16[128,3712]{1,0:T(8,128)(2,1)S(1)}, bf16[152,3584]{1,0:T(8,128)(2,1)S(1)}, bf16[152,3584]{1,0:T(8,128)(2,1)S(1)}, f32[2,152,128]{2,1,0:T(8,128)S(1)}, f32[152,128]{1,0:T(8,128)S(1)}) custom-call(s32[1]{0:T(128)} %bitcast.1.piece_at_ref, bf16[64,2,3584]{2,1,0:T(2,128)(2,1)S(1)} %all_to_all.10.rows_ref, bf16[152,3584]{1,0:T(8,128)(2,1)S(1)} %copy-done, ...), custom_call_target="tpu_custom_call" | custom-call | flops 278921216 | bytes 8388608 | tf_op jit(solution)/shard_map/pallas_call | solution.py:287
  63.8 4.9 %collective-permute-done.1.high_ref = bf16[28,2,3584]{2,1,0:T(2,128)(2,1)S(1)} collective-permute-done((bf16[28,2,3584]{2,1,0:T(2,128)(2,1)}, bf16[28,2,3584]{2,1,0:T(2,128)(2,1)S(1)}, u32[]{:S(2)}, u32[]{:S(2)}) %collective-permute-start.1) | collective-permute-done | bytes 401440 | tf_op jit(solution)/shard_map/ppermute | solution.py:280
  68.7 0.0 collective-permute-done.low_ref
  68.7 1.5 %shard_map.106 = (bf16[8,456,256]{2,1,0:T(8,128)(2,1)S(1)}, bf16[304,128]{1,0:T(8,128)(2,1)S(1)}, bf16[152,128]{1,0:T(8,128)(2,1)S(1)}, bf16[2,128,3712]{2,1,0:T(8,128)(2,1)S(1)}) custom-call(s32[1]{0:T(128)} %bitcast.replica_ref, s32[1]{0:T(128)} %bitcast.1.piece_at_ref, bf16[128,3712]{1,0:T(8,128)(2,1)S(1)} %get-tuple-element.31.first_ref, ...), custom_call_target="tpu_custom_call" | custom-call | tf_op jit(solution)/shard_map/pallas_call | solution.py:305
  70.2 1.9 %collective-permute-start.2 = (bf16[8,456,256]{2,1,0:T(8,128)(2,1)S(1)}, bf16[8,456,256]{2,1,0:T(8,128)(2,1)S(1)}, u32[]{:S(2)}, u32[]{:S(2)}) collective-permute-start(bf16[8,456,256]{2,1,0:T(8,128)(2,1)S(1)} %get-tuple-element.39), channel_id=1, source_target_pairs={{0,1},{1,0},{2,3},{3,2},{4,5},{5,4},{6,7},{7,6},{8,9},{9,8},{10,11... | collective-permute-start | bytes 5603336 | tf_op jit(solution)/shard_map/ppermute | solution.py:322
  72.1 1.6 %shard_map.111 = bf16[64,2,3584]{2,1,0:T(2,128)(2,1)} custom-call(bf16[304,128]{1,0:T(8,128)(2,1)S(1)} %get-tuple-element.36.pre_ref, bf16[152,3584]{1,0:T(8,128)(2,1)S(1)} %copy-done, bf16[152,3584]{1,0:T(8,128)(2,1)S(1)} %get-tuple-element.32.up_ref), custom_call_target="tpu_custom_call" | custom-call | flops 278921216 | bytes 4194304 | tf_op jit(solution)/shard_map/pallas_call | solution.py:351
  73.7 0.7 shard_map.107.mine_ref
  74.4 1.5 %collective-permute-done.2.theirs_ref = bf16[8,456,256]{2,1,0:T(8,128)(2,1)S(1)} collective-permute-done((bf16[8,456,256]{2,1,0:T(8,128)(2,1)S(1)}, bf16[8,456,256]{2,1,0:T(8,128)(2,1)S(1)}, u32[]{:S(2)}, u32[]{:S(2)}) %collective-permute-start.2) | collective-permute-done | bytes 1867808 | tf_op jit(solution)/shard_map/ppermute | solution.py:322
  75.9 0.4 shard_map.108
  76.3 8.7 %all-to-all-start.1 = ((bf16[64,2,3584]{2,1,0:T(2,128)(2,1)}), bf16[64,2,3584]{2,1,0:T(2,128)(2,1)S(1)}, u32[]{:S(2)}, u32[]{:S(2)}) async-start(bf16[64,2,3584]{2,1,0:T(2,128)(2,1)} %shard_map.111), calls=%async_computation.1 | async-start | bytes 1835008 | tf_op jit(solution)/shard_map/all_to_all | solution.py:374
  85.1 2.5 %collective-permute-start.6 = (bf16[456,256]{1,0:T(8,128)(2,1)S(1)}, bf16[456,256]{1,0:T(8,128)(2,1)S(1)}, u32[]{:S(2)}, u32[]{:S(2)}) collective-permute-start(bf16[456,256]{1,0:T(8,128)(2,1)S(1)} %get-tuple-element.47), channel_id=1, source_target_pairs={{0,2},{1,3},{2,4},{3,5},{4,6},{5,7},{6,8},{7,9},{8,10},{9,11},{10,... | collective-permute-start | bytes 700424 | tf_op jit(solution)/shard_map/ppermute | solution.py:368
  87.6 4.6 %collective-permute-start.3 = (bf16[456,256]{1,0:T(8,128)(2,1)S(1)}, bf16[456,256]{1,0:T(8,128)(2,1)S(1)}, u32[]{:S(2)}, u32[]{:S(2)}) collective-permute-start(bf16[456,256]{1,0:T(8,128)(2,1)S(1)} %get-tuple-element.40), channel_id=1, source_target_pairs={{0,14},{1,15},{2,0},{3,1},{4,2},{5,3},{6,4},{7,5},{8,6},{9,7},{10,... | collective-permute-start | bytes 700424 | tf_op jit(solution)/shard_map/ppermute | solution.py:369
  92.1 3.5 %collective-permute-done.6.got_ref = bf16[456,256]{1,0:T(8,128)(2,1)S(1)} collective-permute-done((bf16[456,256]{1,0:T(8,128)(2,1)S(1)}, bf16[456,256]{1,0:T(8,128)(2,1)S(1)}, u32[]{:S(2)}, u32[]{:S(2)}) %collective-permute-start.6) | collective-permute-done | bytes 233504 | tf_op jit(solution)/shard_map/ppermute | solution.py:368
  95.6 0.1 shard_map.113
  95.7 1.9 %collective-permute-start.7 = (bf16[456,256]{1,0:T(8,128)(2,1)S(1)}, bf16[456,256]{1,0:T(8,128)(2,1)S(1)}, u32[]{:S(2)}, u32[]{:S(2)}) collective-permute-start(bf16[456,256]{1,0:T(8,128)(2,1)S(1)} %shard_map.113), channel_id=1, source_target_pairs={{0,2},{1,3},{2,4},{3,5},{4,6},{5,7},{6,8},{7,9},{8,10},{9,11},{10,... | collective-permute-start | bytes 700424 | tf_op jit(solution)/shard_map/ppermute | solution.py:371
  97.6 0.0 collective-permute-done.3.got_ref
  97.6 0.1 shard_map.109
  97.7 5.1 %collective-permute-start.4 = (bf16[456,256]{1,0:T(8,128)(2,1)S(1)}, bf16[456,256]{1,0:T(8,128)(2,1)S(1)}, u32[]{:S(2)}, u32[]{:S(2)}) collective-permute-start(bf16[456,256]{1,0:T(8,128)(2,1)S(1)} %shard_map.109), channel_id=1, source_target_pairs={{0,14},{1,15},{2,0},{3,1},{4,2},{5,3},{6,4},{7,5},{8,6},{9,7},{10,... | collective-permute-start | bytes 700424 | tf_op jit(solution)/shard_map/ppermute | solution.py:373
  102.8 2.5 %collective-permute-done.7.got_ref = bf16[456,256]{1,0:T(8,128)(2,1)S(1)} collective-permute-done((bf16[456,256]{1,0:T(8,128)(2,1)S(1)}, bf16[456,256]{1,0:T(8,128)(2,1)S(1)}, u32[]{:S(2)}, u32[]{:S(2)}) %collective-permute-start.7) | collective-permute-done | bytes 233504 | tf_op jit(solution)/shard_map/ppermute | solution.py:371
  105.4 0.1 shard_map.114
  105.4 1.9 %collective-permute-start.8 = (bf16[456,256]{1,0:T(8,128)(2,1)S(1)}, bf16[456,256]{1,0:T(8,128)(2,1)S(1)}, u32[]{:S(2)}, u32[]{:S(2)}) collective-permute-start(bf16[456,256]{1,0:T(8,128)(2,1)S(1)} %shard_map.114), channel_id=1, source_target_pairs={{0,2},{1,3},{2,4},{3,5},{4,6},{5,7},{6,8},{7,9},{8,10},{9,11},{10,... | collective-permute-start | bytes 700424 | tf_op jit(solution)/shard_map/ppermute | solution.py:371
  107.4 0.0 collective-permute-done.4.got_ref
  107.4 0.1 shard_map.110
  107.4 5.1 %collective-permute-start.5 = (bf16[456,256]{1,0:T(8,128)(2,1)S(1)}, bf16[456,256]{1,0:T(8,128)(2,1)S(1)}, u32[]{:S(2)}, u32[]{:S(2)}) collective-permute-start(bf16[456,256]{1,0:T(8,128)(2,1)S(1)} %shard_map.110), channel_id=1, source_target_pairs={{0,14},{1,15},{2,0},{3,1},{4,2},{5,3},{6,4},{7,5},{8,6},{9,7},{10,... | collective-permute-start | bytes 700424 | tf_op jit(solution)/shard_map/ppermute | solution.py:373
  112.6 2.0 %collective-permute-done.8.got_ref = bf16[456,256]{1,0:T(8,128)(2,1)S(1)} collective-permute-done((bf16[456,256]{1,0:T(8,128)(2,1)S(1)}, bf16[456,256]{1,0:T(8,128)(2,1)S(1)}, u32[]{:S(2)}, u32[]{:S(2)}) %collective-permute-start.8) | collective-permute-done | bytes 233504 | tf_op jit(solution)/shard_map/ppermute | solution.py:371
  114.6 0.1 shard_map.115
  114.7 1.9 %collective-permute-start.9 = (bf16[456,256]{1,0:T(8,128)(2,1)S(1)}, bf16[456,256]{1,0:T(8,128)(2,1)S(1)}, u32[]{:S(2)}, u32[]{:S(2)}) collective-permute-start(bf16[456,256]{1,0:T(8,128)(2,1)S(1)} %shard_map.115), channel_id=1, source_target_pairs={{0,2},{1,3},{2,4},{3,5},{4,6},{5,7},{6,8},{7,9},{8,10},{9,11},{10,... | collective-permute-start | bytes 700424 | tf_op jit(solution)/shard_map/ppermute | solution.py:371
  116.6 0.0 all-to-all-done.1.rows_ref
  116.6 1.3 %shard_map.112 = bf16[128,3584]{1,0:T(8,128)(2,1)} custom-call(bf16[128,128]{1,0:T(8,128)(2,1)S(1)} %get-tuple-element.43.table_ref, bf16[64,2,3584]{2,1,0:T(2,128)(2,1)S(1)} %all-to-all-done.1.rows_ref), custom_call_target="tpu_custom_call" | custom-call | flops 117440512 | bytes 2097152 | tf_op jit(solution)/shard_map/pallas_call | solution.py:375
  118.0 0.0 collective-permute-done.5.down_ring_ref
  118.0 5.9 %collective-permute-done.9.up_ring_ref = bf16[456,256]{1,0:T(8,128)(2,1)S(1)} collective-permute-done((bf16[456,256]{1,0:T(8,128)(2,1)S(1)}, bf16[456,256]{1,0:T(8,128)(2,1)S(1)}, u32[]{:S(2)}, u32[]{:S(2)}) %collective-permute-start.9) | collective-permute-done | bytes 233504 | tf_op jit(solution)/shard_map/ppermute | solution.py:371
  123.8 0.7 shard_map.116
  (1 shorter events, 0.0 us)
Async XLA Ops:
  53.7 8.0 %copy-start = (bf16[152,3584]{1,0:T(8,128)(2,1)S(1)}, bf16[152,3584]{1,0:T(8,128)(2,1)}, u32[]{:S(2)}) copy-start(bf16[152,3584]{1,0:T(8,128)(2,1)} %gate_ref.5) | copy-start | bytes 3268612
  53.8 15.0 %collective-permute-start = (bf16[36,2,3584]{2,1,0:T(2,128)(2,1)S(1)}, bf16[36,2,3584]{2,1,0:T(2,128)(2,1)S(1)}, u32[]{:S(2)}, u32[]{:S(2)}) collective-permute-start(bf16[36,2,3584]{2,1,0:T(2,128)(2,1)S(1)} %shard_map.104), channel_id=1, source_target_pairs={{0,16},{16,32},{32,48},{48,64},{64,80},{80,96},{96,112},{112,0},{1... | collective-permute-start | bytes 1548296 | tf_op jit(solution)/shard_map/ppermute | solution.py:279
  57.7 11.0 %collective-permute-start.1 = (bf16[28,2,3584]{2,1,0:T(2,128)(2,1)}, bf16[28,2,3584]{2,1,0:T(2,128)(2,1)S(1)}, u32[]{:S(2)}, u32[]{:S(2)}) collective-permute-start(bf16[28,2,3584]{2,1,0:T(2,128)(2,1)} %shard_map.105), channel_id=1, source_target_pairs={{0,112},{16,0},{32,16},{48,32},{64,48},{80,64},{96,80},{112,96},{1... | collective-permute-start | bytes 1204232 | tf_op jit(solution)/shard_map/ppermute | solution.py:280
  70.2 5.7 %collective-permute-start.2 = (bf16[8,456,256]{2,1,0:T(8,128)(2,1)S(1)}, bf16[8,456,256]{2,1,0:T(8,128)(2,1)S(1)}, u32[]{:S(2)}, u32[]{:S(2)}) collective-permute-start(bf16[8,456,256]{2,1,0:T(8,128)(2,1)S(1)} %get-tuple-element.39), channel_id=1, source_target_pairs={{0,1},{1,0},{2,3},{3,2},{4,5},{5,4},{6,7},{7,6},{8,9},{9,8},{10,11... | collective-permute-start | bytes 5603336 | tf_op jit(solution)/shard_map/ppermute | solution.py:322
  76.3 40.2 %all-to-all-start.1 = ((bf16[64,2,3584]{2,1,0:T(2,128)(2,1)}), bf16[64,2,3584]{2,1,0:T(2,128)(2,1)S(1)}, u32[]{:S(2)}, u32[]{:S(2)}) async-start(bf16[64,2,3584]{2,1,0:T(2,128)(2,1)} %shard_map.111), calls=%async_computation.1 | async-start | bytes 1835008 | tf_op jit(solution)/shard_map/all_to_all | solution.py:374
  85.1 10.6 %collective-permute-start.6 = (bf16[456,256]{1,0:T(8,128)(2,1)S(1)}, bf16[456,256]{1,0:T(8,128)(2,1)S(1)}, u32[]{:S(2)}, u32[]{:S(2)}) collective-permute-start(bf16[456,256]{1,0:T(8,128)(2,1)S(1)} %get-tuple-element.47), channel_id=1, source_target_pairs={{0,2},{1,3},{2,4},{3,5},{4,6},{5,7},{6,8},{7,9},{8,10},{9,11},{10,... | collective-permute-start | bytes 700424 | tf_op jit(solution)/shard_map/ppermute | solution.py:368
  87.6 10.0 %collective-permute-start.3 = (bf16[456,256]{1,0:T(8,128)(2,1)S(1)}, bf16[456,256]{1,0:T(8,128)(2,1)S(1)}, u32[]{:S(2)}, u32[]{:S(2)}) collective-permute-start(bf16[456,256]{1,0:T(8,128)(2,1)S(1)} %get-tuple-element.40), channel_id=1, source_target_pairs={{0,14},{1,15},{2,0},{3,1},{4,2},{5,3},{6,4},{7,5},{8,6},{9,7},{10,... | collective-permute-start | bytes 700424 | tf_op jit(solution)/shard_map/ppermute | solution.py:369
  95.7 9.7 %collective-permute-start.7 = (bf16[456,256]{1,0:T(8,128)(2,1)S(1)}, bf16[456,256]{1,0:T(8,128)(2,1)S(1)}, u32[]{:S(2)}, u32[]{:S(2)}) collective-permute-start(bf16[456,256]{1,0:T(8,128)(2,1)S(1)} %shard_map.113), channel_id=1, source_target_pairs={{0,2},{1,3},{2,4},{3,5},{4,6},{5,7},{6,8},{7,9},{8,10},{9,11},{10,... | collective-permute-start | bytes 700424 | tf_op jit(solution)/shard_map/ppermute | solution.py:371
  97.7 9.7 %collective-permute-start.4 = (bf16[456,256]{1,0:T(8,128)(2,1)S(1)}, bf16[456,256]{1,0:T(8,128)(2,1)S(1)}, u32[]{:S(2)}, u32[]{:S(2)}) collective-permute-start(bf16[456,256]{1,0:T(8,128)(2,1)S(1)} %shard_map.109), channel_id=1, source_target_pairs={{0,14},{1,15},{2,0},{3,1},{4,2},{5,3},{6,4},{7,5},{8,6},{9,7},{10,... | collective-permute-start | bytes 700424 | tf_op jit(solution)/shard_map/ppermute | solution.py:373
  105.4 9.2 %collective-permute-start.8 = (bf16[456,256]{1,0:T(8,128)(2,1)S(1)}, bf16[456,256]{1,0:T(8,128)(2,1)S(1)}, u32[]{:S(2)}, u32[]{:S(2)}) collective-permute-start(bf16[456,256]{1,0:T(8,128)(2,1)S(1)} %shard_map.114), channel_id=1, source_target_pairs={{0,2},{1,3},{2,4},{3,5},{4,6},{5,7},{6,8},{7,9},{8,10},{9,11},{10,... | collective-permute-start | bytes 700424 | tf_op jit(solution)/shard_map/ppermute | solution.py:371
  107.4 10.5 %collective-permute-start.5 = (bf16[456,256]{1,0:T(8,128)(2,1)S(1)}, bf16[456,256]{1,0:T(8,128)(2,1)S(1)}, u32[]{:S(2)}, u32[]{:S(2)}) collective-permute-start(bf16[456,256]{1,0:T(8,128)(2,1)S(1)} %shard_map.110), channel_id=1, source_target_pairs={{0,14},{1,15},{2,0},{3,1},{4,2},{5,3},{6,4},{7,5},{8,6},{9,7},{10,... | collective-permute-start | bytes 700424 | tf_op jit(solution)/shard_map/ppermute | solution.py:373
  114.7 9.2 %collective-permute-start.9 = (bf16[456,256]{1,0:T(8,128)(2,1)S(1)}, bf16[456,256]{1,0:T(8,128)(2,1)S(1)}, u32[]{:S(2)}, u32[]{:S(2)}) collective-permute-start(bf16[456,256]{1,0:T(8,128)(2,1)S(1)} %shard_map.115), channel_id=1, source_target_pairs={{0,2},{1,3},{2,4},{3,5},{4,6},{5,7},{6,8},{7,9},{8,10},{9,11},{10,... | collective-permute-start | bytes 700424 | tf_op jit(solution)/shard_map/ppermute | solution.py:371
